TPU v7x, 32 devices: a whole 2x2x4 slice. The times are simulated.
32 devices in a mesh: clip: 16 (over z, x, core), val: 2 (over y).
Axes of the slice: x: 2, y: 2, z: 4, core: 2. Of those that a mesh axis runs over, the one named last changes fastest.
Arguments:
- latents: bfloat16 [256, 8192], P('clip', 'val'), may hold values from -10 to 10
- noise: bfloat16 [256, 8192], P('clip', 'val'), may hold values from -10 to 10
- offsets: int32 [256, 2, 2], P('clip'), may hold values from 0 to 15
- times: float32 [256], P('clip'), may hold values from 0.05 to 0.95
- embed: bfloat16 [64, 5120], replicated, may hold values from -0.75 to 0.75
Outputs:
- embedded: bfloat16 [256, 128, 5120], P('clip', 'val')
All inputs are finite; a program needn't handle non-finite values.
Results may differ from a plain program's by a relative error of at most 0.0051.
Values may be sent and summed in bfloat16 or wider, within the bound.
No kernel may reach another device: no remote copies, remote signals or barrier semaphores. Data moves between devices by JAX's collectives and lax.ppermute only.
A program may use at most 64 MiB of HBM per device.

v0:
```python
import math

import jax
import jax.numpy as jnp
from jax import lax
from jax.sharding import PartitionSpec as P

P_SIZE = 64
FR = 2
GW = 16
GH = 4
ITERS = 4
S = 128


def warp_noise(noise, offsets):
    clips = noise.shape[0]
    tokens = FR * GH * GW
    value_cube = noise.reshape(clips, noise.shape[1] // tokens, tokens)
    shift_y = offsets[:, :, 0] % GH
    shift_x = offsets[:, :, 1] % GW
    src_rows = (jnp.arange(GH, dtype=jnp.int32)[None, None, :] - shift_y[:, :, None]) % GH
    src_cols = (jnp.arange(GW, dtype=jnp.int32)[None, None, :] - shift_x[:, :, None]) % GW
    frame_base = (jnp.arange(FR, dtype=jnp.int32) * (GH * GW))[None, :, None, None]
    source = (frame_base + src_rows[:, :, :, None] * GW + src_cols[:, :, None, :]).reshape(
        clips, tokens
    )
    source = jnp.broadcast_to(source[:, None, :], value_cube.shape)
    return jnp.take_along_axis(value_cube, source, axis=2).reshape(noise.shape)


def row_stats(scores):
    top = jnp.max(scores, axis=1)
    total = jnp.sum(jnp.exp(scores - top[:, None]), axis=1)
    return (top, total)


def column_lse(scores):
    top = jnp.max(scores, axis=0)
    top = lax.pmax(top, "clip")
    total = lax.psum(jnp.sum(jnp.exp(scores - top[None, :]), axis=0), "clip")
    return top + jnp.log(total)


def on_device(latents, noise, offsets, times, embed):
    warped = warp_noise(noise, offsets)
    clips = latents.shape[0]
    volume = P_SIZE * S
    entropy = 0.5 / math.sqrt(volume)
    contract = (((1,), (1,)), ((), ()))
    panel_all = lax.all_gather(warped, "clip", axis=0, tiled=True)
    gram_part = lax.dot_general(latents, panel_all, contract, preferred_element_type=jnp.float32)
    square_part = jnp.sum(jnp.square(panel_all.astype(jnp.float32)), axis=1)
    gram, square = lax.psum((gram_part, square_part), "val")
    cost = (square[None, :] - 2.0 * gram) / volume
    column_dual = jnp.zeros((cost.shape[1],), jnp.float32)
    for sweep_index in range(ITERS):
        top, total = row_stats((column_dual[None, :] - cost) / entropy)
        row_dual = -entropy * (top + jnp.log(total))
        column_dual = -entropy * column_lse((row_dual[:, None] - cost) / entropy)
    scores = (column_dual[None, :] - cost) / entropy
    top, total = row_stats(scores)
    weights = (jnp.exp(scores - top[:, None]) / total[:, None]).astype(jnp.bfloat16)
    coupled = jnp.dot(weights, panel_all, preferred_element_type=jnp.float32)
    mixed = (
        (1.0 - times)[:, None] * latents.astype(jnp.float32) + times[:, None] * coupled
    ).astype(jnp.bfloat16)
    value_cube = mixed.reshape(clips, latents.shape[1] // S, S)
    return jnp.einsum(
        "cps,pd->csd",
        lax.all_to_all(value_cube, "val", split_axis=2, concat_axis=1, tiled=True),
        embed,
        preferred_element_type=jnp.float32,
    ).astype(jnp.bfloat16)


def solution(mesh):
    placed = (P("clip", "val"), P("clip", "val"), P("clip", None, None), P("clip"), P())
    return jax.shard_map(
        on_device, mesh=mesh, in_specs=placed, out_specs=P("clip", "val", None), check_vma=False
    )
```

profile of v0, /device:TPU:0, one launch (start us, length us, event | category | flops | bytes accessed | tf_op | source)
XLA Modules:
  0.0 952.7 jit_solution(16736781846496268663)
XLA Ops:
  6.5 0.8 and_select_fusion.3
  7.9 0.9 copy.30
  8.9 624.6 %gather_fusion = bf16[65536]{0:T(1024)(128)(2,1)S(1)} fusion(bf16[16,32,128]{2,1,0:T(8,128)(2,1)S(1)} %bitcast.27, s32[65536]{0:T(1024)S(1)} %bitcast.28), kind=kCustom, calls=%fused_computation | custom fusion | bytes 1048576 | tf_op jit(solution)/shard_map/jit(take_along_axis)/gather | solution.py:29
  633.6 0.7 copy.34
  634.4 44.2 %all-gather.2.cloned.1.call-done = bf16[256,4096]{1,0:T(8,128)(2,1)} async-done(((bf16[16,4096]{1,0:T(8,128)(2,1)}), bf16[256,4096]{1,0:T(8,128)(2,1)}) %all-gather.2.cloned.1.call-update) | async-done | bytes 2097168 | tf_op jit(solution)/shard_map/all_gather | solution.py:51
  678.6 2.1 multiply_reduce_fusion
  680.7 2.2 convolution_bitcast_fusion
  682.9 8.3 all-reduce
  691.6 29.5 %pmax.28 = f32[256]{0:T(256)S(1)} all-reduce(f32[256]{0:T(256)S(1)} %fusion.11), channel_id=1, replica_groups=mesh['clip'=16,'val'=2] {'clip'}, use_global_device_ids=true, to_apply=%region_6.7 | all-reduce | flops 256 | bytes 2048 | tf_op jit(solution)/shard_map/pmax | solution.py:40
  721.2 29.5 %psum.44 = f32[256]{0:T(256)S(1)} all-reduce(f32[256]{0:T(256)S(1)} %exponential_reduce_fusion.6), channel_id=1, replica_groups=mesh['clip'=16,'val'=2] {'clip'}, use_global_device_ids=true, to_apply=%region_8.9 | all-reduce | flops 256 | bytes 2048 | tf_op jit(solution)/shard_map/psum | solution.py:41
  750.8 0.2 exponential_reduce_fusion.5
  751.1 29.5 %pmax.29 = f32[256]{0:T(256)S(1)} all-reduce(f32[256]{0:T(256)S(1)} %fusion.13), channel_id=1, replica_groups=mesh['clip'=16,'val'=2] {'clip'}, use_global_device_ids=true, to_apply=%region_12.13 | all-reduce | flops 256 | bytes 2048 | tf_op jit(solution)/shard_map/pmax | solution.py:40
  780.7 29.5 %psum.45 = f32[256]{0:T(256)S(1)} all-reduce(f32[256]{0:T(256)S(1)} %exponential_reduce_fusion.4), channel_id=1, replica_groups=mesh['clip'=16,'val'=2] {'clip'}, use_global_device_ids=true, to_apply=%region_14.15 | all-reduce | flops 256 | bytes 2048 | tf_op jit(solution)/shard_map/psum | solution.py:41
  810.6 29.5 %pmax.30 = f32[256]{0:T(256)S(1)} all-reduce(f32[256]{0:T(256)S(1)} %fusion.15), channel_id=1, replica_groups=mesh['clip'=16,'val'=2] {'clip'}, use_global_device_ids=true, to_apply=%region_18.19 | all-reduce | flops 256 | bytes 2048 | tf_op jit(solution)/shard_map/pmax | solution.py:40
  840.2 29.5 %psum.46 = f32[256]{0:T(256)S(1)} all-reduce(f32[256]{0:T(256)S(1)} %exponential_reduce_fusion.2), channel_id=1, replica_groups=mesh['clip'=16,'val'=2] {'clip'}, use_global_device_ids=true, to_apply=%region_20.21 | all-reduce | flops 256 | bytes 2048 | tf_op jit(solution)/shard_map/psum | solution.py:41
  870.1 29.5 %pmax.31 = f32[256]{0:T(256)S(1)} all-reduce(f32[256]{0:T(256)S(1)} %fusion.17), channel_id=1, replica_groups=mesh['clip'=16,'val'=2] {'clip'}, use_global_device_ids=true, to_apply=%region_24.25 | all-reduce | flops 256 | bytes 2048 | tf_op jit(solution)/shard_map/pmax | solution.py:40
  899.7 29.5 %psum.47 = f32[256]{0:T(256)S(1)} all-reduce(f32[256]{0:T(256)S(1)} %exponential_reduce_fusion), channel_id=1, replica_groups=mesh['clip'=16,'val'=2] {'clip'}, use_global_device_ids=true, to_apply=%region_26.27 | all-reduce | flops 256 | bytes 2048 | tf_op jit(solution)/shard_map/psum | solution.py:41
  929.5 2.0 fusion.2
  931.6 0.4 copy.24
  932.0 0.5 reshape.134
  932.5 6.8 all_to_all.18
  939.4 0.3 reshape.135
  939.7 0.5 copy.29
  940.2 5.7 convolution_convert_fusion
  (47 shorter events, 2.9 us)
Async XLA Ops:
  6.5 933.7 %copy-start = (bf16[64,5120]{1,0:T(8,128)(2,1)S(1)}, bf16[64,5120]{1,0:T(8,128)(2,1)}, u32[]{:S(2)}) copy-start(bf16[64,5120]{1,0:T(8,128)(2,1)} %param.9) | copy-start | bytes 1966084
  6.5 672.1 %all-gather.2.cloned.1.call-start = ((), (), s32[]{:S(2)}) async-start(), calls=%async_computation.1 | async-start | bytes 2228224 | tf_op jit(solution)/shard_map/all_gather | solution.py:51
  8.9 625.5 %copy-start.2 = (f32[16]{0:T(128)S(1)}, f32[16]{0:T(128)}, u32[]{:S(2)}) copy-start(f32[16]{0:T(128)} %param.8) | copy-start | bytes 196
  8.9 671.8 %copy-start.1 = (bf16[16,4096]{1,0:T(8,128)(2,1)S(1)}, bf16[16,4096]{1,0:T(8,128)(2,1)}, u32[]{:S(2)}) copy-start(bf16[16,4096]{1,0:T(8,128)(2,1)} %param.5) | copy-start | bytes 393220
Sparse Core Ops, SparseCore 0:
  634.5 44.0 all-gather.1
where the time goes:
time: 953 us
  local copies, waits for them, and re-layouts  628 us (66%)
  blocking collectives  251 us (26%)
  waiting for transfers between devices  44.3 us (5%)
  between operations  13.6 us (1%)
  matrix products  9.92 us (1%)
    gather x1, local copies, waits for them, and re-layouts, warp_noise(): return jnp.take_along_axis(value_cube, source, axis=2).reshape(noise.shape)  625 us
    psum x4, blocking collectives, column_lse(): total = lax.psum(jnp.sum(jnp.exp(scores - top[None, :]), axis=0), 'clip')  118 us
    pmax x4, blocking collectives, column_lse(): top = lax.pmax(top, 'clip')  118 us
    all_gather x1, waiting for transfers between devices, on_device(): panel_all = lax.all_gather(warped, 'clip', axis=0, tiled=True)  44.2 us
  transfers between devices with their start and end apart: 1, of which 1 were waited for; matrix products, arithmetic and copies ran while one was open for 0% of the time, Pallas kernels for 0%

commit v1 on v0

v1 whole, which is shorter than its diff:
```python
import functools
import math

import jax
import jax.numpy as jnp
from jax import lax
from jax.experimental import pallas as pl
from jax.experimental.pallas import tpu as pltpu
from jax.sharding import PartitionSpec as P

P_SIZE = 64
D = 5120
FR = 2
GW = 16
GH = 4
ITERS = 4
S = 128
FRAME = GW * GH
SCALE = 2.0 / math.sqrt(P_SIZE * S)
NT = (((1,), (1,)), ((), ()))
TN = (((0,), (0,)), ((), ()))
F32 = jnp.float32
BF16 = jnp.bfloat16
ANY = pl.BlockSpec(memory_space=pl.ANY)
VMEM = pl.BlockSpec(memory_space=pltpu.VMEM)
SMEM = pl.BlockSpec(memory_space=pltpu.SMEM)


def params():
    return pltpu.CompilerParams(vmem_limit_bytes=48 * 1024 * 1024)


def warp_kernel(offsets, noise, out):
    clips, values = noise.shape
    row = lax.broadcasted_iota(jnp.int32, (clips, S), 0)
    token = lax.broadcasted_iota(jnp.int32, (clips, S), 1)
    frame = token // FRAME
    shift_y = jnp.zeros((clips, S), jnp.int32)
    shift_x = jnp.zeros((clips, S), jnp.int32)
    for i in range(clips):
        for f in range(FR):
            here = (row == i) & (frame == f)
            shift_y = jnp.where(here, offsets[i, f * 2], shift_y)
            shift_x = jnp.where(here, offsets[i, f * 2 + 1], shift_x)
    src_row = ((token // GW) - shift_y) & (GH - 1)
    src_col = (token - shift_x) & (GW - 1)
    source = frame * FRAME + src_row * GW + src_col
    for p in range(values // S):
        tile = noise[:, p * S : (p + 1) * S].astype(F32)
        moved = jnp.take_along_axis(tile, source, axis=1, mode="promise_in_bounds")
        out[:, p * S : (p + 1) * S] = moved.astype(BF16)


def warp_noise(noise, offsets):
    clips = noise.shape[0]
    return pl.pallas_call(
        warp_kernel,
        out_shape=jax.ShapeDtypeStruct(noise.shape, BF16),
        in_specs=[SMEM, VMEM],
        out_specs=VMEM,
        compiler_params=params(),
        name="warp",
    )(offsets.reshape(clips, FR * 2), noise)


def gram_kernel(clips, outer, inner, *refs):
    lat = refs[:inner]
    noi = refs[inner : inner + outer]
    out, held, sems = refs[inner + outer :]
    place = lax.axis_index("clip")
    a, b = place // inner, place % inner
    rows = clips * inner
    copies = []
    for k in range(inner):
        at = pl.multiple_of((b ^ k) * clips, clips)
        copies.append(pltpu.make_async_copy(lat[k], held.at[pl.ds(at, clips)], sems.at[k]))
    for s in range(outer):
        at = pl.multiple_of(rows + ((a + outer - s) % outer) * clips, clips)
        copies.append(pltpu.make_async_copy(noi[s], held.at[pl.ds(at, clips)], sems.at[inner + s]))
    for c in copies:
        c.start()
    for c in copies:
        c.wait()
    both = held[...]
    cols = clips * outer
    prod = lax.dot_general(both, both[rows:], NT, preferred_element_type=F32)
    inner_prod, own = prod[:rows], prod[rows:]
    eye = lax.broadcasted_iota(jnp.int32, (cols, cols), 0) == lax.broadcasted_iota(
        jnp.int32, (cols, cols), 1
    )
    square = jnp.sum(jnp.where(eye, own, 0.0), axis=0, keepdims=True)
    part = square - 2.0 * inner_prod
    out[...] = jnp.concatenate([part[: rows // 2], part[rows // 2 :]], axis=1)


def gram_block(lat, noi):
    clips, values = lat[0].shape
    inner, outer = len(lat), len(noi)
    return pl.pallas_call(
        functools.partial(gram_kernel, clips, outer, inner),
        out_shape=jax.ShapeDtypeStruct((clips * inner // 2, clips * outer * 2), F32),
        in_specs=[ANY] * (inner + outer),
        out_specs=VMEM,
        scratch_shapes=[
            pltpu.VMEM((clips * (inner + outer), values), BF16),
            pltpu.SemaphoreType.DMA((inner + outer,)),
        ],
        compiler_params=params(),
        name="gram",
    )(*lat, *noi)


def sinkhorn(kernel, own):
    col = jnp.zeros((1, kernel.shape[1]), F32)
    for _ in range(ITERS):
        u = kernel + col
        top = jnp.max(u, axis=1, keepdims=True)
        row = -(top + jnp.log(jnp.sum(jnp.exp(u - top), axis=1, keepdims=True)))
        u = kernel + row
        top = jnp.max(u, axis=0, keepdims=True)
        col = -(top + jnp.log(jnp.sum(jnp.exp(u - top), axis=0, keepdims=True)))
    u = own + col
    top = jnp.max(u, axis=1, keepdims=True)
    e = jnp.exp(u - top)
    return (e / jnp.sum(e, axis=1, keepdims=True)).astype(BF16)


def plan_kernel(clips, outer, *refs):
    mine, other = refs[:outer], refs[outer : 2 * outer]
    out, full = refs[2 * outer :]
    place = lax.axis_index("clip")
    inner = 4
    b = place % inner
    half = mine[0].shape[0] // 2
    low = lax.broadcasted_iota(jnp.int32, (half, 128), 1) < 64
    for s in range(outer):
        for x in range(2):
            g = mine[s][x * half : (x + 1) * half, :] * (-SCALE)
            h = other[s][x * half : (x + 1) * half, :] * (-SCALE)
            lanes = slice(x * 128, (x + 1) * 128)
            r = s * 2 * half
            full[r : r + half, lanes] = jnp.where(low, g, pltpu.roll(h, 64, 1))
            full[r + half : r + 2 * half, lanes] = jnp.where(low, pltpu.roll(g, 64, 1), h)
    own = full[pl.ds(pl.multiple_of(b * clips, clips), clips), :]
    out[...] = sinkhorn(full[...], own)


def plan(mine, other, clips):
    outer = len(mine)
    n = 256
    return pl.pallas_call(
        functools.partial(plan_kernel, clips, outer),
        out_shape=jax.ShapeDtypeStruct((clips, n), BF16),
        in_specs=[VMEM] * (2 * outer),
        out_specs=VMEM,
        scratch_shapes=[pltpu.VMEM((n, n), F32)],
        compiler_params=params(),
        name="plan",
    )(*mine, *other)


def mix_kernel(clips, outer, groups, times, weights, latents, *refs):
    parts = refs[:groups]
    keep, send, panel, cube, sems = refs[groups:]
    place = lax.axis_index("clip")
    val = lax.axis_index("val")
    inner = 4
    a = place // inner
    copies = []
    for g in range(groups):
        for s in range(outer):
            at = pl.multiple_of((g * outer + (a + outer - s) % outer) * clips, clips)
            copies.append(
                pltpu.make_async_copy(
                    parts[g].at[pl.ds(s * clips, clips)],
                    panel.at[pl.ds(at, clips)],
                    sems.at[g * outer + s],
                )
            )
    for c in copies:
        c.start()
    row = lax.broadcasted_iota(jnp.int32, (clips, 1), 0)
    t = jnp.zeros((clips, 1), F32)
    for i in range(clips):
        t = jnp.where(row == i, times[i], t)
    for c in copies:
        c.wait()
    w = weights[...]
    values = latents.shape[1]
    patch = values // S
    step = 512
    for at in range(0, values, step):
        coupled = jnp.dot(w, panel[:, at : at + step], preferred_element_type=F32)
        mixed = (1.0 - t) * latents[:, at : at + step].astype(F32) + t * coupled
        for q in range(step // S):
            cube[:, at // S + q, :] = mixed[:, q * S : (q + 1) * S]
    low = lax.broadcasted_iota(jnp.int32, (patch, S), 1) < FRAME
    for i in range(0, clips, 2):
        x, y = cube[i], cube[i + 1]
        first = jnp.where(low, x, pltpu.roll(y, FRAME, 1))
        second = jnp.where(low, pltpu.roll(x, FRAME, 1), y)
        lanes = slice(i * FRAME, (i + 2) * FRAME)
        keep[:, lanes] = jnp.where(val == 0, first, second).astype(BF16)
        send[:, lanes] = jnp.where(val == 0, second, first).astype(BF16)


def mix(times, weights, latents, parts, outer):
    clips, values = latents.shape
    groups = len(parts)
    patch = values // S
    shape = jax.ShapeDtypeStruct((patch, clips * FRAME), BF16)
    return pl.pallas_call(
        functools.partial(mix_kernel, clips, outer, groups),
        out_shape=[shape, shape],
        in_specs=[SMEM, VMEM, VMEM] + [ANY] * groups,
        out_specs=[VMEM, VMEM],
        scratch_shapes=[
            pltpu.VMEM((clips * outer * groups, values), BF16),
            pltpu.VMEM((clips, patch, S), F32),
            pltpu.SemaphoreType.DMA((groups * outer,)),
        ],
        compiler_params=params(),
        name="mix",
    )(times, weights, latents, *parts)


def embed_kernel(keep, got, embed, out):
    first = lax.axis_index("val") == 0
    k, g = keep[...], got[...]
    lhs = jnp.concatenate([jnp.where(first, k, g), jnp.where(first, g, k)], axis=0)
    out[...] = lax.dot_general(lhs, embed[...], TN, preferred_element_type=F32).astype(BF16)


def embed_tokens(keep, got, embed):
    patch, tokens = keep.shape
    block = 128
    return pl.pallas_call(
        embed_kernel,
        grid=(tokens // block,),
        out_shape=jax.ShapeDtypeStruct((tokens, embed.shape[1]), BF16),
        in_specs=[
            pl.BlockSpec((patch, block), lambda i: (0, i)),
            pl.BlockSpec((patch, block), lambda i: (0, i)),
            pl.BlockSpec(embed.shape, lambda i: (0, 0)),
        ],
        out_specs=pl.BlockSpec((block, embed.shape[1]), lambda i: (i, 0)),
        compiler_params=params(),
        name="embed",
    )(keep, got, embed)


def flip(n, bit):
    return [(i, i ^ bit) for i in range(n)]


def on_device(n, latents, noise, offsets, times, embed):
    clips = latents.shape[0]
    outer, inner = n // 4, 4

    def core(x):
        return lax.ppermute(x, "clip", flip(n, 1))

    def across(x):
        return lax.ppermute(x, "clip", flip(n, 2))

    def along(x, s):
        hop = [(i, (i + s * inner) % n) for i in range(n)]
        return lax.ppermute(x, "clip", hop)

    def other_val(x):
        return lax.ppermute(x, "val", [(0, 1), (1, 0)])

    def other_both(x):
        pairs = [(2 * i + v, 2 * (i ^ 2) + 1 - v) for i in range(n) for v in range(2)]
        return lax.ppermute(x, ("clip", "val"), pairs)

    warped = warp_noise(noise, offsets)
    lat_x = across(latents)
    lat = [latents, core(latents), lat_x, core(lat_x)]
    noi = [warped] + [along(warped, s) for s in range(1, outer)]
    part = gram_block(lat, noi)
    got_x, got_v, got_b = across(part), other_val(part), other_both(part)
    pair = jnp.concatenate([part + got_v, got_x + got_b], axis=0)
    mine = [pair] + [along(pair, s) for s in range(1, outer)]
    other = core(jnp.concatenate(mine, axis=0))
    rows = pair.shape[0]
    other = [other[s * rows : (s + 1) * rows] for s in range(outer)]
    line = jnp.concatenate(noi, axis=0)
    line_x = across(line)
    parts = [line, core(line), line_x, core(line_x)]
    weights = plan(mine, other, clips)
    keep, send = mix(times, weights, latents, parts, outer)
    out = embed_tokens(keep, other_val(send), embed)
    return out.reshape(clips, FRAME, embed.shape[1])


def warp_and_gather(latents, noise, offsets, times, embed):
    clips = latents.shape[0]
    warped = warp_noise(noise, offsets)
    panel = lax.all_gather(warped, "clip", axis=0, tiled=True)
    gram = lax.dot_general(latents, panel, NT, preferred_element_type=F32)
    square = jnp.sum(jnp.square(panel.astype(F32)), axis=1)
    part = lax.psum(square[None, :] - 2.0 * gram, "val")
    full = lax.all_gather(part, "clip", axis=0, tiled=True) * (-SCALE)
    weights = sinkhorn(full, part * (-SCALE))
    coupled = jnp.dot(weights, panel, preferred_element_type=F32)
    t = times[:, None]
    mixed = ((1.0 - t) * latents.astype(F32) + t * coupled).astype(BF16)
    cube = mixed.reshape(clips, latents.shape[1] // S, S)
    cube = lax.all_to_all(cube, "val", split_axis=2, concat_axis=1, tiled=True)
    return jnp.einsum("cps,pd->csd", cube, embed, preferred_element_type=F32).astype(BF16)


def solution(mesh):
    n, v = mesh.shape["clip"], mesh.shape["val"]
    body = functools.partial(on_device, n) if (n, v) == (16, 2) else warp_and_gather
    placed = (P("clip", "val"), P("clip", "val"), P("clip", None, None), P("clip"), P())
    return jax.shard_map(
        body, mesh=mesh, in_specs=placed, out_specs=P("clip", "val", None), check_vma=False
    )
```

time: 953 us -> 67.6 us (0.07)
  local copies, waits for them, and re-layouts: 628 us -> 5.22 us
  blocking collectives: 251 us -> 0 us
  starting transfers between devices: 0.01 us -> 18.6 us
  waiting for transfers between devices: 44.3 us -> 28.4 us
  Pallas kernels: 0 us -> 15 us
  between operations: 13.6 us -> 0.11 us
  matrix products: 9.92 us -> 0 us
    gather x1 -> x0, local copies, waits for them, and re-layouts: 625 us -> none  [warp_noise(): return jnp.take_along_axis(value_cube, source, axis=2).reshape(noise.shape)]
    psum x5 -> x0, blocking collectives: 126 us -> none  [the longest x4 118 us: column_lse(): total = lax.psum(jnp.sum(jnp.exp(scores - top[None, :]), axis=0), 'clip')]
    pmax x4 -> x0, blocking collectives: 118 us -> none  [column_lse(): top = lax.pmax(top, 'clip')]
    all_gather x1 -> x0, waiting for transfers between devices: 44.2 us -> none  [on_device(): panel_all = lax.all_gather(warped, 'clip', axis=0, tiled=True)]
    ppermute x0 -> x17, waiting for transfers between devices: none -> 28.4 us  [the longest x6 13.1 us: along(): return lax.ppermute(x, 'clip', hop)]
    ppermute x0 -> x17, starting transfers between devices: none -> 18.6 us  [the longest x6 9.47 us: along(): return lax.ppermute(x, 'clip', hop)]
    pallas_call x0 -> x5, Pallas kernels: none -> 15 us  [the longest x1 6.92 us: embed_tokens(): pl.pallas_call(embed_kernel, grid=(tokens // block,), out_shape=jax.Shape...]
    dot_general x3 -> x0, matrix products: 9.92 us -> none  [the longest x1 5.65 us: on_device(): jnp.einsum('cps,pd->csd', lax.all_to_all(value_cube, 'val', split_axis=2,...]
  transfers between devices with their start and end apart: 1 -> 17, of which waited for: 1 -> 8; matrix products, arithmetic and copies ran while one was open for 0% -> 1% of each run, Pallas kernels for 0% -> 3%
where the time goes in v1:
time: 67.6 us; the launch traced here: 67.3 us
  waiting for transfers between devices  28.4 us (42%)
  starting transfers between devices  18.6 us (28%)
  Pallas kernels  15 us (22%)
  local copies, waits for them, and re-layouts  5.22 us (8%)
    ppermute x6, waiting for transfers between devices, along(): return lax.ppermute(x, 'clip', hop)  13.1 us
    ppermute x1, waiting for transfers between devices, other_both(): return lax.ppermute(x, ('clip', 'val'), pairs)  10.7 us
    ppermute x6, starting transfers between devices, along(): return lax.ppermute(x, 'clip', hop)  9.47 us
    pallas_call x1, Pallas kernels, embed_tokens(): pl.pallas_call(embed_kernel, grid=(tokens // block,), out_shape=jax.Shape...  6.92 us
    unnamed x12, local copies, waits for them, and re-layouts  4.45 us
    ppermute x3, starting transfers between devices, across(): return lax.ppermute(x, 'clip', flip(n, 2))  4.09 us
    pallas_call x1, Pallas kernels, mix(): pl.pallas_call(functools.partial(mix_kernel, clips, outer, groups), out_s...  3.98 us
    ppermute x2, waiting for transfers between devices, other_val(): return lax.ppermute(x, 'val', [(0, 1), (1, 0)])  2.97 us
  transfers between devices with their start and end apart: 17, of which 8 were waited for; matrix products, arithmetic and copies ran while one was open for 1% of the time, Pallas kernels for 3%

profile of v1, /device:TPU:0, one launch (start us, length us, event | category | flops | bytes accessed | tf_op | source)
XLA Modules:
  0.0 67.3 jit_solution(11417273025326444858)
XLA Ops:
  0.0 2.9 %collective-permute-start.1 = (bf16[16,4096]{1,0:T(8,128)(2,1)}, bf16[16,4096]{1,0:T(8,128)(2,1)S(1)}, u32[]{:S(2)}, u32[]{:S(2)}) collective-permute-start(bf16[16,4096]{1,0:T(8,128)(2,1)} %latents.1), channel_id=1, source_target_pairs={{0,4},{2,6},{4,0},{6,2},{8,12},{10,14},{12,8},{14,10},{16,20},{18,... | collective-permute-start | bytes 393224 | tf_op jit(solution)/shard_map/ppermute | solution.py:264
  3.7 0.9 %copy-done.3 = bf16[16,4096]{1,0:T(8,128)(2,1)S(1)} copy-done((bf16[16,4096]{1,0:T(8,128)(2,1)S(1)}, bf16[16,4096]{1,0:T(8,128)(2,1)}, u32[]{:S(2)}) %copy-start.3) | copy-done | bytes 131096
  5.4 3.7 %collective-permute-start.5 = (bf16[16,4096]{1,0:T(8,128)(2,1)S(1)}, bf16[16,4096]{1,0:T(8,128)(2,1)S(1)}, u32[]{:S(2)}, u32[]{:S(2)}) collective-permute-start(bf16[16,4096]{1,0:T(8,128)(2,1)S(1)} %warp.1.refs_4_), channel_id=1, source_target_pairs={{0,24},{2,26},{4,28},{6,30},{8,0},{10,2},{12,4},{14,6},{16,8},{18,... | collective-permute-start | bytes 393224 | tf_op jit(solution)/shard_map/ppermute | solution.py:268
  9.1 1.0 %collective-permute-start.3 = (bf16[16,4096]{1,0:T(8,128)(2,1)S(1)}, bf16[16,4096]{1,0:T(8,128)(2,1)S(1)}, u32[]{:S(2)}, u32[]{:S(2)}) collective-permute-start(bf16[16,4096]{1,0:T(8,128)(2,1)S(1)} %warp.1.refs_4_), channel_id=1, source_target_pairs={{0,8},{2,10},{4,12},{6,14},{8,16},{10,18},{12,20},{14,22},{16,24},... | collective-permute-start | bytes 393224 | tf_op jit(solution)/shard_map/ppermute | solution.py:268
  10.6 2.4 %collective-permute-done.5.refs_7_ = bf16[16,4096]{1,0:T(8,128)(2,1)S(1)} collective-permute-done((bf16[16,4096]{1,0:T(8,128)(2,1)S(1)}, bf16[16,4096]{1,0:T(8,128)(2,1)S(1)}, u32[]{:S(2)}, u32[]{:S(2)}) %collective-permute-start.5) | collective-permute-done | bytes 131104 | tf_op jit(solution)/shard_map/ppermute | solution.py:268
  13.0 6.9 %collective-permute-done.4.refs_6_ = bf16[16,4096]{1,0:T(8,128)(2,1)S(1)} collective-permute-done((bf16[16,4096]{1,0:T(8,128)(2,1)S(1)}, bf16[16,4096]{1,0:T(8,128)(2,1)S(1)}, u32[]{:S(2)}, u32[]{:S(2)}) %collective-permute-start.4) | collective-permute-done | bytes 131104 | tf_op jit(solution)/shard_map/ppermute | solution.py:268
  19.9 0.9 %copy-done.1 = bf16[16,4096]{1,0:T(8,128)(2,1)S(1)} copy-done((bf16[16,4096]{1,0:T(8,128)(2,1)S(1)}, bf16[16,4096]{1,0:T(8,128)(2,1)}, u32[]{:S(2)}) %copy-start.1) | copy-done | bytes 131096
  20.8 1.9 %gram.1 = f32[32,128]{1,0:T(8,128)S(1)} custom-call(bf16[16,4096]{1,0:T(8,128)(2,1)S(1)} %copy-done.1, bf16[16,4096]{1,0:T(8,128)(2,1)S(1)} %collective-permute-done.refs_1_, bf16[16,4096]{1,0:T(8,128)(2,1)S(1)} %collective-permute-done.1.refs_2_, bf16[16,4096]{1,0:T(8,128)(2,1)S(1)} %collective-permute-done.2.refs_3_, bf16[16,4096]{1,0:T(8,128)(2,1)S(1)} %warp.1.refs_4_, ...), custom_call_target="tpu_custom_call" | custom-call | tf_op jit(solution)/shard_map/gram/pallas_call | solution.py:99
  22.7 1.6 %collective-permute-start.6 = (f32[32,128]{1,0:T(8,128)S(1)}, f32[32,128]{1,0:T(8,128)S(1)}, u32[]{:S(2)}, u32[]{:S(2)}) collective-permute-start(f32[32,128]{1,0:T(8,128)S(1)} %gram.1), channel_id=1, source_target_pairs={{0,1},{1,0},{2,3},{3,2},{4,5},{5,4},{6,7},{7,6},{8,9},{9,8},{10,11... | collective-permute-start | bytes 49160 | tf_op jit(solution)/shard_map/ppermute | solution.py:271
  25.0 1.4 %collective-permute-start.8 = (f32[32,128]{1,0:T(8,128)S(1)}, f32[32,128]{1,0:T(8,128)S(1)}, u32[]{:S(2)}, u32[]{:S(2)}) collective-permute-start(f32[32,128]{1,0:T(8,128)S(1)} %gram.1), channel_id=1, source_target_pairs={{0,5},{1,4},{2,7},{3,6},{4,1},{5,0},{6,3},{7,2},{8,13},{9,12},{10,... | collective-permute-start | bytes 49160 | tf_op jit(solution)/shard_map/ppermute | solution.py:275
  26.9 10.7 %collective-permute-done.8 = f32[32,128]{1,0:T(8,128)S(1)} collective-permute-done((f32[32,128]{1,0:T(8,128)S(1)}, f32[32,128]{1,0:T(8,128)S(1)}, u32[]{:S(2)}, u32[]{:S(2)}) %collective-permute-start.8) | collective-permute-done | bytes 16416 | tf_op jit(solution)/shard_map/ppermute | solution.py:275
  37.9 0.9 %collective-permute-start.9 = (f32[64,128]{1,0:T(8,128)S(1)}, f32[64,128]{1,0:T(8,128)S(1)}, u32[]{:S(2)}, u32[]{:S(2)}) collective-permute-start(f32[64,128]{1,0:T(8,128)S(1)} %pad_maximum_fusion.1.refs_0_), channel_id=1, source_target_pairs={{0,8},{2,10},{4,12},{6,14},{8,16},{10,18},{12,20},{14,22},{16,24},... | collective-permute-start | bytes 98312 | tf_op jit(solution)/shard_map/ppermute | solution.py:268
  38.8 3.0 %collective-permute-start.11 = (f32[64,128]{1,0:T(8,128)S(1)}, f32[64,128]{1,0:T(8,128)S(1)}, u32[]{:S(2)}, u32[]{:S(2)}) collective-permute-start(f32[64,128]{1,0:T(8,128)S(1)} %pad_maximum_fusion.1.refs_0_), channel_id=1, source_target_pairs={{0,24},{2,26},{4,28},{6,30},{8,0},{10,2},{12,4},{14,6},{16,8},{18,... | collective-permute-start | bytes 98312 | tf_op jit(solution)/shard_map/ppermute | solution.py:268
  41.8 0.9 %collective-permute-start.10 = (f32[64,128]{1,0:T(8,128)S(1)}, f32[64,128]{1,0:T(8,128)S(1)}, u32[]{:S(2)}, u32[]{:S(2)}) collective-permute-start(f32[64,128]{1,0:T(8,128)S(1)} %pad_maximum_fusion.1.refs_0_), channel_id=1, source_target_pairs={{0,16},{2,18},{4,20},{6,22},{8,24},{10,26},{12,28},{14,30},{16,0},... | collective-permute-start | bytes 98312 | tf_op jit(solution)/shard_map/ppermute | solution.py:268
  42.7 1.4 %collective-permute-done.9.refs_1_ = f32[64,128]{1,0:T(8,128)S(1)} collective-permute-done((f32[64,128]{1,0:T(8,128)S(1)}, f32[64,128]{1,0:T(8,128)S(1)}, u32[]{:S(2)}, u32[]{:S(2)}) %collective-permute-start.9) | collective-permute-done | bytes 32800 | tf_op jit(solution)/shard_map/ppermute | solution.py:268
  44.2 2.4 %collective-permute-done.10.refs_2_ = f32[64,128]{1,0:T(8,128)S(1)} collective-permute-done((f32[64,128]{1,0:T(8,128)S(1)}, f32[64,128]{1,0:T(8,128)S(1)}, u32[]{:S(2)}, u32[]{:S(2)}) %collective-permute-start.10) | collective-permute-done | bytes 32800 | tf_op jit(solution)/shard_map/ppermute | solution.py:268
  46.7 1.3 %collective-permute-done.12 = f32[256,128]{1,0:T(8,128)S(1)} collective-permute-done((f32[256,128]{1,0:T(8,128)S(1)}, f32[256,128]{1,0:T(8,128)S(1)}, u32[]{:S(2)}, u32[]{:S(2)}) %collective-permute-start.12) | collective-permute-done | bytes 131104 | tf_op jit(solution)/shard_map/ppermute | solution.py:261
  48.1 1.3 %plan.1.weights = bf16[16,256]{1,0:T(8,128)(2,1)S(1)} custom-call(f32[64,128]{1,0:T(8,128)S(1)} %pad_maximum_fusion.1.refs_0_, f32[64,128]{1,0:T(8,128)S(1)} %collective-permute-done.9.refs_1_, f32[64,128]{1,0:T(8,128)S(1)} %collective-permute-done.10.refs_2_, f32[64,128]{1,0:T(8,128)S(1)} %collective-permute-done.11.refs_3_, ...), custom_call_target="tpu_custom_call" | custom-call | tf_op jit(solution)/shard_map/plan/pallas_call | solution.py:151
  49.4 0.9 %copy-done.2 = bf16[16,4096]{1,0:T(8,128)(2,1)S(1)} copy-done((bf16[16,4096]{1,0:T(8,128)(2,1)S(1)}, bf16[16,4096]{1,0:T(8,128)(2,1)}, u32[]{:S(2)}) %copy-start.2) | copy-done | bytes 131096
  51.0 4.0 %mix.1 = (bf16[32,1024]{1,0:T(8,128)(2,1)S(1)}, bf16[32,1024]{1,0:T(8,128)(2,1)S(1)}) custom-call(f32[16]{0:T(128)S(1)} %copy-done.4, bf16[16,256]{1,0:T(8,128)(2,1)S(1)} %plan.1.weights, bf16[16,4096]{1,0:T(8,128)(2,1)S(1)} %copy-done.2, bf16[64,4096]{1,0:T(8,128)(2,1)S(1)} %pad_maximum_fusion.refs_0_, ...), custom_call_target="tpu_custom_call" | custom-call | tf_op jit(solution)/shard_map/mix/pallas_call | solution.py:212
  55.0 1.4 %collective-permute-start.16 = (bf16[32,1024]{1,0:T(8,128)(2,1)S(1)}, bf16[32,1024]{1,0:T(8,128)(2,1)S(1)}, u32[]{:S(2)}, u32[]{:S(2)}) collective-permute-start(bf16[32,1024]{1,0:T(8,128)(2,1)S(1)} %get-tuple-element.8), channel_id=1, source_target_pairs={{0,1},{1,0},{2,3},{3,2},{4,5},{5,4},{6,7},{7,6},{8,9},{9,8},{10,11... | collective-permute-start | bytes 196616 | tf_op jit(solution)/shard_map/ppermute | solution.py:271
  56.3 3.0 %collective-permute-done.16.got = bf16[32,1024]{1,0:T(8,128)(2,1)S(1)} collective-permute-done((bf16[32,1024]{1,0:T(8,128)(2,1)S(1)}, bf16[32,1024]{1,0:T(8,128)(2,1)S(1)}, u32[]{:S(2)}, u32[]{:S(2)}) %collective-permute-start.16) | collective-permute-done | bytes 65568 | tf_op jit(solution)/shard_map/ppermute | solution.py:271
  59.3 1.1 %copy-done = bf16[64,5120]{1,0:T(8,128)(2,1)S(1)} copy-done((bf16[64,5120]{1,0:T(8,128)(2,1)S(1)}, bf16[64,5120]{1,0:T(8,128)(2,1)}, u32[]{:S(2)}) %copy-start) | copy-done | bytes 655384
  60.4 6.9 %embed.2 = bf16[1024,5120]{1,0:T(8,128)(2,1)} custom-call(bf16[32,1024]{1,0:T(8,128)(2,1)S(1)} %get-tuple-element.7.keep, bf16[32,1024]{1,0:T(8,128)(2,1)S(1)} %collective-permute-done.16.got, bf16[64,5120]{1,0:T(8,128)(2,1)S(1)} %copy-done), custom_call_target="tpu_custom_call" | custom-call | tf_op jit(solution)/shard_map/embed/pallas_call | solution.py:237
  (34 shorter events, 4.4 us)
Async XLA Ops:
  0.0 10.1 %collective-permute-start.1 = (bf16[16,4096]{1,0:T(8,128)(2,1)}, bf16[16,4096]{1,0:T(8,128)(2,1)S(1)}, u32[]{:S(2)}, u32[]{:S(2)}) collective-permute-start(bf16[16,4096]{1,0:T(8,128)(2,1)} %latents.1), channel_id=1, source_target_pairs={{0,4},{2,6},{4,0},{6,2},{8,12},{10,14},{12,8},{14,10},{16,20},{18,... | collective-permute-start | bytes 393224 | tf_op jit(solution)/shard_map/ppermute | solution.py:264
  3.7 0.9 %copy-start.3 = (bf16[16,4096]{1,0:T(8,128)(2,1)S(1)}, bf16[16,4096]{1,0:T(8,128)(2,1)}, u32[]{:S(2)}) copy-start(bf16[16,4096]{1,0:T(8,128)(2,1)} %noise.1) | copy-start | bytes 393220
  5.4 7.6 %collective-permute-start.5 = (bf16[16,4096]{1,0:T(8,128)(2,1)S(1)}, bf16[16,4096]{1,0:T(8,128)(2,1)S(1)}, u32[]{:S(2)}, u32[]{:S(2)}) collective-permute-start(bf16[16,4096]{1,0:T(8,128)(2,1)S(1)} %warp.1.refs_4_), channel_id=1, source_target_pairs={{0,24},{2,26},{4,28},{6,30},{8,0},{10,2},{12,4},{14,6},{16,8},{18,... | collective-permute-start | bytes 393224 | tf_op jit(solution)/shard_map/ppermute | solution.py:268
  9.1 10.8 %collective-permute-start.4 = (bf16[16,4096]{1,0:T(8,128)(2,1)S(1)}, bf16[16,4096]{1,0:T(8,128)(2,1)S(1)}, u32[]{:S(2)}, u32[]{:S(2)}) collective-permute-start(bf16[16,4096]{1,0:T(8,128)(2,1)S(1)} %warp.1.refs_4_), channel_id=1, source_target_pairs={{0,16},{2,18},{4,20},{6,22},{8,24},{10,26},{12,28},{14,30},{16,0},... | collective-permute-start | bytes 393224 | tf_op jit(solution)/shard_map/ppermute | solution.py:268
  9.1 10.8 %collective-permute-start.3 = (bf16[16,4096]{1,0:T(8,128)(2,1)S(1)}, bf16[16,4096]{1,0:T(8,128)(2,1)S(1)}, u32[]{:S(2)}, u32[]{:S(2)}) collective-permute-start(bf16[16,4096]{1,0:T(8,128)(2,1)S(1)} %warp.1.refs_4_), channel_id=1, source_target_pairs={{0,8},{2,10},{4,12},{6,14},{8,16},{10,18},{12,20},{14,22},{16,24},... | collective-permute-start | bytes 393224 | tf_op jit(solution)/shard_map/ppermute | solution.py:268
  10.1 9.8 %collective-permute-start = (bf16[16,4096]{1,0:T(8,128)(2,1)}, bf16[16,4096]{1,0:T(8,128)(2,1)S(1)}, u32[]{:S(2)}, u32[]{:S(2)}) collective-permute-start(bf16[16,4096]{1,0:T(8,128)(2,1)} %latents.1), channel_id=1, source_target_pairs={{0,2},{2,0},{4,6},{6,4},{8,10},{10,8},{12,14},{14,12},{16,18},{18,... | collective-permute-start | bytes 393224 | tf_op jit(solution)/shard_map/ppermute | solution.py:261
  10.1 9.8 %collective-permute-start.2 = (bf16[16,4096]{1,0:T(8,128)(2,1)S(1)}, bf16[16,4096]{1,0:T(8,128)(2,1)S(1)}, u32[]{:S(2)}, u32[]{:S(2)}) collective-permute-start(bf16[16,4096]{1,0:T(8,128)(2,1)S(1)} %collective-permute-done.1.refs_2_), channel_id=1, source_target_pairs={{0,2},{2,0},{4,6},{6,4},{8,10},{10,8},{12,14},{14,12},{16,18},{18,... | collective-permute-start | bytes 393224 | tf_op jit(solution)/shard_map/ppermute | solution.py:261
  19.9 0.9 %copy-start.1 = (bf16[16,4096]{1,0:T(8,128)(2,1)S(1)}, bf16[16,4096]{1,0:T(8,128)(2,1)}, u32[]{:S(2)}) copy-start(bf16[16,4096]{1,0:T(8,128)(2,1)} %latents.1) | copy-start | bytes 393220
  22.7 4.2 %collective-permute-start.6 = (f32[32,128]{1,0:T(8,128)S(1)}, f32[32,128]{1,0:T(8,128)S(1)}, u32[]{:S(2)}, u32[]{:S(2)}) collective-permute-start(f32[32,128]{1,0:T(8,128)S(1)} %gram.1), channel_id=1, source_target_pairs={{0,1},{1,0},{2,3},{3,2},{4,5},{5,4},{6,7},{7,6},{8,9},{9,8},{10,11... | collective-permute-start | bytes 49160 | tf_op jit(solution)/shard_map/ppermute | solution.py:271
  24.3 19.8 %collective-permute-start.14 = (bf16[64,4096]{1,0:T(8,128)(2,1)S(1)}, bf16[64,4096]{1,0:T(8,128)(2,1)S(1)}, u32[]{:S(2)}, u32[]{:S(2)}) collective-permute-start(bf16[64,4096]{1,0:T(8,128)(2,1)S(1)} %pad_maximum_fusion.refs_0_), channel_id=1, source_target_pairs={{0,4},{2,6},{4,0},{6,2},{8,12},{10,14},{12,8},{14,10},{16,20},{18,... | collective-permute-start | bytes 1572872 | tf_op jit(solution)/shard_map/ppermute | solution.py:264
  25.0 12.7 %collective-permute-start.8 = (f32[32,128]{1,0:T(8,128)S(1)}, f32[32,128]{1,0:T(8,128)S(1)}, u32[]{:S(2)}, u32[]{:S(2)}) collective-permute-start(f32[32,128]{1,0:T(8,128)S(1)} %gram.1), channel_id=1, source_target_pairs={{0,5},{1,4},{2,7},{3,6},{4,1},{5,0},{6,3},{7,2},{8,13},{9,12},{10,... | collective-permute-start | bytes 49160 | tf_op jit(solution)/shard_map/ppermute | solution.py:275
  26.4 11.5 %collective-permute-start.7 = (f32[32,128]{1,0:T(8,128)S(1)}, f32[32,128]{1,0:T(8,128)S(1)}, u32[]{:S(2)}, u32[]{:S(2)}) collective-permute-start(f32[32,128]{1,0:T(8,128)S(1)} %gram.1), channel_id=1, source_target_pairs={{0,4},{2,6},{4,0},{6,2},{8,12},{10,14},{12,8},{14,10},{16,20},{18,... | collective-permute-start | bytes 49160 | tf_op jit(solution)/shard_map/ppermute | solution.py:264
  37.9 6.2 %collective-permute-start.9 = (f32[64,128]{1,0:T(8,128)S(1)}, f32[64,128]{1,0:T(8,128)S(1)}, u32[]{:S(2)}, u32[]{:S(2)}) collective-permute-start(f32[64,128]{1,0:T(8,128)S(1)} %pad_maximum_fusion.1.refs_0_), channel_id=1, source_target_pairs={{0,8},{2,10},{4,12},{6,14},{8,16},{10,18},{12,20},{14,22},{16,24},... | collective-permute-start | bytes 98312 | tf_op jit(solution)/shard_map/ppermute | solution.py:268
  38.8 10.6 %collective-permute-start.13 = (bf16[64,4096]{1,0:T(8,128)(2,1)S(1)}, bf16[64,4096]{1,0:T(8,128)(2,1)S(1)}, u32[]{:S(2)}, u32[]{:S(2)}) collective-permute-start(bf16[64,4096]{1,0:T(8,128)(2,1)S(1)} %pad_maximum_fusion.refs_0_), channel_id=1, source_target_pairs={{0,2},{2,0},{4,6},{6,4},{8,10},{10,8},{12,14},{14,12},{16,18},{18,... | collective-permute-start | bytes 1572872 | tf_op jit(solution)/shard_map/ppermute | solution.py:261
  38.8 7.8 %collective-permute-start.11 = (f32[64,128]{1,0:T(8,128)S(1)}, f32[64,128]{1,0:T(8,128)S(1)}, u32[]{:S(2)}, u32[]{:S(2)}) collective-permute-start(f32[64,128]{1,0:T(8,128)S(1)} %pad_maximum_fusion.1.refs_0_), channel_id=1, source_target_pairs={{0,24},{2,26},{4,28},{6,30},{8,0},{10,2},{12,4},{14,6},{16,8},{18,... | collective-permute-start | bytes 98312 | tf_op jit(solution)/shard_map/ppermute | solution.py:268
  41.8 4.8 %collective-permute-start.10 = (f32[64,128]{1,0:T(8,128)S(1)}, f32[64,128]{1,0:T(8,128)S(1)}, u32[]{:S(2)}, u32[]{:S(2)}) collective-permute-start(f32[64,128]{1,0:T(8,128)S(1)} %pad_maximum_fusion.1.refs_0_), channel_id=1, source_target_pairs={{0,16},{2,18},{4,20},{6,22},{8,24},{10,26},{12,28},{14,30},{16,0},... | collective-permute-start | bytes 98312 | tf_op jit(solution)/shard_map/ppermute | solution.py:268
  44.1 5.3 %collective-permute-start.15 = (bf16[64,4096]{1,0:T(8,128)(2,1)S(1)}, bf16[64,4096]{1,0:T(8,128)(2,1)S(1)}, u32[]{:S(2)}, u32[]{:S(2)}) collective-permute-start(bf16[64,4096]{1,0:T(8,128)(2,1)S(1)} %collective-permute-done.14.refs_2_), channel_id=1, source_target_pairs={{0,2},{2,0},{4,6},{6,4},{8,10},{10,8},{12,14},{14,12},{16,18},{18,... | collective-permute-start | bytes 1572872 | tf_op jit(solution)/shard_map/ppermute | solution.py:261
  46.6 1.4 %collective-permute-start.12 = (f32[256,128]{1,0:T(8,128)S(1)}, f32[256,128]{1,0:T(8,128)S(1)}, u32[]{:S(2)}, u32[]{:S(2)}) collective-permute-start(f32[256,128]{1,0:T(8,128)S(1)} %constant_dynamic-update-slice_fusion), channel_id=1, source_target_pairs={{0,2},{2,0},{4,6},{6,4},{8,10},{10,8},{12,14},{14,12},{16,18},{18,... | collective-permute-start | bytes 393224 | tf_op jit(solution)/shard_map/ppermute | solution.py:261
  49.4 0.9 %copy-start.2 = (bf16[16,4096]{1,0:T(8,128)(2,1)S(1)}, bf16[16,4096]{1,0:T(8,128)(2,1)}, u32[]{:S(2)}) copy-start(bf16[16,4096]{1,0:T(8,128)(2,1)} %latents.1) | copy-start | bytes 393220
  50.3 0.7 copy-start.4
  55.0 4.3 %collective-permute-start.16 = (bf16[32,1024]{1,0:T(8,128)(2,1)S(1)}, bf16[32,1024]{1,0:T(8,128)(2,1)S(1)}, u32[]{:S(2)}, u32[]{:S(2)}) collective-permute-start(bf16[32,1024]{1,0:T(8,128)(2,1)S(1)} %get-tuple-element.8), channel_id=1, source_target_pairs={{0,1},{1,0},{2,3},{3,2},{4,5},{5,4},{6,7},{7,6},{8,9},{9,8},{10,11... | collective-permute-start | bytes 196616 | tf_op jit(solution)/shard_map/ppermute | solution.py:271
  59.3 1.1 %copy-start = (bf16[64,5120]{1,0:T(8,128)(2,1)S(1)}, bf16[64,5120]{1,0:T(8,128)(2,1)}, u32[]{:S(2)}) copy-start(bf16[64,5120]{1,0:T(8,128)(2,1)} %embed.3) | copy-start | bytes 1966084

commit v2 on v0

v2 whole, which is shorter than its diff:
```python
import functools
import math

import jax
import jax.numpy as jnp
from jax import lax
from jax.experimental import pallas as pl
from jax.experimental.pallas import tpu as pltpu
from jax.sharding import PartitionSpec as P

P_SIZE = 64
D = 5120
FR = 2
GW = 16
GH = 4
ITERS = 4
S = 128
FRAME = GW * GH
SCALE = 2.0 / math.sqrt(P_SIZE * S)
NT = (((1,), (1,)), ((), ()))
TN = (((0,), (0,)), ((), ()))
F32 = jnp.float32
BF16 = jnp.bfloat16
HBM = pl.BlockSpec(memory_space=pltpu.HBM)
VMEM = pl.BlockSpec(memory_space=pltpu.VMEM)
SMEM = pl.BlockSpec(memory_space=pltpu.SMEM)


def params():
    return pltpu.CompilerParams(vmem_limit_bytes=48 * 1024 * 1024)


def lane_sources(offsets, frame, token, clips):
    square = (clips, clips)
    eye = lax.broadcasted_iota(jnp.int32, square, 0) == lax.broadcasted_iota(jnp.int32, square, 1)

    def column(k):
        spread = jnp.where(eye, jnp.broadcast_to(offsets[k : k + 1, :], square), 0)
        return jnp.sum(spread, axis=1, keepdims=True)

    shift_y = jnp.where(frame == 0, column(0), column(2))
    shift_x = jnp.where(frame == 0, column(1), column(3))
    src_row = ((token // GW) - shift_y) & (GH - 1)
    src_col = (token - shift_x) & (GW - 1)
    return frame * FRAME + src_row * GW + src_col


def gather_lanes(tile, source):
    return jnp.take_along_axis(tile, source, axis=1, mode="promise_in_bounds")


def warp_kernel(offsets, noise, out):
    clips, values = noise.shape
    lane = lax.broadcasted_iota(jnp.int32, (clips, S), 1)
    source = lane_sources(offsets, lane // FRAME, lane % FRAME, clips)
    for p in range(values // S):
        cut = slice(p * S, (p + 1) * S)
        out[:, cut] = gather_lanes(noise[:, cut].astype(F32), source).astype(BF16)


def flat_offsets(offsets):
    return offsets.transpose(1, 2, 0).reshape(FR * 2, offsets.shape[0])


def warp_noise(noise, offsets):
    return pl.pallas_call(
        warp_kernel,
        out_shape=jax.ShapeDtypeStruct(noise.shape, BF16),
        in_specs=[VMEM, VMEM],
        out_specs=VMEM,
        compiler_params=params(),
        name="warp",
    )(flat_offsets(offsets), noise)


def split_kernel(offsets, noise, latents, noise_keep, noise_send, lat_keep, lat_send):
    clips, values = noise.shape
    half = values // S // 2
    val = lax.axis_index("val")
    lane = lax.broadcasted_iota(jnp.int32, (clips, S), 1)
    low = lane < FRAME
    keep_from = lane_sources(offsets, val + lane * 0, lane % FRAME, clips)
    send_from = lane_sources(offsets, 1 - val + lane * 0, lane % FRAME, clips)
    for q in range(half):
        near, far = slice(q * S, (q + 1) * S), slice((q + half) * S, (q + half + 1) * S)
        a, b = noise[:, near].astype(F32), noise[:, far].astype(F32)
        noise_keep[:, near] = jnp.where(
            low, gather_lanes(a, keep_from), gather_lanes(b, keep_from)
        ).astype(BF16)
        noise_send[:, near] = jnp.where(
            low, gather_lanes(a, send_from), gather_lanes(b, send_from)
        ).astype(BF16)
    for q in range(half):
        near, far = slice(q * S, (q + 1) * S), slice((q + half) * S, (q + half + 1) * S)
        a, b = latents[:, near].astype(F32), latents[:, far].astype(F32)
        first = jnp.where(low, a, pltpu.roll(b, FRAME, 1))
        second = jnp.where(low, pltpu.roll(a, FRAME, 1), b)
        lat_keep[:, near] = jnp.where(val == 0, first, second).astype(BF16)
        lat_send[:, near] = jnp.where(val == 0, second, first).astype(BF16)


def split_frames(noise, latents, offsets):
    clips, values = noise.shape
    shape = jax.ShapeDtypeStruct((clips, values // 2), BF16)
    return pl.pallas_call(
        split_kernel,
        out_shape=[shape] * 4,
        in_specs=[VMEM] * 3,
        out_specs=[VMEM] * 4,
        compiler_params=params(),
        name="split",
    )(flat_offsets(offsets), noise, latents)


def turn(x, by, lane):
    return jnp.where(lane % 64 >= by, pltpu.roll(x, by, 1), pltpu.roll(x, (by + 64) % 128, 1))


def gram_kernel(clips, lat_own, lat_core, noi_keep, noi_got, out):
    place = lax.axis_index("clip")
    a, x, c = place // 4, (place // 2) % 2, place % 2
    rows, cols = 4 * clips, noi_keep.shape[0]
    cut = noi_keep.shape[1]
    prod = jnp.zeros((rows + cols, cols), F32)
    for h, noi in enumerate((noi_keep, noi_got)):
        lanes = slice(h * cut, (h + 1) * cut)
        right = noi[...]
        left = jnp.concatenate([lat_own[:, lanes], lat_core[:, lanes], right], axis=0)
        prod += lax.dot_general(left, right, NT, preferred_element_type=F32)
    square = (cols, cols)
    eye = lax.broadcasted_iota(jnp.int32, square, 0) == lax.broadcasted_iota(jnp.int32, square, 1)
    norm = jnp.sum(jnp.where(eye, prod[rows:], 0.0), axis=0, keepdims=True)
    part = norm - 2.0 * prod[:rows]
    blocks = [part[k * clips : (k + 1) * clips] for k in range(4)]
    near0 = jnp.where(c == 0, blocks[0], blocks[2])
    near1 = jnp.where(c == 0, blocks[2], blocks[0])
    far0 = jnp.where(c == 0, blocks[1], blocks[3])
    far1 = jnp.where(c == 0, blocks[3], blocks[1])
    near = jnp.concatenate([near0, near1], axis=0)
    far = jnp.concatenate([far0, far1], axis=0)
    packed = jnp.concatenate([jnp.where(x == 0, near, far), jnp.where(x == 0, far, near)], axis=1)
    lane = lax.broadcasted_iota(jnp.int32, packed.shape, 1)
    out[...] = turn(packed, a * clips, lane)


def gram_block(clips, lat_own, lat_core, noi_keep, noi_got):
    return pl.pallas_call(
        functools.partial(gram_kernel, clips),
        out_shape=jax.ShapeDtypeStruct((2 * clips, 128), F32),
        in_specs=[VMEM] * 4,
        out_specs=VMEM,
        compiler_params=params(),
        name="gram",
    )(lat_own, lat_core, noi_keep, noi_got)


def sinkhorn(kernel, own):
    col = jnp.zeros((1, kernel.shape[1]), F32)
    for _ in range(ITERS):
        u = kernel + col
        top = jnp.max(u, axis=1, keepdims=True)
        row = -(top + jnp.log(jnp.sum(jnp.exp(u - top), axis=1, keepdims=True)))
        u = kernel + row
        top = jnp.max(u, axis=0, keepdims=True)
        col = -(top + jnp.log(jnp.sum(jnp.exp(u - top), axis=0, keepdims=True)))
    u = own + col
    top = jnp.max(u, axis=1, keepdims=True)
    e = jnp.exp(u - top)
    return e / jnp.sum(e, axis=1, keepdims=True)


def plan_kernel(clips, mine, other, out, full):
    place = lax.axis_index("clip")
    a, b = place // 4, place % 4
    half = 2 * clips
    low = lax.broadcasted_iota(jnp.int32, (half, 128), 1) < 64
    for s in range(mine.shape[0] // (2 * half)):
        for x in range(2):
            r = s * 2 * half
            g = mine[r + x * half : r + (x + 1) * half, :] * (-SCALE)
            h = other[r + x * half : r + (x + 1) * half, :] * (-SCALE)
            lanes = slice(x * 128, (x + 1) * 128)
            full[r : r + half, lanes] = jnp.where(low, g, pltpu.roll(h, 64, 1))
            full[r + half : r + 2 * half, lanes] = jnp.where(low, pltpu.roll(g, 64, 1), h)
    own = full[pl.ds(pl.multiple_of(b * clips, clips), clips), :]
    weights = sinkhorn(full[...], own)
    lane = lax.broadcasted_iota(jnp.int32, (clips, 128), 1)
    back = (4 - a) % 4 * clips
    for x in range(2):
        lanes = slice(x * 128, (x + 1) * 128)
        out[:, lanes] = turn(weights[:, lanes], back, lane).astype(BF16)


def plan(mine, other, clips):
    n = mine.shape[0]
    return pl.pallas_call(
        functools.partial(plan_kernel, clips),
        out_shape=jax.ShapeDtypeStruct((clips, n), BF16),
        in_specs=[VMEM] * 2,
        out_specs=VMEM,
        scratch_shapes=[pltpu.VMEM((n, n), F32)],
        compiler_params=params(),
        name="plan",
    )(mine, other)


def finish_kernel(clips, block, times, weights, lat, embed, *refs):
    keep, got = refs[:4], refs[4:8]
    out, cube, lhs, table, result, table_sem, sems = refs[8:]
    load = pltpu.make_async_copy(embed, table, table_sem)
    load.start()
    val = lax.axis_index("val")
    row = lax.broadcasted_iota(jnp.int32, (clips, 1), 0)
    t = jnp.zeros((clips, 1), F32)
    for i in range(clips):
        t = jnp.where(row == i, times[i], t)
    w = weights[...]
    cut = keep[0].shape[1]
    step = 256
    for h, parts in enumerate((keep, got)):
        for at in range(0, cut, step):
            panel = jnp.concatenate([p[:, at : at + step] for p in parts], axis=0)
            coupled = jnp.dot(w, panel, preferred_element_type=F32)
            here = h * cut + at
            mixed = (1.0 - t) * lat[:, here : here + step].astype(F32) + t * coupled
            for q in range(step // S):
                cube[:, here // S + q, :] = mixed[:, q * S : (q + 1) * S]
    tiles = 2 * cut // S
    half = tiles // 2
    low = lax.broadcasted_iota(jnp.int32, (tiles, S), 1) < FRAME
    for i in range(0, clips, 2):
        x, y = cube[i], cube[i + 1]
        near = jnp.where(low, x, pltpu.roll(y, FRAME, 1))
        far = jnp.where(low, pltpu.roll(x, FRAME, 1), y)
        mine = jnp.concatenate([near[:half], far[:half]], axis=0)
        other = jnp.concatenate([near[half:], far[half:]], axis=0)
        lanes = slice(i * FRAME, (i + 2) * FRAME)
        lhs[:tiles, lanes] = jnp.where(val == 0, mine, other).astype(BF16)
        lhs[tiles:, lanes] = jnp.where(val == 0, other, mine).astype(BF16)
    load.wait()
    tokens = lhs.shape[1]
    steps = tokens // block

    def store(k):
        at = pl.multiple_of(k * block, block)
        return pltpu.make_async_copy(result.at[k % 2], out.at[pl.ds(at, block)], sems.at[k % 2])

    for k in range(steps):
        if k >= 2:
            store(k - 2).wait()
        result[k % 2] = lax.dot_general(
            lhs[:, k * block : (k + 1) * block], table[...], TN, preferred_element_type=F32
        ).astype(BF16)
        store(k).start()
    for k in range(max(steps - 2, 0), steps):
        store(k).wait()


def finish(times, weights, lat, embed, keep, got, block=128):
    clips, values = lat.shape
    tokens, width = clips * FRAME, embed.shape[1]
    return pl.pallas_call(
        functools.partial(finish_kernel, clips, block),
        out_shape=jax.ShapeDtypeStruct((tokens, width), BF16),
        in_specs=[SMEM, VMEM, VMEM, HBM] + [VMEM] * 8,
        out_specs=HBM,
        scratch_shapes=[
            pltpu.VMEM((clips, values // S, S), F32),
            pltpu.VMEM((P_SIZE, tokens), BF16),
            pltpu.VMEM(embed.shape, BF16),
            pltpu.VMEM((2, block, width), BF16),
            pltpu.SemaphoreType.DMA,
            pltpu.SemaphoreType.DMA((2,)),
        ],
        compiler_params=params(),
        name="finish",
    )(times, weights, lat, embed, *keep, *got)


def flip(n, bit):
    return [(i, i ^ bit) for i in range(n)]


def on_device(n, latents, noise, offsets, times, embed):
    clips = latents.shape[0]
    outer, inner = n // 4, 4

    def core(x):
        return lax.ppermute(x, "clip", flip(n, 1))

    def across(x):
        return lax.ppermute(x, "clip", flip(n, 2))

    def along(x, s):
        hop = [((i + s * inner) % n, i) for i in range(n)]
        return lax.ppermute(x, "clip", hop)

    def line(x):
        return jnp.concatenate([x] + [along(x, s) for s in range(1, outer)], axis=0)

    def other_val(x):
        return lax.ppermute(x, "val", [(0, 1), (1, 0)])

    def other_both(x):
        pairs = [(2 * i + v, 2 * (i ^ 2) + 1 - v) for i in range(n) for v in range(2)]
        return lax.ppermute(x, ("clip", "val"), pairs)

    noi_keep, noi_send, lat_keep, lat_send = split_frames(noise, latents, offsets)
    noi_got = other_val(noi_send)
    keep_line = line(noi_keep)
    got_line = line(noi_got)
    lat = jnp.concatenate([lat_keep, other_val(lat_send)], axis=1)
    lat_own = jnp.concatenate([lat, across(lat)], axis=0)
    keep_across = across(keep_line)
    part = gram_block(clips, lat_own, core(lat_own), keep_line, got_line)
    got_x, got_v, got_b = across(part), other_val(part), other_both(part)
    pair = jnp.concatenate([part + got_v, got_x + got_b], axis=0)
    pair, got_line = lax.optimization_barrier((pair, got_line))
    got_across = across(got_line)
    mine = line(pair)
    weights = plan(mine, core(mine), clips)
    keep = [keep_line, core(keep_line), keep_across, core(keep_across)]
    got = [got_line, core(got_line), got_across, core(got_across)]
    out = finish(times, weights, lat, embed, keep, got)
    return out.reshape(clips, FRAME, embed.shape[1])


def warp_and_gather(latents, noise, offsets, times, embed):
    clips = latents.shape[0]
    warped = warp_noise(noise, offsets)
    panel = lax.all_gather(warped, "clip", axis=0, tiled=True)
    gram = lax.dot_general(latents, panel, NT, preferred_element_type=F32)
    square = jnp.sum(jnp.square(panel.astype(F32)), axis=1)
    part = lax.psum(square[None, :] - 2.0 * gram, "val")
    full = lax.all_gather(part, "clip", axis=0, tiled=True) * (-SCALE)
    weights = sinkhorn(full, part * (-SCALE)).astype(BF16)
    coupled = jnp.dot(weights, panel, preferred_element_type=F32)
    t = times[:, None]
    mixed = ((1.0 - t) * latents.astype(F32) + t * coupled).astype(BF16)
    cube = mixed.reshape(clips, latents.shape[1] // S, S)
    cube = lax.all_to_all(cube, "val", split_axis=2, concat_axis=1, tiled=True)
    return jnp.einsum("cps,pd->csd", cube, embed, preferred_element_type=F32).astype(BF16)


def solution(mesh):
    n, v = mesh.shape["clip"], mesh.shape["val"]
    body = functools.partial(on_device, n) if (n, v) == (16, 2) else warp_and_gather
    placed = (P("clip", "val"), P("clip", "val"), P("clip", None, None), P("clip"), P())
    return jax.shard_map(
        body, mesh=mesh, in_specs=placed, out_specs=P("clip", "val", None), check_vma=False
    )
```

time: 953 us -> 58.2 us (0.06)
  local copies, waits for them, and re-layouts: 628 us -> 4.3 us
  blocking collectives: 251 us -> 0 us
  waiting for transfers between devices: 44.3 us -> 17 us
  starting transfers between devices: 0.01 us -> 26 us
  between operations: 13.6 us -> 0.14 us
  Pallas kernels: 0 us -> 10.5 us
  matrix products: 9.92 us -> 0 us
    gather x1 -> x0, local copies, waits for them, and re-layouts: 625 us -> none  [warp_noise(): return jnp.take_along_axis(value_cube, source, axis=2).reshape(noise.shape)]
    psum x5 -> x0, blocking collectives: 126 us -> none  [the longest x4 118 us: column_lse(): total = lax.psum(jnp.sum(jnp.exp(scores - top[None, :]), axis=0), 'clip')]
    pmax x4 -> x0, blocking collectives: 118 us -> none  [column_lse(): top = lax.pmax(top, 'clip')]
    all_gather x1 -> x0, waiting for transfers between devices: 44.2 us -> none  [on_device(): panel_all = lax.all_gather(warped, 'clip', axis=0, tiled=True)]
    ppermute x0 -> x23, starting transfers between devices: none -> 26 us  [the longest x9 16.1 us: along(): return lax.ppermute(x, 'clip', hop)]
    ppermute x0 -> x23, waiting for transfers between devices: none -> 17 us  [the longest x9 8.86 us: along(): return lax.ppermute(x, 'clip', hop)]
    pallas_call x0 -> x4, Pallas kernels: none -> 10.5 us  [the longest x1 8.18 us: finish(): pl.pallas_call(functools.partial(finish_kernel, clips, block), out_shape=...]
    dot_general x3 -> x0, matrix products: 9.92 us -> none  [the longest x1 5.65 us: on_device(): jnp.einsum('cps,pd->csd', lax.all_to_all(value_cube, 'val', split_axis=2,...]
  transfers between devices with their start and end apart: 1 -> 23, of which waited for: 1 -> 10; matrix products, arithmetic and copies ran while one was open for 0% -> 0% of each run, Pallas kernels for 0% -> 3%
where the time goes in v2:
time: 58.2 us; the launch traced here: 58 us
  starting transfers between devices  26 us (45%)
  waiting for transfers between devices  17 us (29%)
  Pallas kernels  10.5 us (18%)
  local copies, waits for them, and re-layouts  4.3 us (7%)
    ppermute x9, starting transfers between devices, along(): return lax.ppermute(x, 'clip', hop)  16.1 us
    ppermute x9, waiting for transfers between devices, along(): return lax.ppermute(x, 'clip', hop)  8.86 us
    pallas_call x1, Pallas kernels, finish(): pl.pallas_call(functools.partial(finish_kernel, clips, block), out_shape=...  8.18 us
    unnamed x20, local copies, waits for them, and re-layouts  4.27 us
    ppermute x4, starting transfers between devices, across(): return lax.ppermute(x, 'clip', flip(n, 2))  3.66 us
    ppermute x3, starting transfers between devices, other_val(): return lax.ppermute(x, 'val', [(0, 1), (1, 0)])  3.56 us
    ppermute x6, waiting for transfers between devices, core(): return lax.ppermute(x, 'clip', flip(n, 1))  2.74 us
    ppermute x1, waiting for transfers between devices, other_both(): return lax.ppermute(x, ('clip', 'val'), pairs)  2.49 us
  transfers between devices with their start and end apart: 23, of which 10 were waited for; matrix products, arithmetic and copies ran while one was open for 0% of the time, Pallas kernels for 3%

profile of v2, /device:TPU:0, one launch (start us, length us, event | category | flops | bytes accessed | tf_op | source)
XLA Modules:
  0.0 58.0 jit_solution(6197236401458906754)
XLA Ops:
  0.0 0.9 %copy-done.1 = bf16[16,4096]{1,0:T(8,128)(2,1)S(1)} copy-done((bf16[16,4096]{1,0:T(8,128)(2,1)S(1)}, bf16[16,4096]{1,0:T(8,128)(2,1)}, u32[]{:S(2)}) %copy-start.1) | copy-done | bytes 131096
  2.9 3.1 %collective-permute-start.5 = (bf16[16,2048]{1,0:T(8,128)(2,1)S(1)}, bf16[16,2048]{1,0:T(8,128)(2,1)S(1)}, u32[]{:S(2)}, u32[]{:S(2)}) collective-permute-start(bf16[16,2048]{1,0:T(8,128)(2,1)S(1)} %get-tuple-element.13), channel_id=1, source_target_pairs={{24,0},{26,2},{28,4},{30,6},{0,8},{2,10},{4,12},{6,14},{8,16},{10,... | collective-permute-start | bytes 196616 | tf_op jit(solution)/shard_map/ppermute | solution.py:296
  5.9 2.6 %collective-permute-start.4 = (bf16[16,2048]{1,0:T(8,128)(2,1)S(1)}, bf16[16,2048]{1,0:T(8,128)(2,1)S(1)}, u32[]{:S(2)}, u32[]{:S(2)}) collective-permute-start(bf16[16,2048]{1,0:T(8,128)(2,1)S(1)} %get-tuple-element.13), channel_id=1, source_target_pairs={{16,0},{18,2},{20,4},{22,6},{24,8},{26,10},{28,12},{30,14},{0,16},... | collective-permute-start | bytes 196616 | tf_op jit(solution)/shard_map/ppermute | solution.py:296
  8.5 1.3 %collective-permute-start.3 = (bf16[16,2048]{1,0:T(8,128)(2,1)S(1)}, bf16[16,2048]{1,0:T(8,128)(2,1)S(1)}, u32[]{:S(2)}, u32[]{:S(2)}) collective-permute-start(bf16[16,2048]{1,0:T(8,128)(2,1)S(1)} %get-tuple-element.13), channel_id=1, source_target_pairs={{8,0},{10,2},{12,4},{14,6},{16,8},{18,10},{20,12},{22,14},{24,16},... | collective-permute-start | bytes 196616 | tf_op jit(solution)/shard_map/ppermute | solution.py:296
  9.9 1.5 %collective-permute-start = (bf16[16,2048]{1,0:T(8,128)(2,1)S(1)}, bf16[16,2048]{1,0:T(8,128)(2,1)S(1)}, u32[]{:S(2)}, u32[]{:S(2)}) collective-permute-start(bf16[16,2048]{1,0:T(8,128)(2,1)S(1)} %get-tuple-element.12), channel_id=1, source_target_pairs={{0,1},{1,0},{2,3},{3,2},{4,5},{5,4},{6,7},{7,6},{8,9},{9,8},{10,11... | collective-permute-start | bytes 196616 | tf_op jit(solution)/shard_map/ppermute | solution.py:302
  11.9 2.2 %collective-permute-done = bf16[16,2048]{1,0:T(8,128)(2,1)S(1)} collective-permute-done((bf16[16,2048]{1,0:T(8,128)(2,1)S(1)}, bf16[16,2048]{1,0:T(8,128)(2,1)S(1)}, u32[]{:S(2)}, u32[]{:S(2)}) %collective-permute-start) | collective-permute-done | bytes 65568 | tf_op jit(solution)/shard_map/ppermute | solution.py:302
  14.2 1.5 %collective-permute-start.1 = (bf16[16,4096]{1,0:T(8,128)(2,1)S(1)}, bf16[16,4096]{1,0:T(8,128)(2,1)S(1)}, u32[]{:S(2)}, u32[]{:S(2)}) collective-permute-start(bf16[16,4096]{1,0:T(8,128)(2,1)S(1)} %constant_dynamic-update-slice_fusion.lat), channel_id=1, source_target_pairs={{0,4},{2,6},{4,0},{6,2},{8,12},{10,14},{12,8},{14,10},{16,20},{18,... | collective-permute-start | bytes 393224 | tf_op jit(solution)/shard_map/ppermute | solution.py:292
  17.0 1.5 %collective-permute-start.8 = (bf16[16,2048]{1,0:T(8,128)(2,1)S(1)}, bf16[16,2048]{1,0:T(8,128)(2,1)S(1)}, u32[]{:S(2)}, u32[]{:S(2)}) collective-permute-start(bf16[16,2048]{1,0:T(8,128)(2,1)S(1)} %collective-permute-done.6), channel_id=1, source_target_pairs={{16,0},{18,2},{20,4},{22,6},{24,8},{26,10},{28,12},{30,14},{0,16},... | collective-permute-start | bytes 196616 | tf_op jit(solution)/shard_map/ppermute | solution.py:296
  18.4 1.7 %collective-permute-start.7 = (bf16[16,2048]{1,0:T(8,128)(2,1)S(1)}, bf16[16,2048]{1,0:T(8,128)(2,1)S(1)}, u32[]{:S(2)}, u32[]{:S(2)}) collective-permute-start(bf16[16,2048]{1,0:T(8,128)(2,1)S(1)} %collective-permute-done.6), channel_id=1, source_target_pairs={{8,0},{10,2},{12,4},{14,6},{16,8},{18,10},{20,12},{22,14},{24,16},... | collective-permute-start | bytes 196616 | tf_op jit(solution)/shard_map/ppermute | solution.py:296
  20.1 3.0 %collective-permute-done.7 = bf16[16,2048]{1,0:T(8,128)(2,1)S(1)} collective-permute-done((bf16[16,2048]{1,0:T(8,128)(2,1)S(1)}, bf16[16,2048]{1,0:T(8,128)(2,1)S(1)}, u32[]{:S(2)}, u32[]{:S(2)}) %collective-permute-start.7) | collective-permute-done | bytes 65568 | tf_op jit(solution)/shard_map/ppermute | solution.py:296
  23.6 1.2 %collective-permute-done.2.lat_core = bf16[32,4096]{1,0:T(8,128)(2,1)S(1)} collective-permute-done((bf16[32,4096]{1,0:T(8,128)(2,1)S(1)}, bf16[32,4096]{1,0:T(8,128)(2,1)S(1)}, u32[]{:S(2)}, u32[]{:S(2)}) %collective-permute-start.2) | collective-permute-done | bytes 262176 | tf_op jit(solution)/shard_map/ppermute | solution.py:289
  25.4 1.5 %collective-permute-start.10 = (f32[32,128]{1,0:T(8,128)S(1)}, f32[32,128]{1,0:T(8,128)S(1)}, u32[]{:S(2)}, u32[]{:S(2)}) collective-permute-start(f32[32,128]{1,0:T(8,128)S(1)} %gram.1), channel_id=1, source_target_pairs={{0,1},{1,0},{2,3},{3,2},{4,5},{5,4},{6,7},{7,6},{8,9},{9,8},{10,11... | collective-permute-start | bytes 49160 | tf_op jit(solution)/shard_map/ppermute | solution.py:302
  26.9 1.4 %collective-permute-start.12 = (f32[32,128]{1,0:T(8,128)S(1)}, f32[32,128]{1,0:T(8,128)S(1)}, u32[]{:S(2)}, u32[]{:S(2)}) collective-permute-start(f32[32,128]{1,0:T(8,128)S(1)} %gram.1), channel_id=1, source_target_pairs={{0,5},{1,4},{2,7},{3,6},{4,1},{5,0},{6,3},{7,2},{8,13},{9,12},{10,... | collective-permute-start | bytes 49160 | tf_op jit(solution)/shard_map/ppermute | solution.py:306
  29.1 2.5 %collective-permute-done.12 = f32[32,128]{1,0:T(8,128)S(1)} collective-permute-done((f32[32,128]{1,0:T(8,128)S(1)}, f32[32,128]{1,0:T(8,128)S(1)}, u32[]{:S(2)}, u32[]{:S(2)}) %collective-permute-start.12) | collective-permute-done | bytes 16416 | tf_op jit(solution)/shard_map/ppermute | solution.py:306
  32.1 1.0 %collective-permute-start.21 = (bf16[64,2048]{1,0:T(8,128)(2,1)S(1)}, bf16[64,2048]{1,0:T(8,128)(2,1)S(1)}, u32[]{:S(2)}, u32[]{:S(2)}) collective-permute-start(bf16[64,2048]{1,0:T(8,128)(2,1)S(1)} %constant_dynamic-update-slice_fusion.6.noi_got.refs_4_), channel_id=1, source_target_pairs={{0,4},{2,6},{4,0},{6,2},{8,12},{10,14},{12,8},{14,10},{16,20},{18,... | collective-permute-start | bytes 786440 | tf_op jit(solution)/shard_map/ppermute | solution.py:292
  33.7 1.8 %collective-permute-start.15 = (f32[64,128]{1,0:T(8,128)S(1)}, f32[64,128]{1,0:T(8,128)S(1)}, u32[]{:S(2)}, u32[]{:S(2)}) collective-permute-start(f32[64,128]{1,0:T(8,128)S(1)} %pad_maximum_fusion.1), channel_id=1, source_target_pairs={{24,0},{26,2},{28,4},{30,6},{0,8},{2,10},{4,12},{6,14},{8,16},{10,... | collective-permute-start | bytes 98312 | tf_op jit(solution)/shard_map/ppermute | solution.py:296
  35.4 2.0 %collective-permute-start.13 = (f32[64,128]{1,0:T(8,128)S(1)}, f32[64,128]{1,0:T(8,128)S(1)}, u32[]{:S(2)}, u32[]{:S(2)}) collective-permute-start(f32[64,128]{1,0:T(8,128)S(1)} %pad_maximum_fusion.1), channel_id=1, source_target_pairs={{8,0},{10,2},{12,4},{14,6},{16,8},{18,10},{20,12},{22,14},{24,16},... | collective-permute-start | bytes 98312 | tf_op jit(solution)/shard_map/ppermute | solution.py:296
  37.5 2.2 %collective-permute-done.13 = f32[64,128]{1,0:T(8,128)S(1)} collective-permute-done((f32[64,128]{1,0:T(8,128)S(1)}, f32[64,128]{1,0:T(8,128)S(1)}, u32[]{:S(2)}, u32[]{:S(2)}) %collective-permute-start.13) | collective-permute-done | bytes 32800 | tf_op jit(solution)/shard_map/ppermute | solution.py:296
  39.7 1.5 %collective-permute-start.14 = (f32[64,128]{1,0:T(8,128)S(1)}, f32[64,128]{1,0:T(8,128)S(1)}, u32[]{:S(2)}, u32[]{:S(2)}) collective-permute-start(f32[64,128]{1,0:T(8,128)S(1)} %pad_maximum_fusion.1), channel_id=1, source_target_pairs={{16,0},{18,2},{20,4},{22,6},{24,8},{26,10},{28,12},{30,14},{0,16},... | collective-permute-start | bytes 98312 | tf_op jit(solution)/shard_map/ppermute | solution.py:296
  41.2 3.3 %collective-permute-done.14 = f32[64,128]{1,0:T(8,128)S(1)} collective-permute-done((f32[64,128]{1,0:T(8,128)S(1)}, f32[64,128]{1,0:T(8,128)S(1)}, u32[]{:S(2)}, u32[]{:S(2)}) %collective-permute-start.14) | collective-permute-done | bytes 32800 | tf_op jit(solution)/shard_map/ppermute | solution.py:296
  45.1 1.5 %collective-permute-done.16.other = f32[256,128]{1,0:T(8,128)S(1)} collective-permute-done((f32[256,128]{1,0:T(8,128)S(1)}, f32[256,128]{1,0:T(8,128)S(1)}, u32[]{:S(2)}, u32[]{:S(2)}) %collective-permute-start.16) | collective-permute-done | bytes 131104 | tf_op jit(solution)/shard_map/ppermute | solution.py:289
  46.6 1.4 %plan.1.weights = bf16[16,256]{1,0:T(8,128)(2,1)S(1)} custom-call(f32[256,128]{1,0:T(8,128)S(1)} %constant_dynamic-update-slice_fusion.10.mine, f32[256,128]{1,0:T(8,128)S(1)} %collective-permute-done.16.other), custom_call_target="tpu_custom_call" | custom-call | tf_op jit(solution)/shard_map/plan/pallas_call | solution.py:196
  48.1 1.1 %copy-done = bf16[64,5120]{1,0:T(8,128)(2,1)S(1)} copy-done((bf16[64,5120]{1,0:T(8,128)(2,1)S(1)}, bf16[64,5120]{1,0:T(8,128)(2,1)}, u32[]{:S(2)}) %copy-start) | copy-done | bytes 655384
  49.8 8.2 %finish.1 = bf16[1024,5120]{1,0:T(8,128)(2,1)} custom-call(f32[16]{0:T(128)S(1)} %copy-done.4, bf16[16,256]{1,0:T(8,128)(2,1)S(1)} %plan.1.weights, bf16[16,4096]{1,0:T(8,128)(2,1)S(1)} %constant_dynamic-update-slice_fusion.lat, bf16[64,5120]{1,0:T(8,128)(2,1)S(1)} %copy-done, bf16[64,2048]{1,0:T(8,128)(2,1)S(1)} %constant_dynamic-update-slice_fusion.2.noi_keep.refs_0_, ...), custom_call_target="tpu_custom_call" | custom-call | tf_op jit(solution)/shard_map/finish/pallas_call | solution.py:262
  (54 shorter events, 7.8 us)
Async XLA Ops:
  2.9 12.8 %collective-permute-start.5 = (bf16[16,2048]{1,0:T(8,128)(2,1)S(1)}, bf16[16,2048]{1,0:T(8,128)(2,1)S(1)}, u32[]{:S(2)}, u32[]{:S(2)}) collective-permute-start(bf16[16,2048]{1,0:T(8,128)(2,1)S(1)} %get-tuple-element.13), channel_id=1, source_target_pairs={{24,0},{26,2},{28,4},{30,6},{0,8},{2,10},{4,12},{6,14},{8,16},{10,... | collective-permute-start | bytes 196616 | tf_op jit(solution)/shard_map/ppermute | solution.py:296
  5.9 9.7 %collective-permute-start.4 = (bf16[16,2048]{1,0:T(8,128)(2,1)S(1)}, bf16[16,2048]{1,0:T(8,128)(2,1)S(1)}, u32[]{:S(2)}, u32[]{:S(2)}) collective-permute-start(bf16[16,2048]{1,0:T(8,128)(2,1)S(1)} %get-tuple-element.13), channel_id=1, source_target_pairs={{16,0},{18,2},{20,4},{22,6},{24,8},{26,10},{28,12},{30,14},{0,16},... | collective-permute-start | bytes 196616 | tf_op jit(solution)/shard_map/ppermute | solution.py:296
  8.5 7.1 %collective-permute-start.3 = (bf16[16,2048]{1,0:T(8,128)(2,1)S(1)}, bf16[16,2048]{1,0:T(8,128)(2,1)S(1)}, u32[]{:S(2)}, u32[]{:S(2)}) collective-permute-start(bf16[16,2048]{1,0:T(8,128)(2,1)S(1)} %get-tuple-element.13), channel_id=1, source_target_pairs={{8,0},{10,2},{12,4},{14,6},{16,8},{18,10},{20,12},{22,14},{24,16},... | collective-permute-start | bytes 196616 | tf_op jit(solution)/shard_map/ppermute | solution.py:296
  9.9 4.3 %collective-permute-start = (bf16[16,2048]{1,0:T(8,128)(2,1)S(1)}, bf16[16,2048]{1,0:T(8,128)(2,1)S(1)}, u32[]{:S(2)}, u32[]{:S(2)}) collective-permute-start(bf16[16,2048]{1,0:T(8,128)(2,1)S(1)} %get-tuple-element.12), channel_id=1, source_target_pairs={{0,1},{1,0},{2,3},{3,2},{4,5},{5,4},{6,7},{7,6},{8,9},{9,8},{10,11... | collective-permute-start | bytes 196616 | tf_op jit(solution)/shard_map/ppermute | solution.py:302
  11.4 4.9 %collective-permute-start.6 = (bf16[16,2048]{1,0:T(8,128)(2,1)S(1)}, bf16[16,2048]{1,0:T(8,128)(2,1)S(1)}, u32[]{:S(2)}, u32[]{:S(2)}) collective-permute-start(bf16[16,2048]{1,0:T(8,128)(2,1)S(1)} %get-tuple-element.14), channel_id=1, source_target_pairs={{0,1},{1,0},{2,3},{3,2},{4,5},{5,4},{6,7},{7,6},{8,9},{9,8},{10,11... | collective-permute-start | bytes 196616 | tf_op jit(solution)/shard_map/ppermute | solution.py:302
  14.2 9.0 %collective-permute-start.1 = (bf16[16,4096]{1,0:T(8,128)(2,1)S(1)}, bf16[16,4096]{1,0:T(8,128)(2,1)S(1)}, u32[]{:S(2)}, u32[]{:S(2)}) collective-permute-start(bf16[16,4096]{1,0:T(8,128)(2,1)S(1)} %constant_dynamic-update-slice_fusion.lat), channel_id=1, source_target_pairs={{0,4},{2,6},{4,0},{6,2},{8,12},{10,14},{12,8},{14,10},{16,20},{18,... | collective-permute-start | bytes 393224 | tf_op jit(solution)/shard_map/ppermute | solution.py:292
  15.7 17.4 %collective-permute-start.18 = (bf16[64,2048]{1,0:T(8,128)(2,1)S(1)}, bf16[64,2048]{1,0:T(8,128)(2,1)S(1)}, u32[]{:S(2)}, u32[]{:S(2)}) collective-permute-start(bf16[64,2048]{1,0:T(8,128)(2,1)S(1)} %constant_dynamic-update-slice_fusion.2.noi_keep.refs_0_), channel_id=1, source_target_pairs={{0,4},{2,6},{4,0},{6,2},{8,12},{10,14},{12,8},{14,10},{16,20},{18,... | collective-permute-start | bytes 786440 | tf_op jit(solution)/shard_map/ppermute | solution.py:292
  16.3 7.3 %collective-permute-start.9 = (bf16[16,2048]{1,0:T(8,128)(2,1)S(1)}, bf16[16,2048]{1,0:T(8,128)(2,1)S(1)}, u32[]{:S(2)}, u32[]{:S(2)}) collective-permute-start(bf16[16,2048]{1,0:T(8,128)(2,1)S(1)} %collective-permute-done.6), channel_id=1, source_target_pairs={{24,0},{26,2},{28,4},{30,6},{0,8},{2,10},{4,12},{6,14},{8,16},{10,... | collective-permute-start | bytes 196616 | tf_op jit(solution)/shard_map/ppermute | solution.py:296
  17.0 6.6 %collective-permute-start.8 = (bf16[16,2048]{1,0:T(8,128)(2,1)S(1)}, bf16[16,2048]{1,0:T(8,128)(2,1)S(1)}, u32[]{:S(2)}, u32[]{:S(2)}) collective-permute-start(bf16[16,2048]{1,0:T(8,128)(2,1)S(1)} %collective-permute-done.6), channel_id=1, source_target_pairs={{16,0},{18,2},{20,4},{22,6},{24,8},{26,10},{28,12},{30,14},{0,16},... | collective-permute-start | bytes 196616 | tf_op jit(solution)/shard_map/ppermute | solution.py:296
  18.4 4.7 %collective-permute-start.7 = (bf16[16,2048]{1,0:T(8,128)(2,1)S(1)}, bf16[16,2048]{1,0:T(8,128)(2,1)S(1)}, u32[]{:S(2)}, u32[]{:S(2)}) collective-permute-start(bf16[16,2048]{1,0:T(8,128)(2,1)S(1)} %collective-permute-done.6), channel_id=1, source_target_pairs={{8,0},{10,2},{12,4},{14,6},{16,8},{18,10},{20,12},{22,14},{24,16},... | collective-permute-start | bytes 196616 | tf_op jit(solution)/shard_map/ppermute | solution.py:296
  23.2 1.6 %collective-permute-start.2 = (bf16[32,4096]{1,0:T(8,128)(2,1)S(1)}, bf16[32,4096]{1,0:T(8,128)(2,1)S(1)}, u32[]{:S(2)}, u32[]{:S(2)}) collective-permute-start(bf16[32,4096]{1,0:T(8,128)(2,1)S(1)} %pad_maximum_fusion.lat_own), channel_id=1, source_target_pairs={{0,2},{2,0},{4,6},{6,4},{8,10},{10,8},{12,14},{14,12},{16,18},{18,... | collective-permute-start | bytes 786440 | tf_op jit(solution)/shard_map/ppermute | solution.py:289
  25.4 3.8 %collective-permute-start.10 = (f32[32,128]{1,0:T(8,128)S(1)}, f32[32,128]{1,0:T(8,128)S(1)}, u32[]{:S(2)}, u32[]{:S(2)}) collective-permute-start(f32[32,128]{1,0:T(8,128)S(1)} %gram.1), channel_id=1, source_target_pairs={{0,1},{1,0},{2,3},{3,2},{4,5},{5,4},{6,7},{7,6},{8,9},{9,8},{10,11... | collective-permute-start | bytes 49160 | tf_op jit(solution)/shard_map/ppermute | solution.py:302
  26.9 4.7 %collective-permute-start.12 = (f32[32,128]{1,0:T(8,128)S(1)}, f32[32,128]{1,0:T(8,128)S(1)}, u32[]{:S(2)}, u32[]{:S(2)}) collective-permute-start(f32[32,128]{1,0:T(8,128)S(1)} %gram.1), channel_id=1, source_target_pairs={{0,5},{1,4},{2,7},{3,6},{4,1},{5,0},{6,3},{7,2},{8,13},{9,12},{10,... | collective-permute-start | bytes 49160 | tf_op jit(solution)/shard_map/ppermute | solution.py:306
  28.4 3.7 %collective-permute-start.11 = (f32[32,128]{1,0:T(8,128)S(1)}, f32[32,128]{1,0:T(8,128)S(1)}, u32[]{:S(2)}, u32[]{:S(2)}) collective-permute-start(f32[32,128]{1,0:T(8,128)S(1)} %gram.1), channel_id=1, source_target_pairs={{0,4},{2,6},{4,0},{6,2},{8,12},{10,14},{12,8},{14,10},{16,20},{18,... | collective-permute-start | bytes 49160 | tf_op jit(solution)/shard_map/ppermute | solution.py:292
  32.1 12.4 %collective-permute-start.21 = (bf16[64,2048]{1,0:T(8,128)(2,1)S(1)}, bf16[64,2048]{1,0:T(8,128)(2,1)S(1)}, u32[]{:S(2)}, u32[]{:S(2)}) collective-permute-start(bf16[64,2048]{1,0:T(8,128)(2,1)S(1)} %constant_dynamic-update-slice_fusion.6.noi_got.refs_4_), channel_id=1, source_target_pairs={{0,4},{2,6},{4,0},{6,2},{8,12},{10,14},{12,8},{14,10},{16,20},{18,... | collective-permute-start | bytes 786440 | tf_op jit(solution)/shard_map/ppermute | solution.py:292
  33.1 14.9 %collective-permute-start.17 = (bf16[64,2048]{1,0:T(8,128)(2,1)S(1)}, bf16[64,2048]{1,0:T(8,128)(2,1)S(1)}, u32[]{:S(2)}, u32[]{:S(2)}) collective-permute-start(bf16[64,2048]{1,0:T(8,128)(2,1)S(1)} %constant_dynamic-update-slice_fusion.2.noi_keep.refs_0_), channel_id=1, source_target_pairs={{0,2},{2,0},{4,6},{6,4},{8,10},{10,8},{12,14},{14,12},{16,18},{18,... | collective-permute-start | bytes 786440 | tf_op jit(solution)/shard_map/ppermute | solution.py:289
  33.1 14.9 %collective-permute-start.19 = (bf16[64,2048]{1,0:T(8,128)(2,1)S(1)}, bf16[64,2048]{1,0:T(8,128)(2,1)S(1)}, u32[]{:S(2)}, u32[]{:S(2)}) collective-permute-start(bf16[64,2048]{1,0:T(8,128)(2,1)S(1)} %collective-permute-done.18.refs_2_), channel_id=1, source_target_pairs={{0,2},{2,0},{4,6},{6,4},{8,10},{10,8},{12,14},{14,12},{16,18},{18,... | collective-permute-start | bytes 786440 | tf_op jit(solution)/shard_map/ppermute | solution.py:289
  33.7 11.4 %collective-permute-start.15 = (f32[64,128]{1,0:T(8,128)S(1)}, f32[64,128]{1,0:T(8,128)S(1)}, u32[]{:S(2)}, u32[]{:S(2)}) collective-permute-start(f32[64,128]{1,0:T(8,128)S(1)} %pad_maximum_fusion.1), channel_id=1, source_target_pairs={{24,0},{26,2},{28,4},{30,6},{0,8},{2,10},{4,12},{6,14},{8,16},{10,... | collective-permute-start | bytes 98312 | tf_op jit(solution)/shard_map/ppermute | solution.py:296
  35.4 4.2 %collective-permute-start.13 = (f32[64,128]{1,0:T(8,128)S(1)}, f32[64,128]{1,0:T(8,128)S(1)}, u32[]{:S(2)}, u32[]{:S(2)}) collective-permute-start(f32[64,128]{1,0:T(8,128)S(1)} %pad_maximum_fusion.1), channel_id=1, source_target_pairs={{8,0},{10,2},{12,4},{14,6},{16,8},{18,10},{20,12},{22,14},{24,16},... | collective-permute-start | bytes 98312 | tf_op jit(solution)/shard_map/ppermute | solution.py:296
  39.7 4.8 %collective-permute-start.14 = (f32[64,128]{1,0:T(8,128)S(1)}, f32[64,128]{1,0:T(8,128)S(1)}, u32[]{:S(2)}, u32[]{:S(2)}) collective-permute-start(f32[64,128]{1,0:T(8,128)S(1)} %pad_maximum_fusion.1), channel_id=1, source_target_pairs={{16,0},{18,2},{20,4},{22,6},{24,8},{26,10},{28,12},{30,14},{0,16},... | collective-permute-start | bytes 98312 | tf_op jit(solution)/shard_map/ppermute | solution.py:296
  44.5 3.5 %collective-permute-start.20 = (bf16[64,2048]{1,0:T(8,128)(2,1)S(1)}, bf16[64,2048]{1,0:T(8,128)(2,1)S(1)}, u32[]{:S(2)}, u32[]{:S(2)}) collective-permute-start(bf16[64,2048]{1,0:T(8,128)(2,1)S(1)} %constant_dynamic-update-slice_fusion.6.noi_got.refs_4_), channel_id=1, source_target_pairs={{0,2},{2,0},{4,6},{6,4},{8,10},{10,8},{12,14},{14,12},{16,18},{18,... | collective-permute-start | bytes 786440 | tf_op jit(solution)/shard_map/ppermute | solution.py:289
  44.5 3.5 %collective-permute-start.22 = (bf16[64,2048]{1,0:T(8,128)(2,1)S(1)}, bf16[64,2048]{1,0:T(8,128)(2,1)S(1)}, u32[]{:S(2)}, u32[]{:S(2)}) collective-permute-start(bf16[64,2048]{1,0:T(8,128)(2,1)S(1)} %collective-permute-done.21.refs_6_), channel_id=1, source_target_pairs={{0,2},{2,0},{4,6},{6,4},{8,10},{10,8},{12,14},{14,12},{16,18},{18,... | collective-permute-start | bytes 786440 | tf_op jit(solution)/shard_map/ppermute | solution.py:289
  45.0 1.6 %collective-permute-start.16 = (f32[256,128]{1,0:T(8,128)S(1)}, f32[256,128]{1,0:T(8,128)S(1)}, u32[]{:S(2)}, u32[]{:S(2)}) collective-permute-start(f32[256,128]{1,0:T(8,128)S(1)} %constant_dynamic-update-slice_fusion.10.mine), channel_id=1, source_target_pairs={{0,2},{2,0},{4,6},{6,4},{8,10},{10,8},{12,14},{14,12},{16,18},{18,... | collective-permute-start | bytes 393224 | tf_op jit(solution)/shard_map/ppermute | solution.py:289
  48.1 1.1 %copy-start = (bf16[64,5120]{1,0:T(8,128)(2,1)S(1)}, bf16[64,5120]{1,0:T(8,128)(2,1)}, u32[]{:S(2)}) copy-start(bf16[64,5120]{1,0:T(8,128)(2,1)} %embed.1) | copy-start | bytes 1966084
  (4 other events, 3.1 us)

commit v3 on v2

v3 whole, which is shorter than its diff:
```python
import functools
import math

import jax
import jax.numpy as jnp
from jax import lax
from jax.experimental import pallas as pl
from jax.experimental.pallas import tpu as pltpu
from jax.sharding import PartitionSpec as P

P_SIZE = 64
D = 5120
FR = 2
GW = 16
GH = 4
ITERS = 4
S = 128
FRAME = GW * GH
SCALE = 2.0 / math.sqrt(P_SIZE * S)
NT = (((1,), (1,)), ((), ()))
TN = (((0,), (0,)), ((), ()))
F32 = jnp.float32
BF16 = jnp.bfloat16
HBM = pl.BlockSpec(memory_space=pltpu.HBM)
VMEM = pl.BlockSpec(memory_space=pltpu.VMEM)
SMEM = pl.BlockSpec(memory_space=pltpu.SMEM)


def params(mib=48):
    return pltpu.CompilerParams(vmem_limit_bytes=mib * 1024 * 1024)


def cost(us):
    return pl.CostEstimate(flops=0, bytes_accessed=us * 3_500_000, transcendentals=0)


def lane_sources(offsets, frame, token, clips):
    square = (clips, clips)
    eye = lax.broadcasted_iota(jnp.int32, square, 0) == lax.broadcasted_iota(jnp.int32, square, 1)

    def column(k):
        spread = jnp.where(eye, jnp.broadcast_to(offsets[k : k + 1, :], square), 0)
        return jnp.sum(spread, axis=1, keepdims=True)

    shift_y = jnp.where(frame == 0, column(0), column(2))
    shift_x = jnp.where(frame == 0, column(1), column(3))
    src_row = ((token // GW) - shift_y) & (GH - 1)
    src_col = (token - shift_x) & (GW - 1)
    return frame * FRAME + src_row * GW + src_col


def gather_lanes(tile, source):
    return jnp.take_along_axis(tile, source, axis=1, mode="promise_in_bounds")


def warp_kernel(offsets, noise, out):
    clips, values = noise.shape
    lane = lax.broadcasted_iota(jnp.int32, (clips, S), 1)
    source = lane_sources(offsets, lane // FRAME, lane % FRAME, clips)
    for p in range(values // S):
        cut = slice(p * S, (p + 1) * S)
        out[:, cut] = gather_lanes(noise[:, cut].astype(F32), source).astype(BF16)


def flat_offsets(offsets):
    return offsets.transpose(1, 2, 0).reshape(FR * 2, offsets.shape[0])


def warp_noise(noise, offsets):
    return pl.pallas_call(
        warp_kernel,
        out_shape=jax.ShapeDtypeStruct(noise.shape, BF16),
        in_specs=[VMEM, VMEM],
        out_specs=VMEM,
        compiler_params=params(),
        name="warp",
    )(flat_offsets(offsets), noise)


def warp_frame(offsets, noise, frame, out):
    clips, values = noise.shape
    half = values // S // 2
    lane = lax.broadcasted_iota(jnp.int32, (clips, S), 1)
    low = lane < FRAME
    source = lane_sources(offsets, frame + lane * 0, lane % FRAME, clips)
    for q in range(half):
        near, far = slice(q * S, (q + 1) * S), slice((q + half) * S, (q + half + 1) * S)
        a, b = noise[:, near].astype(F32), noise[:, far].astype(F32)
        out[:, near] = jnp.where(low, gather_lanes(a, source), gather_lanes(b, source)).astype(BF16)


def take_frame(latents, frame, out):
    clips, values = latents.shape
    half = values // S // 2
    low = lax.broadcasted_iota(jnp.int32, (clips, S), 1) < FRAME
    for q in range(half):
        near, far = slice(q * S, (q + 1) * S), slice((q + half) * S, (q + half + 1) * S)
        a, b = latents[:, near].astype(F32), latents[:, far].astype(F32)
        first = jnp.where(low, a, pltpu.roll(b, FRAME, 1))
        second = jnp.where(low, pltpu.roll(a, FRAME, 1), b)
        out[:, near] = jnp.where(frame == 0, first, second).astype(BF16)


def split_kernel(
    offsets_in, noise_in, latents_in, keep, send, offsets, noise, latents, sems
):
    copies = [
        pltpu.make_async_copy(src, dst, sems.at[k])
        for k, (src, dst) in enumerate(
            ((offsets_in, offsets), (noise_in, noise), (latents_in, latents))
        )
    ]
    for c in copies:
        c.start()
    val = lax.axis_index("val")
    copies[0].wait()
    copies[1].wait()
    clips = noise.shape[0]
    warp_frame(offsets, noise, val, keep.at[:clips])
    warp_frame(offsets, noise, 1 - val, send.at[:clips])
    copies[2].wait()
    take_frame(latents, val, keep.at[clips:])
    take_frame(latents, 1 - val, send.at[clips:])


def in_hbm(x):
    return pltpu.with_memory_space_constraint(x, pltpu.HBM)


def split_frames(noise, latents, offsets):
    clips, values = noise.shape
    inputs = [flat_offsets(offsets), noise, latents]
    half = jax.ShapeDtypeStruct((2 * clips, values // 2), BF16)
    return pl.pallas_call(
        split_kernel,
        out_shape=[half] * 2,
        in_specs=[HBM] * 3,
        out_specs=[VMEM] * 2,
        scratch_shapes=[pltpu.VMEM(x.shape, x.dtype) for x in inputs]
        + [pltpu.SemaphoreType.DMA((3,))],
        compiler_params=params(),
        name="split",
    )(*map(in_hbm, inputs))


def stage_kernel(times, embed, table, column, sem):
    load = pltpu.make_async_copy(embed, table, sem)
    load.start()
    clips, lanes = column.shape
    row = lax.broadcasted_iota(jnp.int32, (clips, lanes), 0)
    t = jnp.zeros((clips, lanes), F32)
    for i in range(clips):
        t = jnp.where(row == i, times[i], t)
    column[...] = t
    load.wait()


def stage(times, embed):
    return pl.pallas_call(
        stage_kernel,
        out_shape=[
            jax.ShapeDtypeStruct(embed.shape, BF16),
            jax.ShapeDtypeStruct((times.shape[0], 128), F32),
        ],
        in_specs=[SMEM, HBM],
        out_specs=[VMEM] * 2,
        scratch_shapes=[pltpu.SemaphoreType.DMA],
        compiler_params=params(),
        cost_estimate=cost(2),
        name="stage",
    )(times, in_hbm(embed))


def swap_groups(x, a, clips):
    lane = lax.broadcasted_iota(jnp.int32, x.shape, 1)
    for bit in (1, 2):
        w = bit * clips
        moved = jnp.where(lane & w == 0, pltpu.roll(x, x.shape[1] - w, 1), pltpu.roll(x, w, 1))
        x = jnp.where(a & bit == 0, x, moved)
    return x


def gram_kernel(clips, lat, lat_far, lat_core, *refs):
    place = lax.axis_index("clip")
    a, x, c = place // 4, (place // 2) % 2, place % 2
    rows = 4 * clips
    out = refs[-1]
    noi = jnp.concatenate([r[...] for r in refs[:-1]], axis=0)
    cols = noi.shape[0]
    left = jnp.concatenate([lat[...], lat_far[...], lat_core[...], noi], axis=0)
    prod = lax.dot_general(left, noi, NT, preferred_element_type=F32)
    square = (cols, cols)
    eye = lax.broadcasted_iota(jnp.int32, square, 0) == lax.broadcasted_iota(jnp.int32, square, 1)
    norm = jnp.sum(jnp.where(eye, prod[rows:], 0.0), axis=0, keepdims=True)
    part = norm - 2.0 * prod[:rows]
    blocks = [part[k * clips : (k + 1) * clips] for k in range(4)]
    near0 = jnp.where(c == 0, blocks[0], blocks[2])
    near1 = jnp.where(c == 0, blocks[2], blocks[0])
    far0 = jnp.where(c == 0, blocks[1], blocks[3])
    far1 = jnp.where(c == 0, blocks[3], blocks[1])
    near = jnp.concatenate([near0, near1], axis=0)
    far = jnp.concatenate([far0, far1], axis=0)
    packed = jnp.concatenate([jnp.where(x == 0, near, far), jnp.where(x == 0, far, near)], axis=1)
    out[...] = swap_groups(packed, a, clips)


def gram_block(clips, *args):
    return pl.pallas_call(
        functools.partial(gram_kernel, clips),
        out_shape=jax.ShapeDtypeStruct((2 * clips, 128), F32),
        in_specs=[VMEM] * len(args),
        out_specs=VMEM,
        compiler_params=params(),
        cost_estimate=cost(5),
        name="gram",
    )(*args)


def sinkhorn(kernel, own):
    col = jnp.zeros((1, kernel.shape[1]), F32)
    for _ in range(ITERS):
        u = kernel + col
        top = jnp.max(u, axis=1, keepdims=True)
        row = -(top + jnp.log(jnp.sum(jnp.exp(u - top), axis=1, keepdims=True)))
        u = kernel + row
        top = jnp.max(u, axis=0, keepdims=True)
        col = -(top + jnp.log(jnp.sum(jnp.exp(u - top), axis=0, keepdims=True)))
    u = own + col
    top = jnp.max(u, axis=1, keepdims=True)
    e = jnp.exp(u - top)
    return e / jnp.sum(e, axis=1, keepdims=True)


def plan_kernel(clips, mine, other, out, full):
    place = lax.axis_index("clip")
    a, b = place // 4, place % 4
    half = 2 * clips
    low = lax.broadcasted_iota(jnp.int32, (half, 128), 1) < 64
    for s in range(mine.shape[0] // (2 * half)):
        for x in range(2):
            r = s * 2 * half
            g = mine[r + x * half : r + (x + 1) * half, :] * (-SCALE)
            h = other[r + x * half : r + (x + 1) * half, :] * (-SCALE)
            lanes = slice(x * 128, (x + 1) * 128)
            full[r : r + half, lanes] = jnp.where(low, g, pltpu.roll(h, 64, 1))
            full[r + half : r + 2 * half, lanes] = jnp.where(low, pltpu.roll(g, 64, 1), h)
    own = full[pl.ds(pl.multiple_of(b * clips, clips), clips), :]
    weights = sinkhorn(full[...], own)
    for x in range(2):
        lanes = slice(x * 128, (x + 1) * 128)
        out[:, lanes] = swap_groups(weights[:, lanes], a, clips).astype(BF16)


def plan(mine, other, clips):
    n = mine.shape[0]
    return pl.pallas_call(
        functools.partial(plan_kernel, clips),
        out_shape=jax.ShapeDtypeStruct((clips, n), BF16),
        in_specs=[VMEM] * 2,
        out_specs=VMEM,
        scratch_shapes=[pltpu.VMEM((n, n), F32)],
        compiler_params=params(),
        name="plan",
    )(mine, other)


def finish_kernel(clips, block, column, weights, lat, table, *refs):
    parts = refs[:-5]
    out, cube, lhs, result, sems = refs[-5:]
    val = lax.axis_index("val")
    t = column[:, :1]
    w = weights[...]
    values = lat.shape[1]
    step = 256
    for at in range(0, values, step):
        panel = jnp.concatenate([p[:, at : at + step] for p in parts], axis=0)
        coupled = jnp.dot(w, panel, preferred_element_type=F32)
        mixed = (1.0 - t) * lat[:, at : at + step].astype(F32) + t * coupled
        for q in range(step // S):
            cube[:, at // S + q, :] = mixed[:, q * S : (q + 1) * S]
    tiles = values // S
    half = tiles // 2
    low = lax.broadcasted_iota(jnp.int32, (tiles, S), 1) < FRAME
    for i in range(0, clips, 2):
        x, y = cube[i], cube[i + 1]
        near = jnp.where(low, x, pltpu.roll(y, FRAME, 1))
        far = jnp.where(low, pltpu.roll(x, FRAME, 1), y)
        mine = jnp.concatenate([near[:half], far[:half]], axis=0)
        other = jnp.concatenate([near[half:], far[half:]], axis=0)
        lanes = slice(i * FRAME, (i + 2) * FRAME)
        lhs[:tiles, lanes] = jnp.where(val == 0, mine, other).astype(BF16)
        lhs[tiles:, lanes] = jnp.where(val == 0, other, mine).astype(BF16)
    tokens = lhs.shape[1]
    steps = tokens // block

    def store(k):
        at = pl.multiple_of(k * block, block)
        return pltpu.make_async_copy(result.at[k], out.at[pl.ds(at, block)], sems.at[k])

    for k in range(steps):
        result[k] = lax.dot_general(
            lhs[:, k * block : (k + 1) * block], table[...], TN, preferred_element_type=F32
        ).astype(BF16)
        store(k).start()
    for k in range(steps):
        store(k).wait()


def finish(column, weights, lat, table, parts, block=128):
    clips, values = lat.shape
    tokens, width = clips * FRAME, table.shape[1]
    return pl.pallas_call(
        functools.partial(finish_kernel, clips, block),
        out_shape=jax.ShapeDtypeStruct((tokens, width), BF16),
        in_specs=[VMEM] * (4 + len(parts)),
        out_specs=HBM,
        scratch_shapes=[
            pltpu.VMEM((clips, values // S, S), F32),
            pltpu.VMEM((P_SIZE, tokens), BF16),
            pltpu.VMEM((tokens // block, block, width), BF16),
            pltpu.SemaphoreType.DMA((tokens // block,)),
        ],
        compiler_params=params(),
        name="finish",
    )(column, weights, lat, table, *parts)


def flip(n, bit):
    return [(i, i ^ bit) for i in range(n)]


def on_device(n, latents, noise, offsets, times, embed):
    clips = latents.shape[0]

    def core(x):
        return lax.ppermute(x, "clip", flip(n, 1))

    def across(x):
        return lax.ppermute(x, "clip", flip(n, 2))

    def along(x, k):
        return lax.ppermute(x, "clip", flip(n, 4 * k))

    def other_val(x):
        return lax.ppermute(x, "val", [(0, 1), (1, 0)])

    def other_both(x):
        pairs = [(2 * i + v, 2 * (i ^ 2) + 1 - v) for i in range(n) for v in range(2)]
        return lax.ppermute(x, ("clip", "val"), pairs)

    def beside(*x):
        return jnp.concatenate(x, axis=1)

    def below(*x):
        return jnp.concatenate(x, axis=0)

    keep, send = split_frames(noise, latents, offsets)
    got, keep_far = lax.optimization_barrier((other_val(send), across(keep)))
    own, far_own = beside(keep, got), beside(keep_far, across(got))
    lat, lat_far = own[clips:], far_own[clips:]
    noi = [own[:clips]]
    noi.append(along(noi[0], 1))
    noi.append(along(noi[0], 2))
    noi.append(along(noi[2], 1))
    lat_core = core(below(lat, lat_far))
    times, embed, _ = lax.optimization_barrier((times, embed, keep))
    table, column = stage(times, embed)
    lat_core, table, column = lax.optimization_barrier((lat_core, table, column))
    part = gram_block(clips, lat, lat_far, lat_core, *noi)
    got_x, got_v, got_b = across(part), other_val(part), other_both(part)
    far_mid, got_x = lax.optimization_barrier((across(below(noi[1], noi[2])), got_x))
    last, got_x = lax.optimization_barrier((noi[3], got_x))
    pair = below(part + got_v, got_x + got_b)
    far_last, *rows = lax.optimization_barrier([across(last)] + [along(pair, k) for k in (1, 2, 3)])
    mine = below(pair, *rows)
    weights = plan(mine, core(mine), clips)
    far = [far_own[:clips], far_mid]
    parts = [*noi, core(below(*noi)), *far, far_last, core(below(*far)), core(far_last)]
    out = finish(column, weights, lat, table, parts)
    return out.reshape(clips, FRAME, out.shape[1])


def warp_and_gather(latents, noise, offsets, times, embed):
    clips = latents.shape[0]
    warped = warp_noise(noise, offsets)
    panel = lax.all_gather(warped, "clip", axis=0, tiled=True)
    gram = lax.dot_general(latents, panel, NT, preferred_element_type=F32)
    square = jnp.sum(jnp.square(panel.astype(F32)), axis=1)
    part = lax.psum(square[None, :] - 2.0 * gram, "val")
    full = lax.all_gather(part, "clip", axis=0, tiled=True) * (-SCALE)
    weights = sinkhorn(full, part * (-SCALE)).astype(BF16)
    coupled = jnp.dot(weights, panel, preferred_element_type=F32)
    t = times[:, None]
    mixed = ((1.0 - t) * latents.astype(F32) + t * coupled).astype(BF16)
    cube = mixed.reshape(clips, latents.shape[1] // S, S)
    cube = lax.all_to_all(cube, "val", split_axis=2, concat_axis=1, tiled=True)
    return jnp.einsum("cps,pd->csd", cube, embed, preferred_element_type=F32).astype(BF16)


def solution(mesh):
    n, v = mesh.shape["clip"], mesh.shape["val"]
    body = functools.partial(on_device, n) if (n, v) == (16, 2) else warp_and_gather
    placed = (P("clip", "val"), P("clip", "val"), P("clip", None, None), P("clip"), P())
    return jax.shard_map(
        body, mesh=mesh, in_specs=placed, out_specs=P("clip", "val", None), check_vma=False
    )
```

time: 58.2 us -> 48 us (0.82)
  starting transfers between devices: 26 us -> 21.7 us
  local copies, waits for them, and re-layouts: 4.3 us -> 0.75 us
  waiting for transfers between devices: 17 us -> 14.7 us
    ppermute x9 -> x6, starting transfers between devices: 16.1 us -> 9.2 us  [along(): return lax.ppermute(x, 'clip', flip(n, 4 * k))]
    ppermute x4 -> x5, waiting for transfers between devices: 0.47 us -> 4.43 us  [across(): return lax.ppermute(x, 'clip', flip(n, 2))]
    unnamed x20 -> x6, local copies, waits for them, and re-layouts: 4.27 us -> 0.68 us
    pallas_call x1, Pallas kernels: 8.18 us -> 5.14 us  [finish(): pl.pallas_call(functools.partial(finish_kernel, clips, block), out_shape=...]
    ppermute x4 -> x5, starting transfers between devices: 3.66 us -> 6.67 us  [across(): return lax.ppermute(x, 'clip', flip(n, 2))]
    pallas_call x1 -> x2, Pallas kernels: 0.37 us -> 3.16 us  [the longest x1 1.64 us: stage(): pl.pallas_call(stage_kernel, out_shape=[jax.ShapeDtypeStruct(embed.shape,...]
    ppermute x1, waiting for transfers between devices: 2.49 us -> 0.01 us  [other_both(): return lax.ppermute(x, ('clip', 'val'), pairs)]
    ppermute x3 -> x2, waiting for transfers between devices: 2.48 us -> 0.07 us  [other_val(): return lax.ppermute(x, 'val', [(0, 1), (1, 0)])]
  transfers between devices with their start and end apart: 23 -> 19, of which waited for: 10 -> 8; matrix products, arithmetic and copies ran while one was open for 0% -> 0% of each run, Pallas kernels for 3% -> 8%
where the time goes in v3:
time: 48 us; the launch traced here: 47.8 us
  starting transfers between devices  21.7 us (45%)
  waiting for transfers between devices  14.7 us (31%)
  Pallas kernels  10.4 us (22%)
  local copies, waits for them, and re-layouts  0.75 us (2%)
    ppermute x6, waiting for transfers between devices, along(): return lax.ppermute(x, 'clip', flip(n, 4 * k))  9.32 us
    ppermute x6, starting transfers between devices, along(): return lax.ppermute(x, 'clip', flip(n, 4 * k))  9.2 us
    ppermute x5, starting transfers between devices, across(): return lax.ppermute(x, 'clip', flip(n, 2))  6.67 us
    pallas_call x1, Pallas kernels, finish(): pl.pallas_call(functools.partial(finish_kernel, clips, block), out_shape=...  5.14 us
    ppermute x5, waiting for transfers between devices, across(): return lax.ppermute(x, 'clip', flip(n, 2))  4.43 us
    ppermute x2, starting transfers between devices, other_val(): return lax.ppermute(x, 'val', [(0, 1), (1, 0)])  3.59 us
    pallas_call x1, Pallas kernels, stage(): pl.pallas_call(stage_kernel, out_shape=[jax.ShapeDtypeStruct(embed.shape,...  1.64 us
    pallas_call x1, Pallas kernels, split_frames(): pl.pallas_call(split_kernel, out_shape=[half] * 2, in_specs=[HBM] * 3, ou...  1.53 us
  transfers between devices with their start and end apart: 19, of which 8 were waited for; matrix products, arithmetic and copies ran while one was open for 0% of the time, Pallas kernels for 8%

profile of v3, /device:TPU:0, one launch (start us, length us, event | category | flops | bytes accessed | tf_op | source)
XLA Modules:
  0.0 47.8 jit_solution(1761647155544903630)
XLA Ops:
  0.0 1.5 %split.1 = (bf16[32,2048]{1,0:T(8,128)(2,1)S(1)}, bf16[32,2048]{1,0:T(8,128)(2,1)S(1)}) custom-call(s32[4,16]{1,0:T(4,128)} %bitcast.4, bf16[16,4096]{1,0:T(8,128)(2,1)} %noise_in.1, bf16[16,4096]{1,0:T(8,128)(2,1)} %latents_in.1), custom_call_target="tpu_custom_call" | custom-call | tf_op jit(solution)/shard_map/split/pallas_call | solution.py:134
  1.5 3.0 %collective-permute-start = (bf16[32,2048]{1,0:T(8,128)(2,1)S(1)}, bf16[32,2048]{1,0:T(8,128)(2,1)S(1)}, u32[]{:S(2)}, u32[]{:S(2)}) collective-permute-start(bf16[32,2048]{1,0:T(8,128)(2,1)S(1)} %get-tuple-element.25), channel_id=1, source_target_pairs={{0,1},{1,0},{2,3},{3,2},{4,5},{5,4},{6,7},{7,6},{8,9},{9,8},{10,11... | collective-permute-start | bytes 393224 | tf_op jit(solution)/shard_map/ppermute | solution.py:345
  4.6 1.5 %collective-permute-start.1 = (bf16[32,2048]{1,0:T(8,128)(2,1)S(1)}, bf16[32,2048]{1,0:T(8,128)(2,1)S(1)}, u32[]{:S(2)}, u32[]{:S(2)}) collective-permute-start(bf16[32,2048]{1,0:T(8,128)(2,1)S(1)} %get-tuple-element.24), channel_id=1, source_target_pairs={{0,4},{2,6},{4,0},{6,2},{8,12},{10,14},{12,8},{14,10},{16,20},{18,... | collective-permute-start | bytes 393224 | tf_op jit(solution)/shard_map/ppermute | solution.py:339
  6.1 0.7 %copy-done = f32[16]{0:T(128)S(1)} copy-done((f32[16]{0:T(128)S(1)}, f32[16]{0:T(128)}, u32[]{:S(2)}) %copy-start) | copy-done | bytes 88
  6.7 1.6 %stage.1 = (bf16[64,5120]{1,0:T(8,128)(2,1)S(1)}, f32[16,128]{1,0:T(8,128)S(1)}) custom-call(f32[16]{0:T(128)S(1)} %copy-done, bf16[64,5120]{1,0:T(8,128)(2,1)} %embed), custom_call_target="tpu_custom_call" | custom-call | bytes 7000000 | tf_op jit(solution)/shard_map/stage/pallas_call | solution.py:159
  8.4 1.1 %collective-permute-done.1 = bf16[32,2048]{1,0:T(8,128)(2,1)S(1)} collective-permute-done((bf16[32,2048]{1,0:T(8,128)(2,1)S(1)}, bf16[32,2048]{1,0:T(8,128)(2,1)S(1)}, u32[]{:S(2)}, u32[]{:S(2)}) %collective-permute-start.1) | collective-permute-done | bytes 131104 | tf_op jit(solution)/shard_map/ppermute | solution.py:339
  9.5 1.5 %collective-permute-start.2 = (bf16[32,2048]{1,0:T(8,128)(2,1)S(1)}, bf16[32,2048]{1,0:T(8,128)(2,1)S(1)}, u32[]{:S(2)}, u32[]{:S(2)}) collective-permute-start(bf16[32,2048]{1,0:T(8,128)(2,1)S(1)} %collective-permute-done), channel_id=1, source_target_pairs={{0,4},{2,6},{4,0},{6,2},{8,12},{10,14},{12,8},{14,10},{16,20},{18,... | collective-permute-start | bytes 393224 | tf_op jit(solution)/shard_map/ppermute | solution.py:339
  11.1 2.7 %collective-permute-start.5 = (bf16[16,4096]{1,0:T(8,128)(2,1)S(1)}, bf16[16,4096]{1,0:T(8,128)(2,1)S(1)}, u32[]{:S(2)}, u32[]{:S(2)}) collective-permute-start(bf16[16,4096]{1,0:T(8,128)(2,1)S(1)} %get-tuple-element.49.refs_0_), channel_id=1, source_target_pairs={{0,16},{2,18},{4,20},{6,22},{8,24},{10,26},{12,28},{14,30},{16,0},... | collective-permute-start | bytes 393224 | tf_op jit(solution)/shard_map/ppermute | solution.py:342
  13.7 1.6 %collective-permute-start.4 = (bf16[16,4096]{1,0:T(8,128)(2,1)S(1)}, bf16[16,4096]{1,0:T(8,128)(2,1)S(1)}, u32[]{:S(2)}, u32[]{:S(2)}) collective-permute-start(bf16[16,4096]{1,0:T(8,128)(2,1)S(1)} %get-tuple-element.49.refs_0_), channel_id=1, source_target_pairs={{0,8},{2,10},{4,12},{6,14},{8,0},{10,2},{12,4},{14,6},{16,24},{18,... | collective-permute-start | bytes 393224 | tf_op jit(solution)/shard_map/ppermute | solution.py:342
  15.5 3.3 %collective-permute-done.5.refs_2_ = bf16[16,4096]{1,0:T(8,128)(2,1)S(1)} collective-permute-done((bf16[16,4096]{1,0:T(8,128)(2,1)S(1)}, bf16[16,4096]{1,0:T(8,128)(2,1)S(1)}, u32[]{:S(2)}, u32[]{:S(2)}) %collective-permute-start.5) | collective-permute-done | bytes 131104 | tf_op jit(solution)/shard_map/ppermute | solution.py:342
  19.4 0.6 %collective-permute-start.8 = (bf16[32,4096]{1,0:T(8,128)(2,1)S(1)}, bf16[32,4096]{1,0:T(8,128)(2,1)S(1)}, u32[]{:S(2)}, u32[]{:S(2)}) collective-permute-start(bf16[32,4096]{1,0:T(8,128)(2,1)S(1)} %pad_maximum_fusion.3), channel_id=1, source_target_pairs={{0,4},{2,6},{4,0},{6,2},{8,12},{10,14},{12,8},{14,10},{16,20},{18,... | collective-permute-start | bytes 786440 | tf_op jit(solution)/shard_map/ppermute | solution.py:339
  20.0 3.8 %collective-permute-done.6.refs_3_ = bf16[16,4096]{1,0:T(8,128)(2,1)S(1)} collective-permute-done((bf16[16,4096]{1,0:T(8,128)(2,1)S(1)}, bf16[16,4096]{1,0:T(8,128)(2,1)S(1)}, u32[]{:S(2)}, u32[]{:S(2)}) %collective-permute-start.6) | collective-permute-done | bytes 131104 | tf_op jit(solution)/shard_map/ppermute | solution.py:342
  23.8 0.6 %gram.1 = f32[32,128]{1,0:T(8,128)S(1)} custom-call(bf16[16,4096]{1,0:T(8,128)(2,1)S(1)} %get-tuple-element.50.lat, bf16[16,4096]{1,0:T(8,128)(2,1)S(1)} %get-tuple-element.48.lat_far, bf16[32,4096]{1,0:T(8,128)(2,1)S(1)} %collective-permute-done.3.lat_core, bf16[16,4096]{1,0:T(8,128)(2,1)S(1)} %get-tuple-element.49.refs_0_, ...), custom_call_target="tpu_custom_call" | custom-call | bytes 17500000 | tf_op jit(solution)/shard_map/gram/pallas_call | solution.py:208
  25.1 1.5 %collective-permute-start.10 = (f32[32,128]{1,0:T(8,128)S(1)}, f32[32,128]{1,0:T(8,128)S(1)}, u32[]{:S(2)}, u32[]{:S(2)}) collective-permute-start(f32[32,128]{1,0:T(8,128)S(1)} %gram.1), channel_id=1, source_target_pairs={{0,5},{1,4},{2,7},{3,6},{4,1},{5,0},{6,3},{7,2},{8,13},{9,12},{10,... | collective-permute-start | bytes 49160 | tf_op jit(solution)/shard_map/ppermute | solution.py:349
  26.6 1.5 %collective-permute-start.9 = (f32[32,128]{1,0:T(8,128)S(1)}, f32[32,128]{1,0:T(8,128)S(1)}, u32[]{:S(2)}, u32[]{:S(2)}) collective-permute-start(f32[32,128]{1,0:T(8,128)S(1)} %gram.1), channel_id=1, source_target_pairs={{0,4},{2,6},{4,0},{6,2},{8,12},{10,14},{12,8},{14,10},{16,20},{18,... | collective-permute-start | bytes 49160 | tf_op jit(solution)/shard_map/ppermute | solution.py:339
  28.2 2.1 %collective-permute-done.9 = f32[32,128]{1,0:T(8,128)S(1)} collective-permute-done((f32[32,128]{1,0:T(8,128)S(1)}, f32[32,128]{1,0:T(8,128)S(1)}, u32[]{:S(2)}, u32[]{:S(2)}) %collective-permute-start.9) | collective-permute-done | bytes 16416 | tf_op jit(solution)/shard_map/ppermute | solution.py:339
  30.3 3.4 %collective-permute-start.14 = (f32[64,128]{1,0:T(8,128)S(1)}, f32[64,128]{1,0:T(8,128)S(1)}, u32[]{:S(2)}, u32[]{:S(2)}) collective-permute-start(f32[64,128]{1,0:T(8,128)S(1)} %pad_maximum_fusion.4), channel_id=1, source_target_pairs={{0,24},{2,26},{4,28},{6,30},{8,16},{10,18},{12,20},{14,22},{16,8},... | collective-permute-start | bytes 98312 | tf_op jit(solution)/shard_map/ppermute | solution.py:342
  33.8 1.0 %collective-permute-start.12 = (f32[64,128]{1,0:T(8,128)S(1)}, f32[64,128]{1,0:T(8,128)S(1)}, u32[]{:S(2)}, u32[]{:S(2)}) collective-permute-start(f32[64,128]{1,0:T(8,128)S(1)} %pad_maximum_fusion.4), channel_id=1, source_target_pairs={{0,8},{2,10},{4,12},{6,14},{8,0},{10,2},{12,4},{14,6},{16,24},{18,... | collective-permute-start | bytes 98312 | tf_op jit(solution)/shard_map/ppermute | solution.py:342
  34.8 1.5 %collective-permute-start.11 = (bf16[16,4096]{1,0:T(8,128)(2,1)S(1)}, bf16[16,4096]{1,0:T(8,128)(2,1)S(1)}, u32[]{:S(2)}, u32[]{:S(2)}) collective-permute-start(bf16[16,4096]{1,0:T(8,128)(2,1)S(1)} %collective-permute-done.6.refs_3_), channel_id=1, source_target_pairs={{0,4},{2,6},{4,0},{6,2},{8,12},{10,14},{12,8},{14,10},{16,20},{18,... | collective-permute-start | bytes 393224 | tf_op jit(solution)/shard_map/ppermute | solution.py:339
  36.4 2.1 %collective-permute-done.13 = f32[64,128]{1,0:T(8,128)S(1)} collective-permute-done((f32[64,128]{1,0:T(8,128)S(1)}, f32[64,128]{1,0:T(8,128)S(1)}, u32[]{:S(2)}, u32[]{:S(2)}) %collective-permute-start.13) | collective-permute-done | bytes 32800 | tf_op jit(solution)/shard_map/ppermute | solution.py:342
  38.6 1.2 %collective-permute-done.11.refs_7_ = bf16[16,4096]{1,0:T(8,128)(2,1)S(1)} collective-permute-done((bf16[16,4096]{1,0:T(8,128)(2,1)S(1)}, bf16[16,4096]{1,0:T(8,128)(2,1)S(1)}, u32[]{:S(2)}, u32[]{:S(2)}) %collective-permute-start.11) | collective-permute-done | bytes 131104 | tf_op jit(solution)/shard_map/ppermute | solution.py:339
  40.4 0.8 %collective-permute-done.15.other = f32[256,128]{1,0:T(8,128)S(1)} collective-permute-done((f32[256,128]{1,0:T(8,128)S(1)}, f32[256,128]{1,0:T(8,128)S(1)}, u32[]{:S(2)}, u32[]{:S(2)}) %collective-permute-start.15) | collective-permute-done | bytes 131104 | tf_op jit(solution)/shard_map/ppermute | solution.py:336
  41.2 1.5 %plan.1.weights = bf16[16,256]{1,0:T(8,128)(2,1)S(1)} custom-call(f32[256,128]{1,0:T(8,128)S(1)} %constant_dynamic-update-slice_fusion.4.mine, f32[256,128]{1,0:T(8,128)S(1)} %collective-permute-done.15.other), custom_call_target="tpu_custom_call" | custom-call | tf_op jit(solution)/shard_map/plan/pallas_call | solution.py:256
  42.7 5.1 %finish.1 = bf16[1024,5120]{1,0:T(8,128)(2,1)} custom-call(f32[16,128]{1,0:T(8,128)S(1)} %get-tuple-element.32.column, bf16[16,256]{1,0:T(8,128)(2,1)S(1)} %plan.1.weights, bf16[16,4096]{1,0:T(8,128)(2,1)S(1)} %get-tuple-element.50.lat, bf16[64,5120]{1,0:T(8,128)(2,1)S(1)} %get-tuple-element.40.table, bf16[16,4096]{1,0:T(8,128)(2,1)S(1)} %get-tuple-element.49.refs_0_, ...), custom_call_target="tpu_custom_call" | custom-call | tf_op jit(solution)/shard_map/finish/pallas_call | solution.py:312
  (37 shorter events, 2.2 us)
Async XLA Ops:
  1.5 6.8 %collective-permute-start = (bf16[32,2048]{1,0:T(8,128)(2,1)S(1)}, bf16[32,2048]{1,0:T(8,128)(2,1)S(1)}, u32[]{:S(2)}, u32[]{:S(2)}) collective-permute-start(bf16[32,2048]{1,0:T(8,128)(2,1)S(1)} %get-tuple-element.25), channel_id=1, source_target_pairs={{0,1},{1,0},{2,3},{3,2},{4,5},{5,4},{6,7},{7,6},{8,9},{9,8},{10,11... | collective-permute-start | bytes 393224 | tf_op jit(solution)/shard_map/ppermute | solution.py:345
  4.6 5.0 %collective-permute-start.1 = (bf16[32,2048]{1,0:T(8,128)(2,1)S(1)}, bf16[32,2048]{1,0:T(8,128)(2,1)S(1)}, u32[]{:S(2)}, u32[]{:S(2)}) collective-permute-start(bf16[32,2048]{1,0:T(8,128)(2,1)S(1)} %get-tuple-element.24), channel_id=1, source_target_pairs={{0,4},{2,6},{4,0},{6,2},{8,12},{10,14},{12,8},{14,10},{16,20},{18,... | collective-permute-start | bytes 393224 | tf_op jit(solution)/shard_map/ppermute | solution.py:339
  6.1 0.7 %copy-start = (f32[16]{0:T(128)S(1)}, f32[16]{0:T(128)}, u32[]{:S(2)}) copy-start(f32[16]{0:T(128)} %times) | copy-start | bytes 196
  9.5 5.8 %collective-permute-start.2 = (bf16[32,2048]{1,0:T(8,128)(2,1)S(1)}, bf16[32,2048]{1,0:T(8,128)(2,1)S(1)}, u32[]{:S(2)}, u32[]{:S(2)}) collective-permute-start(bf16[32,2048]{1,0:T(8,128)(2,1)S(1)} %collective-permute-done), channel_id=1, source_target_pairs={{0,4},{2,6},{4,0},{6,2},{8,12},{10,14},{12,8},{14,10},{16,20},{18,... | collective-permute-start | bytes 393224 | tf_op jit(solution)/shard_map/ppermute | solution.py:339
  11.1 7.7 %collective-permute-start.5 = (bf16[16,4096]{1,0:T(8,128)(2,1)S(1)}, bf16[16,4096]{1,0:T(8,128)(2,1)S(1)}, u32[]{:S(2)}, u32[]{:S(2)}) collective-permute-start(bf16[16,4096]{1,0:T(8,128)(2,1)S(1)} %get-tuple-element.49.refs_0_), channel_id=1, source_target_pairs={{0,16},{2,18},{4,20},{6,22},{8,24},{10,26},{12,28},{14,30},{16,0},... | collective-permute-start | bytes 393224 | tf_op jit(solution)/shard_map/ppermute | solution.py:342
  13.7 5.6 %collective-permute-start.4 = (bf16[16,4096]{1,0:T(8,128)(2,1)S(1)}, bf16[16,4096]{1,0:T(8,128)(2,1)S(1)}, u32[]{:S(2)}, u32[]{:S(2)}) collective-permute-start(bf16[16,4096]{1,0:T(8,128)(2,1)S(1)} %get-tuple-element.49.refs_0_), channel_id=1, source_target_pairs={{0,8},{2,10},{4,12},{6,14},{8,0},{10,2},{12,4},{14,6},{16,24},{18,... | collective-permute-start | bytes 393224 | tf_op jit(solution)/shard_map/ppermute | solution.py:342
  15.4 4.6 %collective-permute-start.3 = (bf16[32,4096]{1,0:T(8,128)(2,1)S(1)}, bf16[32,4096]{1,0:T(8,128)(2,1)S(1)}, u32[]{:S(2)}, u32[]{:S(2)}) collective-permute-start(bf16[32,4096]{1,0:T(8,128)(2,1)S(1)} %pad_maximum_fusion.2), channel_id=1, source_target_pairs={{0,2},{2,0},{4,6},{6,4},{8,10},{10,8},{12,14},{14,12},{16,18},{18,... | collective-permute-start | bytes 786440 | tf_op jit(solution)/shard_map/ppermute | solution.py:336
  18.8 5.0 %collective-permute-start.6 = (bf16[16,4096]{1,0:T(8,128)(2,1)S(1)}, bf16[16,4096]{1,0:T(8,128)(2,1)S(1)}, u32[]{:S(2)}, u32[]{:S(2)}) collective-permute-start(bf16[16,4096]{1,0:T(8,128)(2,1)S(1)} %collective-permute-done.5.refs_2_), channel_id=1, source_target_pairs={{0,8},{2,10},{4,12},{6,14},{8,0},{10,2},{12,4},{14,6},{16,24},{18,... | collective-permute-start | bytes 393224 | tf_op jit(solution)/shard_map/ppermute | solution.py:342
  19.4 8.8 %collective-permute-start.8 = (bf16[32,4096]{1,0:T(8,128)(2,1)S(1)}, bf16[32,4096]{1,0:T(8,128)(2,1)S(1)}, u32[]{:S(2)}, u32[]{:S(2)}) collective-permute-start(bf16[32,4096]{1,0:T(8,128)(2,1)S(1)} %pad_maximum_fusion.3), channel_id=1, source_target_pairs={{0,4},{2,6},{4,0},{6,2},{8,12},{10,14},{12,8},{14,10},{16,20},{18,... | collective-permute-start | bytes 786440 | tf_op jit(solution)/shard_map/ppermute | solution.py:339
  24.4 3.8 %collective-permute-start.7 = (f32[32,128]{1,0:T(8,128)S(1)}, f32[32,128]{1,0:T(8,128)S(1)}, u32[]{:S(2)}, u32[]{:S(2)}) collective-permute-start(f32[32,128]{1,0:T(8,128)S(1)} %gram.1), channel_id=1, source_target_pairs={{0,1},{1,0},{2,3},{3,2},{4,5},{5,4},{6,7},{7,6},{8,9},{9,8},{10,11... | collective-permute-start | bytes 49160 | tf_op jit(solution)/shard_map/ppermute | solution.py:345
  25.0 17.7 %collective-permute-start.16 = (bf16[64,4096]{1,0:T(8,128)(2,1)S(1)}, bf16[64,4096]{1,0:T(8,128)(2,1)S(1)}, u32[]{:S(2)}, u32[]{:S(2)}) collective-permute-start(bf16[64,4096]{1,0:T(8,128)(2,1)S(1)} %pad_maximum_fusion), channel_id=1, source_target_pairs={{0,2},{2,0},{4,6},{6,4},{8,10},{10,8},{12,14},{14,12},{16,18},{18,... | collective-permute-start | bytes 1572872 | tf_op jit(solution)/shard_map/ppermute | solution.py:336
  25.1 5.2 %collective-permute-start.10 = (f32[32,128]{1,0:T(8,128)S(1)}, f32[32,128]{1,0:T(8,128)S(1)}, u32[]{:S(2)}, u32[]{:S(2)}) collective-permute-start(f32[32,128]{1,0:T(8,128)S(1)} %gram.1), channel_id=1, source_target_pairs={{0,5},{1,4},{2,7},{3,6},{4,1},{5,0},{6,3},{7,2},{8,13},{9,12},{10,... | collective-permute-start | bytes 49160 | tf_op jit(solution)/shard_map/ppermute | solution.py:349
  26.6 3.7 %collective-permute-start.9 = (f32[32,128]{1,0:T(8,128)S(1)}, f32[32,128]{1,0:T(8,128)S(1)}, u32[]{:S(2)}, u32[]{:S(2)}) collective-permute-start(f32[32,128]{1,0:T(8,128)S(1)} %gram.1), channel_id=1, source_target_pairs={{0,4},{2,6},{4,0},{6,2},{8,12},{10,14},{12,8},{14,10},{16,20},{18,... | collective-permute-start | bytes 49160 | tf_op jit(solution)/shard_map/ppermute | solution.py:339
  30.3 6.0 %collective-permute-start.14 = (f32[64,128]{1,0:T(8,128)S(1)}, f32[64,128]{1,0:T(8,128)S(1)}, u32[]{:S(2)}, u32[]{:S(2)}) collective-permute-start(f32[64,128]{1,0:T(8,128)S(1)} %pad_maximum_fusion.4), channel_id=1, source_target_pairs={{0,24},{2,26},{4,28},{6,30},{8,16},{10,18},{12,20},{14,22},{16,8},... | collective-permute-start | bytes 98312 | tf_op jit(solution)/shard_map/ppermute | solution.py:342
  33.8 4.8 %collective-permute-start.13 = (f32[64,128]{1,0:T(8,128)S(1)}, f32[64,128]{1,0:T(8,128)S(1)}, u32[]{:S(2)}, u32[]{:S(2)}) collective-permute-start(f32[64,128]{1,0:T(8,128)S(1)} %pad_maximum_fusion.4), channel_id=1, source_target_pairs={{0,16},{2,18},{4,20},{6,22},{8,24},{10,26},{12,28},{14,30},{16,0},... | collective-permute-start | bytes 98312 | tf_op jit(solution)/shard_map/ppermute | solution.py:342
  33.8 4.8 %collective-permute-start.12 = (f32[64,128]{1,0:T(8,128)S(1)}, f32[64,128]{1,0:T(8,128)S(1)}, u32[]{:S(2)}, u32[]{:S(2)}) collective-permute-start(f32[64,128]{1,0:T(8,128)S(1)} %pad_maximum_fusion.4), channel_id=1, source_target_pairs={{0,8},{2,10},{4,12},{6,14},{8,0},{10,2},{12,4},{14,6},{16,24},{18,... | collective-permute-start | bytes 98312 | tf_op jit(solution)/shard_map/ppermute | solution.py:342
  34.8 5.0 %collective-permute-start.11 = (bf16[16,4096]{1,0:T(8,128)(2,1)S(1)}, bf16[16,4096]{1,0:T(8,128)(2,1)S(1)}, u32[]{:S(2)}, u32[]{:S(2)}) collective-permute-start(bf16[16,4096]{1,0:T(8,128)(2,1)S(1)} %collective-permute-done.6.refs_3_), channel_id=1, source_target_pairs={{0,4},{2,6},{4,0},{6,2},{8,12},{10,14},{12,8},{14,10},{16,20},{18,... | collective-permute-start | bytes 393224 | tf_op jit(solution)/shard_map/ppermute | solution.py:339
  36.4 6.3 %collective-permute-start.17 = (bf16[48,4096]{1,0:T(8,128)(2,1)S(1)}, bf16[48,4096]{1,0:T(8,128)(2,1)S(1)}, u32[]{:S(2)}, u32[]{:S(2)}) collective-permute-start(bf16[48,4096]{1,0:T(8,128)(2,1)S(1)} %pad_maximum_fusion.1), channel_id=1, source_target_pairs={{0,2},{2,0},{4,6},{6,4},{8,10},{10,8},{12,14},{14,12},{16,18},{18,... | collective-permute-start | bytes 1179656 | tf_op jit(solution)/shard_map/ppermute | solution.py:336
  39.8 1.4 %collective-permute-start.15 = (f32[256,128]{1,0:T(8,128)S(1)}, f32[256,128]{1,0:T(8,128)S(1)}, u32[]{:S(2)}, u32[]{:S(2)}) collective-permute-start(f32[256,128]{1,0:T(8,128)S(1)} %constant_dynamic-update-slice_fusion.4.mine), channel_id=1, source_target_pairs={{0,2},{2,0},{4,6},{6,4},{8,10},{10,8},{12,14},{14,12},{16,18},{18,... | collective-permute-start | bytes 393224 | tf_op jit(solution)/shard_map/ppermute | solution.py:336
  39.9 2.8 %collective-permute-start.18 = (bf16[16,4096]{1,0:T(8,128)(2,1)S(1)}, bf16[16,4096]{1,0:T(8,128)(2,1)S(1)}, u32[]{:S(2)}, u32[]{:S(2)}) collective-permute-start(bf16[16,4096]{1,0:T(8,128)(2,1)S(1)} %collective-permute-done.11.refs_7_), channel_id=1, source_target_pairs={{0,2},{2,0},{4,6},{6,4},{8,10},{10,8},{12,14},{14,12},{16,18},{18,... | collective-permute-start | bytes 393224 | tf_op jit(solution)/shard_map/ppermute | solution.py:336

commit v4 on v3

--- a/solution.py
+++ b/solution.py
@@ -102,7 +102,7 @@
 
 
 def split_kernel(
-    offsets_in, noise_in, latents_in, keep, send, offsets, noise, latents, sems
+    offsets_in, noise_in, latents_in, noise_out, lat_out, offsets, noise, latents, sems
 ):
     copies = [
         pltpu.make_async_copy(src, dst, sems.at[k])
@@ -115,12 +115,12 @@
     val = lax.axis_index("val")
     copies[0].wait()
     copies[1].wait()
-    clips = noise.shape[0]
-    warp_frame(offsets, noise, val, keep.at[:clips])
-    warp_frame(offsets, noise, 1 - val, send.at[:clips])
+    cut = noise.shape[1] // 2
+    warp_frame(offsets, noise, val, noise_out.at[:, :cut])
+    warp_frame(offsets, noise, 1 - val, noise_out.at[:, cut:])
     copies[2].wait()
-    take_frame(latents, val, keep.at[clips:])
-    take_frame(latents, 1 - val, send.at[clips:])
+    take_frame(latents, val, lat_out.at[:, :cut])
+    take_frame(latents, 1 - val, lat_out.at[:, cut:])
 
 
 def in_hbm(x):
@@ -128,12 +128,10 @@
 
 
 def split_frames(noise, latents, offsets):
-    clips, values = noise.shape
     inputs = [flat_offsets(offsets), noise, latents]
-    half = jax.ShapeDtypeStruct((2 * clips, values // 2), BF16)
     return pl.pallas_call(
         split_kernel,
-        out_shape=[half] * 2,
+        out_shape=[jax.ShapeDtypeStruct(noise.shape, BF16)] * 2,
         in_specs=[HBM] * 3,
         out_specs=[VMEM] * 2,
         scratch_shapes=[pltpu.VMEM(x.shape, x.dtype) for x in inputs]
@@ -143,12 +141,15 @@
     )(*map(in_hbm, inputs))
 
 
-def stage_kernel(times, embed, table, column, sem):
-    load = pltpu.make_async_copy(embed, table, sem)
+def stage_kernel(times_in, embed, table, column, times, sems):
+    load = pltpu.make_async_copy(embed, table, sems.at[0])
     load.start()
+    small = pltpu.make_async_copy(times_in, times, sems.at[1])
+    small.start()
     clips, lanes = column.shape
     row = lax.broadcasted_iota(jnp.int32, (clips, lanes), 0)
     t = jnp.zeros((clips, lanes), F32)
+    small.wait()
     for i in range(clips):
         t = jnp.where(row == i, times[i], t)
     column[...] = t
@@ -162,13 +163,13 @@
             jax.ShapeDtypeStruct(embed.shape, BF16),
             jax.ShapeDtypeStruct((times.shape[0], 128), F32),
         ],
-        in_specs=[SMEM, HBM],
+        in_specs=[HBM] * 2,
         out_specs=[VMEM] * 2,
-        scratch_shapes=[pltpu.SemaphoreType.DMA],
+        scratch_shapes=[pltpu.SMEM(times.shape, F32), pltpu.SemaphoreType.DMA((2,))],
         compiler_params=params(),
         cost_estimate=cost(2),
         name="stage",
-    )(times, in_hbm(embed))
+    )(in_hbm(times), in_hbm(embed))
 
 
 def swap_groups(x, a, clips):
@@ -264,20 +265,23 @@
     )(mine, other)
 
 
-def finish_kernel(clips, block, column, weights, lat, table, *refs):
+def finish_kernel(clips, block, layout, column, weights, lat_keep, lat_got, table, *refs):
     parts = refs[:-5]
     out, cube, lhs, result, sems = refs[-5:]
     val = lax.axis_index("val")
     t = column[:, :1]
     w = weights[...]
-    values = lat.shape[1]
+    cut = lat_got.shape[1]
     step = 256
-    for at in range(0, values, step):
-        panel = jnp.concatenate([p[:, at : at + step] for p in parts], axis=0)
-        coupled = jnp.dot(w, panel, preferred_element_type=F32)
-        mixed = (1.0 - t) * lat[:, at : at + step].astype(F32) + t * coupled
-        for q in range(step // S):
-            cube[:, at // S + q, :] = mixed[:, q * S : (q + 1) * S]
+    for h, lat in enumerate((lat_keep, lat_got)):
+        for at in range(0, cut, step):
+            lanes = slice(at, at + step)
+            panel = jnp.concatenate([parts[k][r : r + clips, lanes] for k, r in layout[h]], axis=0)
+            coupled = jnp.dot(w, panel, preferred_element_type=F32)
+            mixed = (1.0 - t) * lat[:, lanes].astype(F32) + t * coupled
+            for q in range(step // S):
+                cube[:, (h * cut + at) // S + q, :] = mixed[:, q * S : (q + 1) * S]
+    values = 2 * cut
     tiles = values // S
     half = tiles // 2
     low = lax.broadcasted_iota(jnp.int32, (tiles, S), 1) < FRAME
@@ -306,13 +310,13 @@
         store(k).wait()
 
 
-def finish(column, weights, lat, table, parts, block=128):
-    clips, values = lat.shape
+def finish(column, weights, lat_keep, lat_got, table, parts, layout, block=128):
+    clips, values = lat_keep.shape
     tokens, width = clips * FRAME, table.shape[1]
     return pl.pallas_call(
-        functools.partial(finish_kernel, clips, block),
+        functools.partial(finish_kernel, clips, block, layout),
         out_shape=jax.ShapeDtypeStruct((tokens, width), BF16),
-        in_specs=[VMEM] * (4 + len(parts)),
+        in_specs=[VMEM] * (5 + len(parts)),
         out_specs=HBM,
         scratch_shapes=[
             pltpu.VMEM((clips, values // S, S), F32),
@@ -322,7 +326,31 @@
         ],
         compiler_params=params(),
         name="finish",
-    )(column, weights, lat, table, *parts)
+    )(column, weights, lat_keep, lat_got, table, *parts)
+
+
+def stack_kernel(*refs):
+    parts, (firsts, seconds) = refs[:-2], refs[-2:]
+    clips, values = parts[0].shape
+    cut = values // 2
+    for k, part in enumerate(parts):
+        firsts[k * clips : (k + 1) * clips, :] = part[:, :cut]
+        if k:
+            seconds[(k - 1) * clips : k * clips, :] = part[:, cut:]
+
+
+def stack(parts):
+    clips, values = parts[0].shape
+    shapes = [(k * clips, values // 2) for k in (len(parts), len(parts) - 1)]
+    return pl.pallas_call(
+        stack_kernel,
+        out_shape=[jax.ShapeDtypeStruct(x, BF16) for x in shapes],
+        in_specs=[VMEM] * len(parts),
+        out_specs=[VMEM] * 2,
+        compiler_params=params(),
+        cost_estimate=cost(3),
+        name="stack",
+    )(*parts)
 
 
 def flip(n, bit):
@@ -354,29 +382,47 @@
     def below(*x):
         return jnp.concatenate(x, axis=0)
 
-    keep, send = split_frames(noise, latents, offsets)
-    got, keep_far = lax.optimization_barrier((other_val(send), across(keep)))
-    own, far_own = beside(keep, got), beside(keep_far, across(got))
-    lat, lat_far = own[clips:], far_own[clips:]
-    noi = [own[:clips]]
-    noi.append(along(noi[0], 1))
-    noi.append(along(noi[0], 2))
+    own, lat = split_frames(noise, latents, offsets)
+    cut = own.shape[1] // 2
+    noi = [own]
+    noi.append(along(own, 1))
+    noi.append(along(own, 2))
     noi.append(along(noi[2], 1))
+    keep = [x[:, :cut] for x in noi]
+    send = [x[:, cut:] for x in noi]
+    times, embed, _ = lax.optimization_barrier((times, embed, own))
+    table, column = stage(times, embed)
+    lat_late, own_late, table, column = lax.optimization_barrier((lat, own, table, column))
+    got_own = other_val(below(own_late[:, cut:], lat_late[:, cut:]))
+    lat_far, _ = lax.optimization_barrier((across(lat_late), noi[2]))
     lat_core = core(below(lat, lat_far))
-    times, embed, _ = lax.optimization_barrier((times, embed, keep))
-    table, column = stage(times, embed)
-    lat_core, table, column = lax.optimization_barrier((lat_core, table, column))
     part = gram_block(clips, lat, lat_far, lat_core, *noi)
     got_x, got_v, got_b = across(part), other_val(part), other_both(part)
-    far_mid, got_x = lax.optimization_barrier((across(below(noi[1], noi[2])), got_x))
-    last, got_x = lax.optimization_barrier((noi[3], got_x))
+    own_late, _ = lax.optimization_barrier((own, lat_far))
+    to_far, to_val = stack([own_late, *noi[1:3]])
+    got_mid, far = other_val(to_val), across(to_far)
+    got_last = other_val(send[3])
+    got_own, got_mid, far, got_x = lax.optimization_barrier((got_own, got_mid, far, got_x))
+    got, lat_got = below(got_own[:clips], got_mid, got_last), got_own[clips:]
+    far_rest = across(below(keep[3], got))
     pair = below(part + got_v, got_x + got_b)
-    far_last, *rows = lax.optimization_barrier([across(last)] + [along(pair, k) for k in (1, 2, 3)])
+    rows = [along(pair, k) for k in (1, 2, 3)]
+    far_rest, *rows = lax.optimization_barrier([far_rest] + rows)
     mine = below(pair, *rows)
-    weights = plan(mine, core(mine), clips)
-    far = [far_own[:clips], far_mid]
-    parts = [*noi, core(below(*noi)), *far, far_last, core(below(*far)), core(far_last)]
-    out = finish(column, weights, lat, table, parts)
+    line = below(*keep)
+    beside_core = [core(x) for x in (line, got, far)]
+    other, *beside_core = lax.optimization_barrier([core(mine)] + beside_core)
+    weights = plan(mine, other, clips)
+    parts = [line, beside_core[0], got, beside_core[1]]
+    parts += [far, beside_core[2], far_rest, core(far_rest)]
+    first, second = [], []
+    for k in (0, 1):
+        first += [(k, s * clips) for s in range(4)]
+        second += [(2 + k, s * clips) for s in range(4)]
+    for k in (0, 1):
+        first += [(4 + k, s * clips) for s in range(3)] + [(6 + k, 0)]
+        second += [(6 + k, s * clips) for s in range(1, 5)]
+    out = finish(column, weights, lat, lat_got, table, parts, (first, second))
     return out.reshape(clips, FRAME, out.shape[1])
 
 

time: 48 us -> 43.3 us (0.902)
  waiting for transfers between devices: 14.7 us -> 8.61 us
  starting transfers between devices: 21.7 us -> 24.3 us
  local copies, waits for them, and re-layouts: 0.75 us -> 0.06 us
  Pallas kernels: 10.4 us -> 9.9 us
    ppermute x5 -> x4, waiting for transfers between devices: 4.43 us -> 0.09 us  [across(): return lax.ppermute(x, 'clip', flip(n, 2))]
    ppermute x6, waiting for transfers between devices: 9.32 us -> 5.99 us  [along(): return lax.ppermute(x, 'clip', flip(n, 4 * k))]
    ppermute x2 -> x4, starting transfers between devices: 3.59 us -> 6.26 us  [other_val(): return lax.ppermute(x, 'val', [(0, 1), (1, 0)])]
    ppermute x6, starting transfers between devices: 9.2 us -> 10.6 us  [along(): return lax.ppermute(x, 'clip', flip(n, 4 * k))]
    ppermute x1, starting transfers between devices: 1.48 us -> 0.56 us  [other_both(): return lax.ppermute(x, ('clip', 'val'), pairs)]
    unnamed x6 -> x2, local copies, waits for them, and re-layouts: 0.68 us -> 0.01 us
    ppermute x5 -> x6, waiting for transfers between devices: 0.85 us -> 1.52 us  [core(): return lax.ppermute(x, 'clip', flip(n, 1))]
    pallas_call x1, Pallas kernels: 1.64 us -> 1.1 us  [stage(): pl.pallas_call(stage_kernel, out_shape=[jax.ShapeDtypeStruct(embed.shape,...]
  transfers between devices with their start and end apart: 19 -> 21, of which waited for: 8 -> 9; matrix products, arithmetic and copies ran while one was open for 0% -> 0% of each run, Pallas kernels for 8% -> 7%
where the time goes in v4:
time: 43.3 us; the launch traced here: 43.2 us
  starting transfers between devices  24.3 us (56%)
  Pallas kernels  9.9 us (23%)
  waiting for transfers between devices  8.61 us (20%)
    ppermute x6, starting transfers between devices, along(): return lax.ppermute(x, 'clip', flip(n, 4 * k))  10.6 us
    ppermute x4, starting transfers between devices, other_val(): return lax.ppermute(x, 'val', [(0, 1), (1, 0)])  6.26 us
    ppermute x4, starting transfers between devices, across(): return lax.ppermute(x, 'clip', flip(n, 2))  6.14 us
    ppermute x6, waiting for transfers between devices, along(): return lax.ppermute(x, 'clip', flip(n, 4 * k))  5.99 us
    pallas_call x1, Pallas kernels, finish(): pl.pallas_call(functools.partial(finish_kernel, clips, block, layout), ou...  5.14 us
    pallas_call x1, Pallas kernels, split_frames(): pl.pallas_call(split_kernel, out_shape=[jax.ShapeDtypeStruct(noise.shape,...  1.53 us
    ppermute x6, waiting for transfers between devices, core(): return lax.ppermute(x, 'clip', flip(n, 1))  1.52 us
    pallas_call x1, Pallas kernels, plan(): pl.pallas_call(functools.partial(plan_kernel, clips), out_shape=jax.Shape...  1.48 us
  transfers between devices with their start and end apart: 21, of which 9 were waited for; matrix products, arithmetic and copies ran while one was open for 0% of the time, Pallas kernels for 7%

profile of v4, /device:TPU:0, one launch (start us, length us, event | category | flops | bytes accessed | tf_op | source)
XLA Modules:
  0.0 43.2 jit_solution(16543866953824772924)
XLA Ops:
  0.0 1.5 %split.1 = (bf16[16,4096]{1,0:T(8,128)(2,1)S(1)}, bf16[16,4096]{1,0:T(8,128)(2,1)S(1)}) custom-call(s32[4,16]{1,0:T(4,128)} %bitcast.4, bf16[16,4096]{1,0:T(8,128)(2,1)} %noise_in.1, bf16[16,4096]{1,0:T(8,128)(2,1)} %latents_in.1), custom_call_target="tpu_custom_call" | custom-call | tf_op jit(solution)/shard_map/split/pallas_call | solution.py:132
  1.5 3.1 %collective-permute-start.3 = (bf16[16,4096]{1,0:T(8,128)(2,1)S(1)}, bf16[16,4096]{1,0:T(8,128)(2,1)S(1)}, u32[]{:S(2)}, u32[]{:S(2)}) collective-permute-start(bf16[16,4096]{1,0:T(8,128)(2,1)S(1)} %get-tuple-element.41.refs_0_), channel_id=1, source_target_pairs={{0,8},{2,10},{4,12},{6,14},{8,0},{10,2},{12,4},{14,6},{16,24},{18,... | collective-permute-start | bytes 393224 | tf_op jit(solution)/shard_map/ppermute | solution.py:370
  4.6 2.6 %collective-permute-start.1 = (bf16[16,4096]{1,0:T(8,128)(2,1)S(1)}, bf16[16,4096]{1,0:T(8,128)(2,1)S(1)}, u32[]{:S(2)}, u32[]{:S(2)}) collective-permute-start(bf16[16,4096]{1,0:T(8,128)(2,1)S(1)} %get-tuple-element.41.refs_0_), channel_id=1, source_target_pairs={{0,16},{2,18},{4,20},{6,22},{8,24},{10,26},{12,28},{14,30},{16,0},... | collective-permute-start | bytes 393224 | tf_op jit(solution)/shard_map/ppermute | solution.py:370
  7.2 1.1 %stage.1 = (bf16[64,5120]{1,0:T(8,128)(2,1)S(1)}, f32[16,128]{1,0:T(8,128)S(1)}) custom-call(f32[16]{0:T(128)} %times_in, bf16[64,5120]{1,0:T(8,128)(2,1)} %embed), custom_call_target="tpu_custom_call" | custom-call | bytes 7000000 | tf_op jit(solution)/shard_map/stage/pallas_call | solution.py:160
  8.3 1.6 %collective-permute-start = (bf16[16,4096]{1,0:T(8,128)(2,1)S(1)}, bf16[16,4096]{1,0:T(8,128)(2,1)S(1)}, u32[]{:S(2)}, u32[]{:S(2)}) collective-permute-start(bf16[16,4096]{1,0:T(8,128)(2,1)S(1)} %get-tuple-element.38.lat.lat_keep), channel_id=1, source_target_pairs={{0,4},{2,6},{4,0},{6,2},{8,12},{10,14},{12,8},{14,10},{16,20},{18,... | collective-permute-start | bytes 393224 | tf_op jit(solution)/shard_map/ppermute | solution.py:367
  9.9 1.6 %collective-permute-start.6 = (bf16[32,2048]{1,0:T(8,128)(2,1)S(1)}, bf16[32,2048]{1,0:T(8,128)(2,1)S(1)}, u32[]{:S(2)}, u32[]{:S(2)}) collective-permute-start(bf16[32,2048]{1,0:T(8,128)(2,1)S(1)} %pad_maximum_fusion.4), channel_id=1, source_target_pairs={{0,1},{1,0},{2,3},{3,2},{4,5},{5,4},{6,7},{7,6},{8,9},{9,8},{10,11... | collective-permute-start | bytes 393224 | tf_op jit(solution)/shard_map/ppermute | solution.py:373
  11.5 1.8 %collective-permute-done.1.refs_2_ = bf16[16,4096]{1,0:T(8,128)(2,1)S(1)} collective-permute-done((bf16[16,4096]{1,0:T(8,128)(2,1)S(1)}, bf16[16,4096]{1,0:T(8,128)(2,1)S(1)}, u32[]{:S(2)}, u32[]{:S(2)}) %collective-permute-start.1) | collective-permute-done | bytes 131104 | tf_op jit(solution)/shard_map/ppermute | solution.py:370
  14.0 1.6 %collective-permute-start.7 = (bf16[32,2048]{1,0:T(8,128)(2,1)S(1)}, bf16[32,2048]{1,0:T(8,128)(2,1)S(1)}, u32[]{:S(2)}, u32[]{:S(2)}) collective-permute-start(bf16[32,2048]{1,0:T(8,128)(2,1)S(1)} %get-tuple-element.42), channel_id=1, source_target_pairs={{0,1},{1,0},{2,3},{3,2},{4,5},{5,4},{6,7},{7,6},{8,9},{9,8},{10,11... | collective-permute-start | bytes 393224 | tf_op jit(solution)/shard_map/ppermute | solution.py:373
  15.5 1.5 %collective-permute-start.8 = (bf16[48,2048]{1,0:T(8,128)(2,1)S(1)}, bf16[48,2048]{1,0:T(8,128)(2,1)S(1)}, u32[]{:S(2)}, u32[]{:S(2)}) collective-permute-start(bf16[48,2048]{1,0:T(8,128)(2,1)S(1)} %get-tuple-element.43), channel_id=1, source_target_pairs={{0,4},{2,6},{4,0},{6,2},{8,12},{10,14},{12,8},{14,10},{16,20},{18,... | collective-permute-start | bytes 589832 | tf_op jit(solution)/shard_map/ppermute | solution.py:367
  17.0 1.3 %collective-permute-done.4.refs_3_ = bf16[16,4096]{1,0:T(8,128)(2,1)S(1)} collective-permute-done((bf16[16,4096]{1,0:T(8,128)(2,1)S(1)}, bf16[16,4096]{1,0:T(8,128)(2,1)S(1)}, u32[]{:S(2)}, u32[]{:S(2)}) %collective-permute-start.4) | collective-permute-done | bytes 131104 | tf_op jit(solution)/shard_map/ppermute | solution.py:370
  18.3 1.6 %collective-permute-start.11 = (bf16[16,2048]{1,0:T(8,128)(2,1)S(1)}, bf16[16,2048]{1,0:T(8,128)(2,1)S(1)}, u32[]{:S(2)}, u32[]{:S(2)}) collective-permute-start(bf16[16,2048]{1,0:T(8,128)(2,1)S(1)} %get-tuple-element.64), channel_id=1, source_target_pairs={{0,1},{1,0},{2,3},{3,2},{4,5},{5,4},{6,7},{7,6},{8,9},{9,8},{10,11... | collective-permute-start | bytes 196616 | tf_op jit(solution)/shard_map/ppermute | solution.py:373
  19.9 0.6 %gram.1 = f32[32,128]{1,0:T(8,128)S(1)} custom-call(bf16[16,4096]{1,0:T(8,128)(2,1)S(1)} %get-tuple-element.38.lat.lat_keep, bf16[16,4096]{1,0:T(8,128)(2,1)S(1)} %collective-permute-done.lat_far, bf16[32,4096]{1,0:T(8,128)(2,1)S(1)} %collective-permute-done.2.lat_core, bf16[16,4096]{1,0:T(8,128)(2,1)S(1)} %get-tuple-element.41.refs_0_, ...), custom_call_target="tpu_custom_call" | custom-call | bytes 17500000 | tf_op jit(solution)/shard_map/gram/pallas_call | solution.py:209
  20.6 1.5 %collective-permute-start.9 = (f32[32,128]{1,0:T(8,128)S(1)}, f32[32,128]{1,0:T(8,128)S(1)}, u32[]{:S(2)}, u32[]{:S(2)}) collective-permute-start(f32[32,128]{1,0:T(8,128)S(1)} %gram.1), channel_id=1, source_target_pairs={{0,4},{2,6},{4,0},{6,2},{8,12},{10,14},{12,8},{14,10},{16,20},{18,... | collective-permute-start | bytes 49160 | tf_op jit(solution)/shard_map/ppermute | solution.py:367
  22.8 1.5 %collective-permute-start.5 = (f32[32,128]{1,0:T(8,128)S(1)}, f32[32,128]{1,0:T(8,128)S(1)}, u32[]{:S(2)}, u32[]{:S(2)}) collective-permute-start(f32[32,128]{1,0:T(8,128)S(1)} %gram.1), channel_id=1, source_target_pairs={{0,1},{1,0},{2,3},{3,2},{4,5},{5,4},{6,7},{7,6},{8,9},{9,8},{10,11... | collective-permute-start | bytes 49160 | tf_op jit(solution)/shard_map/ppermute | solution.py:373
  24.4 1.6 %collective-permute-start.12 = (bf16[80,2048]{1,0:T(8,128)(2,1)S(1)}, bf16[80,2048]{1,0:T(8,128)(2,1)S(1)}, u32[]{:S(2)}, u32[]{:S(2)}) collective-permute-start(bf16[80,2048]{1,0:T(8,128)(2,1)S(1)} %pad_maximum_fusion), channel_id=1, source_target_pairs={{0,4},{2,6},{4,0},{6,2},{8,12},{10,14},{12,8},{14,10},{16,20},{18,... | collective-permute-start | bytes 983048 | tf_op jit(solution)/shard_map/ppermute | solution.py:367
  26.0 0.6 %collective-permute-done.5 = f32[32,128]{1,0:T(8,128)S(1)} collective-permute-done((f32[32,128]{1,0:T(8,128)S(1)}, f32[32,128]{1,0:T(8,128)S(1)}, u32[]{:S(2)}, u32[]{:S(2)}) %collective-permute-start.5) | collective-permute-done | bytes 16416 | tf_op jit(solution)/shard_map/ppermute | solution.py:373
  27.0 2.5 %collective-permute-start.15 = (f32[64,128]{1,0:T(8,128)S(1)}, f32[64,128]{1,0:T(8,128)S(1)}, u32[]{:S(2)}, u32[]{:S(2)}) collective-permute-start(f32[64,128]{1,0:T(8,128)S(1)} %pad_maximum_fusion.5), channel_id=1, source_target_pairs={{0,24},{2,26},{4,28},{6,30},{8,16},{10,18},{12,20},{14,22},{16,8},... | collective-permute-start | bytes 98312 | tf_op jit(solution)/shard_map/ppermute | solution.py:370
  29.6 1.8 %collective-permute-start.13 = (f32[64,128]{1,0:T(8,128)S(1)}, f32[64,128]{1,0:T(8,128)S(1)}, u32[]{:S(2)}, u32[]{:S(2)}) collective-permute-start(f32[64,128]{1,0:T(8,128)S(1)} %pad_maximum_fusion.5), channel_id=1, source_target_pairs={{0,8},{2,10},{4,12},{6,14},{8,0},{10,2},{12,4},{14,6},{16,24},{18,... | collective-permute-start | bytes 98312 | tf_op jit(solution)/shard_map/ppermute | solution.py:370
  31.5 1.3 %collective-permute-done.15 = f32[64,128]{1,0:T(8,128)S(1)} collective-permute-done((f32[64,128]{1,0:T(8,128)S(1)}, f32[64,128]{1,0:T(8,128)S(1)}, u32[]{:S(2)}, u32[]{:S(2)}) %collective-permute-start.15) | collective-permute-done | bytes 32800 | tf_op jit(solution)/shard_map/ppermute | solution.py:370
  32.8 1.6 %collective-permute-done.14 = f32[64,128]{1,0:T(8,128)S(1)} collective-permute-done((f32[64,128]{1,0:T(8,128)S(1)}, f32[64,128]{1,0:T(8,128)S(1)}, u32[]{:S(2)}, u32[]{:S(2)}) %collective-permute-start.14) | collective-permute-done | bytes 32800 | tf_op jit(solution)/shard_map/ppermute | solution.py:370
  35.0 0.9 %collective-permute-done.18.refs_3_ = bf16[64,2048]{1,0:T(8,128)(2,1)S(1)} collective-permute-done((bf16[64,2048]{1,0:T(8,128)(2,1)S(1)}, bf16[64,2048]{1,0:T(8,128)(2,1)S(1)}, u32[]{:S(2)}, u32[]{:S(2)}) %collective-permute-start.18) | collective-permute-done | bytes 262176 | tf_op jit(solution)/shard_map/ppermute | solution.py:364
  35.9 0.7 %collective-permute-done.16.other = f32[256,128]{1,0:T(8,128)S(1)} collective-permute-done((f32[256,128]{1,0:T(8,128)S(1)}, f32[256,128]{1,0:T(8,128)S(1)}, u32[]{:S(2)}, u32[]{:S(2)}) %collective-permute-start.16) | collective-permute-done | bytes 131104 | tf_op jit(solution)/shard_map/ppermute | solution.py:364
  36.5 1.5 %plan.1.weights = bf16[16,256]{1,0:T(8,128)(2,1)S(1)} custom-call(f32[256,128]{1,0:T(8,128)S(1)} %constant_dynamic-update-slice_fusion.mine, f32[256,128]{1,0:T(8,128)S(1)} %collective-permute-done.16.other), custom_call_target="tpu_custom_call" | custom-call | tf_op jit(solution)/shard_map/plan/pallas_call | solution.py:257
  38.0 5.1 %finish.1 = bf16[1024,5120]{1,0:T(8,128)(2,1)} custom-call(f32[16,128]{1,0:T(8,128)S(1)} %get-tuple-element.37.column, bf16[16,256]{1,0:T(8,128)(2,1)S(1)} %plan.1.weights, bf16[16,4096]{1,0:T(8,128)(2,1)S(1)} %get-tuple-element.38.lat.lat_keep, bf16[16,2048]{1,0:T(8,128)(2,1)S(1)} %get-tuple-element.61.lat_got, ...), custom_call_target="tpu_custom_call" | custom-call | tf_op jit(solution)/shard_map/finish/pallas_call | solution.py:316
  (42 shorter events, 2.7 us)
Async XLA Ops:
  1.5 12.4 %collective-permute-start.3 = (bf16[16,4096]{1,0:T(8,128)(2,1)S(1)}, bf16[16,4096]{1,0:T(8,128)(2,1)S(1)}, u32[]{:S(2)}, u32[]{:S(2)}) collective-permute-start(bf16[16,4096]{1,0:T(8,128)(2,1)S(1)} %get-tuple-element.41.refs_0_), channel_id=1, source_target_pairs={{0,8},{2,10},{4,12},{6,14},{8,0},{10,2},{12,4},{14,6},{16,24},{18,... | collective-permute-start | bytes 393224 | tf_op jit(solution)/shard_map/ppermute | solution.py:370
  4.6 8.7 %collective-permute-start.1 = (bf16[16,4096]{1,0:T(8,128)(2,1)S(1)}, bf16[16,4096]{1,0:T(8,128)(2,1)S(1)}, u32[]{:S(2)}, u32[]{:S(2)}) collective-permute-start(bf16[16,4096]{1,0:T(8,128)(2,1)S(1)} %get-tuple-element.41.refs_0_), channel_id=1, source_target_pairs={{0,16},{2,18},{4,20},{6,22},{8,24},{10,26},{12,28},{14,30},{16,0},... | collective-permute-start | bytes 393224 | tf_op jit(solution)/shard_map/ppermute | solution.py:370
  8.3 5.0 %collective-permute-start = (bf16[16,4096]{1,0:T(8,128)(2,1)S(1)}, bf16[16,4096]{1,0:T(8,128)(2,1)S(1)}, u32[]{:S(2)}, u32[]{:S(2)}) collective-permute-start(bf16[16,4096]{1,0:T(8,128)(2,1)S(1)} %get-tuple-element.38.lat.lat_keep), channel_id=1, source_target_pairs={{0,4},{2,6},{4,0},{6,2},{8,12},{10,14},{12,8},{14,10},{16,20},{18,... | collective-permute-start | bytes 393224 | tf_op jit(solution)/shard_map/ppermute | solution.py:367
  9.9 12.2 %collective-permute-start.6 = (bf16[32,2048]{1,0:T(8,128)(2,1)S(1)}, bf16[32,2048]{1,0:T(8,128)(2,1)S(1)}, u32[]{:S(2)}, u32[]{:S(2)}) collective-permute-start(bf16[32,2048]{1,0:T(8,128)(2,1)S(1)} %pad_maximum_fusion.4), channel_id=1, source_target_pairs={{0,1},{1,0},{2,3},{3,2},{4,5},{5,4},{6,7},{7,6},{8,9},{9,8},{10,11... | collective-permute-start | bytes 393224 | tf_op jit(solution)/shard_map/ppermute | solution.py:373
  13.4 5.0 %collective-permute-start.4 = (bf16[16,4096]{1,0:T(8,128)(2,1)S(1)}, bf16[16,4096]{1,0:T(8,128)(2,1)S(1)}, u32[]{:S(2)}, u32[]{:S(2)}) collective-permute-start(bf16[16,4096]{1,0:T(8,128)(2,1)S(1)} %collective-permute-done.1.refs_2_), channel_id=1, source_target_pairs={{0,8},{2,10},{4,12},{6,14},{8,0},{10,2},{12,4},{14,6},{16,24},{18,... | collective-permute-start | bytes 393224 | tf_op jit(solution)/shard_map/ppermute | solution.py:370
  13.8 6.1 %collective-permute-start.2 = (bf16[32,4096]{1,0:T(8,128)(2,1)S(1)}, bf16[32,4096]{1,0:T(8,128)(2,1)S(1)}, u32[]{:S(2)}, u32[]{:S(2)}) collective-permute-start(bf16[32,4096]{1,0:T(8,128)(2,1)S(1)} %pad_maximum_fusion.1), channel_id=1, source_target_pairs={{0,2},{2,0},{4,6},{6,4},{8,10},{10,8},{12,14},{14,12},{16,18},{18,... | collective-permute-start | bytes 786440 | tf_op jit(solution)/shard_map/ppermute | solution.py:364
  14.0 8.2 %collective-permute-start.7 = (bf16[32,2048]{1,0:T(8,128)(2,1)S(1)}, bf16[32,2048]{1,0:T(8,128)(2,1)S(1)}, u32[]{:S(2)}, u32[]{:S(2)}) collective-permute-start(bf16[32,2048]{1,0:T(8,128)(2,1)S(1)} %get-tuple-element.42), channel_id=1, source_target_pairs={{0,1},{1,0},{2,3},{3,2},{4,5},{5,4},{6,7},{7,6},{8,9},{9,8},{10,11... | collective-permute-start | bytes 393224 | tf_op jit(solution)/shard_map/ppermute | solution.py:373
  15.5 7.2 %collective-permute-start.8 = (bf16[48,2048]{1,0:T(8,128)(2,1)S(1)}, bf16[48,2048]{1,0:T(8,128)(2,1)S(1)}, u32[]{:S(2)}, u32[]{:S(2)}) collective-permute-start(bf16[48,2048]{1,0:T(8,128)(2,1)S(1)} %get-tuple-element.43), channel_id=1, source_target_pairs={{0,4},{2,6},{4,0},{6,2},{8,12},{10,14},{12,8},{14,10},{16,20},{18,... | collective-permute-start | bytes 589832 | tf_op jit(solution)/shard_map/ppermute | solution.py:367
  18.3 6.0 %collective-permute-start.11 = (bf16[16,2048]{1,0:T(8,128)(2,1)S(1)}, bf16[16,2048]{1,0:T(8,128)(2,1)S(1)}, u32[]{:S(2)}, u32[]{:S(2)}) collective-permute-start(bf16[16,2048]{1,0:T(8,128)(2,1)S(1)} %get-tuple-element.64), channel_id=1, source_target_pairs={{0,1},{1,0},{2,3},{3,2},{4,5},{5,4},{6,7},{7,6},{8,9},{9,8},{10,11... | collective-permute-start | bytes 196616 | tf_op jit(solution)/shard_map/ppermute | solution.py:373
  20.6 3.8 %collective-permute-start.9 = (f32[32,128]{1,0:T(8,128)S(1)}, f32[32,128]{1,0:T(8,128)S(1)}, u32[]{:S(2)}, u32[]{:S(2)}) collective-permute-start(f32[32,128]{1,0:T(8,128)S(1)} %gram.1), channel_id=1, source_target_pairs={{0,4},{2,6},{4,0},{6,2},{8,12},{10,14},{12,8},{14,10},{16,20},{18,... | collective-permute-start | bytes 49160 | tf_op jit(solution)/shard_map/ppermute | solution.py:367
  22.1 12.9 %collective-permute-start.17 = (bf16[64,2048]{1,0:T(8,128)(2,1)S(1)}, bf16[64,2048]{1,0:T(8,128)(2,1)S(1)}, u32[]{:S(2)}, u32[]{:S(2)}) collective-permute-start(bf16[64,2048]{1,0:T(8,128)(2,1)S(1)} %pad_maximum_fusion.2.refs_0_), channel_id=1, source_target_pairs={{0,2},{2,0},{4,6},{6,4},{8,10},{10,8},{12,14},{14,12},{16,18},{18,... | collective-permute-start | bytes 786440 | tf_op jit(solution)/shard_map/ppermute | solution.py:364
  22.2 4.8 %collective-permute-start.10 = (f32[32,128]{1,0:T(8,128)S(1)}, f32[32,128]{1,0:T(8,128)S(1)}, u32[]{:S(2)}, u32[]{:S(2)}) collective-permute-start(f32[32,128]{1,0:T(8,128)S(1)} %gram.1), channel_id=1, source_target_pairs={{0,5},{1,4},{2,7},{3,6},{4,1},{5,0},{6,3},{7,2},{8,13},{9,12},{10,... | collective-permute-start | bytes 49160 | tf_op jit(solution)/shard_map/ppermute | solution.py:377
  22.8 3.8 %collective-permute-start.5 = (f32[32,128]{1,0:T(8,128)S(1)}, f32[32,128]{1,0:T(8,128)S(1)}, u32[]{:S(2)}, u32[]{:S(2)}) collective-permute-start(f32[32,128]{1,0:T(8,128)S(1)} %gram.1), channel_id=1, source_target_pairs={{0,1},{1,0},{2,3},{3,2},{4,5},{5,4},{6,7},{7,6},{8,9},{9,8},{10,11... | collective-permute-start | bytes 49160 | tf_op jit(solution)/shard_map/ppermute | solution.py:373
  24.4 10.0 %collective-permute-start.12 = (bf16[80,2048]{1,0:T(8,128)(2,1)S(1)}, bf16[80,2048]{1,0:T(8,128)(2,1)S(1)}, u32[]{:S(2)}, u32[]{:S(2)}) collective-permute-start(bf16[80,2048]{1,0:T(8,128)(2,1)S(1)} %pad_maximum_fusion), channel_id=1, source_target_pairs={{0,4},{2,6},{4,0},{6,2},{8,12},{10,14},{12,8},{14,10},{16,20},{18,... | collective-permute-start | bytes 983048 | tf_op jit(solution)/shard_map/ppermute | solution.py:367
  27.0 5.8 %collective-permute-start.15 = (f32[64,128]{1,0:T(8,128)S(1)}, f32[64,128]{1,0:T(8,128)S(1)}, u32[]{:S(2)}, u32[]{:S(2)}) collective-permute-start(f32[64,128]{1,0:T(8,128)S(1)} %pad_maximum_fusion.5), channel_id=1, source_target_pairs={{0,24},{2,26},{4,28},{6,30},{8,16},{10,18},{12,20},{14,22},{16,8},... | collective-permute-start | bytes 98312 | tf_op jit(solution)/shard_map/ppermute | solution.py:370
  29.5 4.8 %collective-permute-start.14 = (f32[64,128]{1,0:T(8,128)S(1)}, f32[64,128]{1,0:T(8,128)S(1)}, u32[]{:S(2)}, u32[]{:S(2)}) collective-permute-start(f32[64,128]{1,0:T(8,128)S(1)} %pad_maximum_fusion.5), channel_id=1, source_target_pairs={{0,16},{2,18},{4,20},{6,22},{8,24},{10,26},{12,28},{14,30},{16,0},... | collective-permute-start | bytes 98312 | tf_op jit(solution)/shard_map/ppermute | solution.py:370
  29.6 4.7 %collective-permute-start.13 = (f32[64,128]{1,0:T(8,128)S(1)}, f32[64,128]{1,0:T(8,128)S(1)}, u32[]{:S(2)}, u32[]{:S(2)}) collective-permute-start(f32[64,128]{1,0:T(8,128)S(1)} %pad_maximum_fusion.5), channel_id=1, source_target_pairs={{0,8},{2,10},{4,12},{6,14},{8,0},{10,2},{12,4},{14,6},{16,24},{18,... | collective-permute-start | bytes 98312 | tf_op jit(solution)/shard_map/ppermute | solution.py:370
  32.8 2.3 %collective-permute-start.19 = (bf16[48,2048]{1,0:T(8,128)(2,1)S(1)}, bf16[48,2048]{1,0:T(8,128)(2,1)S(1)}, u32[]{:S(2)}, u32[]{:S(2)}) collective-permute-start(bf16[48,2048]{1,0:T(8,128)(2,1)S(1)} %collective-permute-done.8.refs_4_), channel_id=1, source_target_pairs={{0,2},{2,0},{4,6},{6,4},{8,10},{10,8},{12,14},{14,12},{16,18},{18,... | collective-permute-start | bytes 589832 | tf_op jit(solution)/shard_map/ppermute | solution.py:364
  34.3 1.5 %collective-permute-start.18 = (bf16[64,2048]{1,0:T(8,128)(2,1)S(1)}, bf16[64,2048]{1,0:T(8,128)(2,1)S(1)}, u32[]{:S(2)}, u32[]{:S(2)}) collective-permute-start(bf16[64,2048]{1,0:T(8,128)(2,1)S(1)} %pad_maximum_fusion.3.refs_2_), channel_id=1, source_target_pairs={{0,2},{2,0},{4,6},{6,4},{8,10},{10,8},{12,14},{14,12},{16,18},{18,... | collective-permute-start | bytes 786440 | tf_op jit(solution)/shard_map/ppermute | solution.py:364
  34.3 3.7 %collective-permute-start.20 = (bf16[80,2048]{1,0:T(8,128)(2,1)S(1)}, bf16[80,2048]{1,0:T(8,128)(2,1)S(1)}, u32[]{:S(2)}, u32[]{:S(2)}) collective-permute-start(bf16[80,2048]{1,0:T(8,128)(2,1)S(1)} %collective-permute-done.12.refs_6_), channel_id=1, source_target_pairs={{0,2},{2,0},{4,6},{6,4},{8,10},{10,8},{12,14},{14,12},{16,18},{18,... | collective-permute-start | bytes 983048 | tf_op jit(solution)/shard_map/ppermute | solution.py:364
  34.9 1.6 %collective-permute-start.16 = (f32[256,128]{1,0:T(8,128)S(1)}, f32[256,128]{1,0:T(8,128)S(1)}, u32[]{:S(2)}, u32[]{:S(2)}) collective-permute-start(f32[256,128]{1,0:T(8,128)S(1)} %constant_dynamic-update-slice_fusion.mine), channel_id=1, source_target_pairs={{0,2},{2,0},{4,6},{6,4},{8,10},{10,8},{12,14},{14,12},{16,18},{18,... | collective-permute-start | bytes 393224 | tf_op jit(solution)/shard_map/ppermute | solution.py:364

commit v5 on v4

--- a/solution.py
+++ b/solution.py
@@ -101,51 +101,44 @@
         out[:, near] = jnp.where(frame == 0, first, second).astype(BF16)
 
 
-def split_kernel(
-    offsets_in, noise_in, latents_in, noise_out, lat_out, offsets, noise, latents, sems
-):
-    copies = [
-        pltpu.make_async_copy(src, dst, sems.at[k])
-        for k, (src, dst) in enumerate(
-            ((offsets_in, offsets), (noise_in, noise), (latents_in, latents))
-        )
-    ]
-    for c in copies:
-        c.start()
+def split_kernel(offsets_in, noise_in, noise_out, offsets, noise, sems):
+    small = pltpu.make_async_copy(offsets_in, offsets, sems.at[0])
+    load = pltpu.make_async_copy(noise_in, noise, sems.at[1])
+    small.start()
+    load.start()
     val = lax.axis_index("val")
-    copies[0].wait()
-    copies[1].wait()
     cut = noise.shape[1] // 2
+    small.wait()
+    load.wait()
     warp_frame(offsets, noise, val, noise_out.at[:, :cut])
     warp_frame(offsets, noise, 1 - val, noise_out.at[:, cut:])
-    copies[2].wait()
-    take_frame(latents, val, lat_out.at[:, :cut])
-    take_frame(latents, 1 - val, lat_out.at[:, cut:])
 
 
 def in_hbm(x):
     return pltpu.with_memory_space_constraint(x, pltpu.HBM)
 
 
-def split_frames(noise, latents, offsets):
-    inputs = [flat_offsets(offsets), noise, latents]
+def split_frames(noise, offsets):
+    inputs = [flat_offsets(offsets), noise]
     return pl.pallas_call(
         split_kernel,
-        out_shape=[jax.ShapeDtypeStruct(noise.shape, BF16)] * 2,
-        in_specs=[HBM] * 3,
-        out_specs=[VMEM] * 2,
+        out_shape=jax.ShapeDtypeStruct(noise.shape, BF16),
+        in_specs=[HBM] * 2,
+        out_specs=VMEM,
         scratch_shapes=[pltpu.VMEM(x.shape, x.dtype) for x in inputs]
-        + [pltpu.SemaphoreType.DMA((3,))],
+        + [pltpu.SemaphoreType.DMA((2,))],
         compiler_params=params(),
         name="split",
     )(*map(in_hbm, inputs))
 
 
-def stage_kernel(times_in, embed, table, column, times, sems):
-    load = pltpu.make_async_copy(embed, table, sems.at[0])
-    load.start()
-    small = pltpu.make_async_copy(times_in, times, sems.at[1])
-    small.start()
+def stage_kernel(times_in, embed, latents_in, table, column, lat, times, latents, sems):
+    small = pltpu.make_async_copy(times_in, times, sems.at[0])
+    load = pltpu.make_async_copy(latents_in, latents, sems.at[1])
+    large = pltpu.make_async_copy(embed, table, sems.at[2])
+    for copy in (small, load, large):
+        copy.start()
+    val = lax.axis_index("val")
     clips, lanes = column.shape
     row = lax.broadcasted_iota(jnp.int32, (clips, lanes), 0)
     t = jnp.zeros((clips, lanes), F32)
@@ -153,23 +146,32 @@
     for i in range(clips):
         t = jnp.where(row == i, times[i], t)
     column[...] = t
+    cut = latents.shape[1] // 2
     load.wait()
-
-
-def stage(times, embed):
+    take_frame(latents, val, lat.at[:, :cut])
+    take_frame(latents, 1 - val, lat.at[:, cut:])
+    large.wait()
+
+
+def stage(times, embed, latents):
     return pl.pallas_call(
         stage_kernel,
         out_shape=[
             jax.ShapeDtypeStruct(embed.shape, BF16),
             jax.ShapeDtypeStruct((times.shape[0], 128), F32),
+            jax.ShapeDtypeStruct(latents.shape, BF16),
         ],
-        in_specs=[HBM] * 2,
-        out_specs=[VMEM] * 2,
-        scratch_shapes=[pltpu.SMEM(times.shape, F32), pltpu.SemaphoreType.DMA((2,))],
+        in_specs=[HBM] * 3,
+        out_specs=[VMEM] * 3,
+        scratch_shapes=[
+            pltpu.SMEM(times.shape, F32),
+            pltpu.VMEM(latents.shape, BF16),
+            pltpu.SemaphoreType.DMA((3,)),
+        ],
         compiler_params=params(),
         cost_estimate=cost(2),
         name="stage",
-    )(in_hbm(times), in_hbm(embed))
+    )(*map(in_hbm, (times, embed, latents)))
 
 
 def swap_groups(x, a, clips):
@@ -217,18 +219,21 @@
     )(*args)
 
 
-def sinkhorn(kernel, own):
-    col = jnp.zeros((1, kernel.shape[1]), F32)
-    for _ in range(ITERS):
-        u = kernel + col
-        top = jnp.max(u, axis=1, keepdims=True)
-        row = -(top + jnp.log(jnp.sum(jnp.exp(u - top), axis=1, keepdims=True)))
-        u = kernel + row
-        top = jnp.max(u, axis=0, keepdims=True)
-        col = -(top + jnp.log(jnp.sum(jnp.exp(u - top), axis=0, keepdims=True)))
-    u = own + col
-    top = jnp.max(u, axis=1, keepdims=True)
-    e = jnp.exp(u - top)
+def sinkhorn(kernel):
+    top = jnp.max(kernel, axis=1, keepdims=True)
+    row = top + jnp.log(jnp.sum(jnp.exp(kernel - top), axis=1, keepdims=True))
+    u = kernel - row
+    top = jnp.max(u, axis=0, keepdims=True)
+    share = jnp.exp(u - top)
+    right = 1.0 / jnp.sum(share, axis=0, keepdims=True)
+    for _ in range(ITERS - 1):
+        left = 1.0 / jnp.sum(share * right, axis=1, keepdims=True)
+        right = 1.0 / jnp.sum(share * left, axis=0, keepdims=True)
+    return share, right
+
+
+def softmax_rows(share, right):
+    e = share * right
     return e / jnp.sum(e, axis=1, keepdims=True)
 
 
@@ -245,8 +250,10 @@
             lanes = slice(x * 128, (x + 1) * 128)
             full[r : r + half, lanes] = jnp.where(low, g, pltpu.roll(h, 64, 1))
             full[r + half : r + 2 * half, lanes] = jnp.where(low, pltpu.roll(g, 64, 1), h)
+    share, right = sinkhorn(full[...])
+    full[...] = share
     own = full[pl.ds(pl.multiple_of(b * clips, clips), clips), :]
-    weights = sinkhorn(full[...], own)
+    weights = softmax_rows(own, right)
     for x in range(2):
         lanes = slice(x * 128, (x + 1) * 128)
         out[:, lanes] = swap_groups(weights[:, lanes], a, clips).astype(BF16)
@@ -266,8 +273,8 @@
 
 
 def finish_kernel(clips, block, layout, column, weights, lat_keep, lat_got, table, *refs):
-    parts = refs[:-5]
-    out, cube, lhs, result, sems = refs[-5:]
+    parts = refs[:-4]
+    out, cube, result, sems = refs[-4:]
     val = lax.axis_index("val")
     t = column[:, :1]
     w = weights[...]
@@ -285,32 +292,31 @@
     tiles = values // S
     half = tiles // 2
     low = lax.broadcasted_iota(jnp.int32, (tiles, S), 1) < FRAME
-    for i in range(0, clips, 2):
-        x, y = cube[i], cube[i + 1]
+    per_pair = 2 * FRAME // block
+    steps = clips * FRAME // block
+
+    def store(k):
+        return pltpu.make_async_copy(result.at[k], out.at[pl.ds(k * block, block)], sems.at[k])
+
+    for k in range(clips // 2):
+        x, y = cube[2 * k], cube[2 * k + 1]
         near = jnp.where(low, x, pltpu.roll(y, FRAME, 1))
         far = jnp.where(low, pltpu.roll(x, FRAME, 1), y)
         mine = jnp.concatenate([near[:half], far[:half]], axis=0)
         other = jnp.concatenate([near[half:], far[half:]], axis=0)
-        lanes = slice(i * FRAME, (i + 2) * FRAME)
-        lhs[:tiles, lanes] = jnp.where(val == 0, mine, other).astype(BF16)
-        lhs[tiles:, lanes] = jnp.where(val == 0, other, mine).astype(BF16)
-    tokens = lhs.shape[1]
-    steps = tokens // block
-
-    def store(k):
-        at = pl.multiple_of(k * block, block)
-        return pltpu.make_async_copy(result.at[k], out.at[pl.ds(at, block)], sems.at[k])
-
-    for k in range(steps):
-        result[k] = lax.dot_general(
-            lhs[:, k * block : (k + 1) * block], table[...], TN, preferred_element_type=F32
-        ).astype(BF16)
-        store(k).start()
+        both = [jnp.where(val == 0, mine, other), jnp.where(val == 0, other, mine)]
+        lhs = jnp.concatenate(both, axis=0).astype(BF16)
+        for j in range(per_pair):
+            step = k * per_pair + j
+            tokens = lhs[:, j * block : (j + 1) * block]
+            full = lax.dot_general(tokens, table[...], TN, preferred_element_type=F32)
+            result[step] = full.astype(BF16)
+            store(step).start()
     for k in range(steps):
         store(k).wait()
 
 
-def finish(column, weights, lat_keep, lat_got, table, parts, layout, block=128):
+def finish(column, weights, lat_keep, lat_got, table, parts, layout, block=FRAME):
     clips, values = lat_keep.shape
     tokens, width = clips * FRAME, table.shape[1]
     return pl.pallas_call(
@@ -320,7 +326,6 @@
         out_specs=HBM,
         scratch_shapes=[
             pltpu.VMEM((clips, values // S, S), F32),
-            pltpu.VMEM((P_SIZE, tokens), BF16),
             pltpu.VMEM((tokens // block, block, width), BF16),
             pltpu.SemaphoreType.DMA((tokens // block,)),
         ],
@@ -382,7 +387,7 @@
     def below(*x):
         return jnp.concatenate(x, axis=0)
 
-    own, lat = split_frames(noise, latents, offsets)
+    own = split_frames(noise, offsets)
     cut = own.shape[1] // 2
     noi = [own]
     noi.append(along(own, 1))
@@ -390,11 +395,11 @@
     noi.append(along(noi[2], 1))
     keep = [x[:, :cut] for x in noi]
     send = [x[:, cut:] for x in noi]
-    times, embed, _ = lax.optimization_barrier((times, embed, own))
-    table, column = stage(times, embed)
-    lat_late, own_late, table, column = lax.optimization_barrier((lat, own, table, column))
-    got_own = other_val(below(own_late[:, cut:], lat_late[:, cut:]))
-    lat_far, _ = lax.optimization_barrier((across(lat_late), noi[2]))
+    times, embed, latents, _ = lax.optimization_barrier((times, embed, latents, own))
+    table, column, lat = stage(times, embed, latents)
+    own_late, lat = lax.optimization_barrier((own, lat))
+    got_own = other_val(below(own_late[:, cut:], lat[:, cut:]))
+    lat_far, _ = lax.optimization_barrier((across(lat), noi[2]))
     lat_core = core(below(lat, lat_far))
     part = gram_block(clips, lat, lat_far, lat_core, *noi)
     got_x, got_v, got_b = across(part), other_val(part), other_both(part)
@@ -411,7 +416,7 @@
     mine = below(pair, *rows)
     line = below(*keep)
     beside_core = [core(x) for x in (line, got, far)]
-    other, *beside_core = lax.optimization_barrier([core(mine)] + beside_core)
+    other = core(mine)
     weights = plan(mine, other, clips)
     parts = [line, beside_core[0], got, beside_core[1]]
     parts += [far, beside_core[2], far_rest, core(far_rest)]
@@ -434,7 +439,9 @@
     square = jnp.sum(jnp.square(panel.astype(F32)), axis=1)
     part = lax.psum(square[None, :] - 2.0 * gram, "val")
     full = lax.all_gather(part, "clip", axis=0, tiled=True) * (-SCALE)
-    weights = sinkhorn(full, part * (-SCALE)).astype(BF16)
+    share, right = sinkhorn(full)
+    own = lax.dynamic_slice_in_dim(share, lax.axis_index("clip") * clips, clips, axis=0)
+    weights = softmax_rows(own, right).astype(BF16)
     coupled = jnp.dot(weights, panel, preferred_element_type=F32)
     t = times[:, None]
     mixed = ((1.0 - t) * latents.astype(F32) + t * coupled).astype(BF16)

time: 43.3 us -> 42.5 us (0.982)
  Pallas kernels: 9.9 us -> 9.11 us
    pallas_call x1, Pallas kernels: 1.48 us -> 0.98 us  [plan(): pl.pallas_call(functools.partial(plan_kernel, clips), out_shape=jax.Shape...]
where the time goes in v5:
time: 42.5 us; the launch traced here: 42.3 us
  starting transfers between devices  24.3 us (57%)
  Pallas kernels  9.11 us (21%)
  waiting for transfers between devices  8.54 us (20%)
    ppermute x6, starting transfers between devices, along(): return lax.ppermute(x, 'clip', flip(n, 4 * k))  10.6 us
    ppermute x4, starting transfers between devices, other_val(): return lax.ppermute(x, 'val', [(0, 1), (1, 0)])  6.25 us
    ppermute x4, starting transfers between devices, across(): return lax.ppermute(x, 'clip', flip(n, 2))  6.15 us
    ppermute x6, waiting for transfers between devices, along(): return lax.ppermute(x, 'clip', flip(n, 4 * k))  5.82 us
    pallas_call x1, Pallas kernels, finish(): pl.pallas_call(functools.partial(finish_kernel, clips, block, layout), ou...  4.92 us
    ppermute x6, waiting for transfers between devices, core(): return lax.ppermute(x, 'clip', flip(n, 1))  1.53 us
    pallas_call x1, Pallas kernels, split_frames(): pl.pallas_call(split_kernel, out_shape=jax.ShapeDtypeStruct(noise.shape,...  1.38 us
    pallas_call x1, Pallas kernels, stage(): pl.pallas_call(stage_kernel, out_shape=[jax.ShapeDtypeStruct(embed.shape,...  1.19 us
  transfers between devices with their start and end apart: 21, of which 9 were waited for; matrix products, arithmetic and copies ran while one was open for 0% of the time, Pallas kernels for 7%

profile of v5, /device:TPU:0, one launch (start us, length us, event | category | flops | bytes accessed | tf_op | source)
XLA Modules:
  0.0 42.3 jit_solution(5578285179729310764)
XLA Ops:
  0.0 1.4 %split.1.refs_0_ = bf16[16,4096]{1,0:T(8,128)(2,1)S(1)} custom-call(s32[4,16]{1,0:T(4,128)} %bitcast.4, bf16[16,4096]{1,0:T(8,128)(2,1)} %noise_in.1), custom_call_target="tpu_custom_call" | custom-call | tf_op jit(solution)/shard_map/split/pallas_call | solution.py:123
  1.4 3.1 %collective-permute-start.3 = (bf16[16,4096]{1,0:T(8,128)(2,1)S(1)}, bf16[16,4096]{1,0:T(8,128)(2,1)S(1)}, u32[]{:S(2)}, u32[]{:S(2)}) collective-permute-start(bf16[16,4096]{1,0:T(8,128)(2,1)S(1)} %split.1.refs_0_), channel_id=1, source_target_pairs={{0,8},{2,10},{4,12},{6,14},{8,0},{10,2},{12,4},{14,6},{16,24},{18,... | collective-permute-start | bytes 393224 | tf_op jit(solution)/shard_map/ppermute | solution.py:375
  4.5 2.6 %collective-permute-start.1 = (bf16[16,4096]{1,0:T(8,128)(2,1)S(1)}, bf16[16,4096]{1,0:T(8,128)(2,1)S(1)}, u32[]{:S(2)}, u32[]{:S(2)}) collective-permute-start(bf16[16,4096]{1,0:T(8,128)(2,1)S(1)} %split.1.refs_0_), channel_id=1, source_target_pairs={{0,16},{2,18},{4,20},{6,22},{8,24},{10,26},{12,28},{14,30},{16,0},... | collective-permute-start | bytes 393224 | tf_op jit(solution)/shard_map/ppermute | solution.py:375
  7.1 1.2 %stage.1 = (bf16[64,5120]{1,0:T(8,128)(2,1)S(1)}, f32[16,128]{1,0:T(8,128)S(1)}, bf16[16,4096]{1,0:T(8,128)(2,1)S(1)}) custom-call(f32[16]{0:T(128)} %times_in, bf16[64,5120]{1,0:T(8,128)(2,1)} %embed, bf16[16,4096]{1,0:T(8,128)(2,1)} %latents_in), custom_call_target="tpu_custom_call" | custom-call | bytes 7000000 | tf_op jit(solution)/shard_map/stage/pallas_call | solution.py:157
  8.3 1.6 %collective-permute-start = (bf16[16,4096]{1,0:T(8,128)(2,1)S(1)}, bf16[16,4096]{1,0:T(8,128)(2,1)S(1)}, u32[]{:S(2)}, u32[]{:S(2)}) collective-permute-start(bf16[16,4096]{1,0:T(8,128)(2,1)S(1)} %get-tuple-element.30.lat.lat_keep), channel_id=1, source_target_pairs={{0,4},{2,6},{4,0},{6,2},{8,12},{10,14},{12,8},{14,10},{16,20},{18,... | collective-permute-start | bytes 393224 | tf_op jit(solution)/shard_map/ppermute | solution.py:372
  9.8 1.6 %collective-permute-start.6 = (bf16[32,2048]{1,0:T(8,128)(2,1)S(1)}, bf16[32,2048]{1,0:T(8,128)(2,1)S(1)}, u32[]{:S(2)}, u32[]{:S(2)}) collective-permute-start(bf16[32,2048]{1,0:T(8,128)(2,1)S(1)} %pad_maximum_fusion.4), channel_id=1, source_target_pairs={{0,1},{1,0},{2,3},{3,2},{4,5},{5,4},{6,7},{7,6},{8,9},{9,8},{10,11... | collective-permute-start | bytes 393224 | tf_op jit(solution)/shard_map/ppermute | solution.py:378
  11.4 1.7 %collective-permute-done.1.refs_2_ = bf16[16,4096]{1,0:T(8,128)(2,1)S(1)} collective-permute-done((bf16[16,4096]{1,0:T(8,128)(2,1)S(1)}, bf16[16,4096]{1,0:T(8,128)(2,1)S(1)}, u32[]{:S(2)}, u32[]{:S(2)}) %collective-permute-start.1) | collective-permute-done | bytes 131104 | tf_op jit(solution)/shard_map/ppermute | solution.py:375
  13.9 1.6 %collective-permute-start.7 = (bf16[32,2048]{1,0:T(8,128)(2,1)S(1)}, bf16[32,2048]{1,0:T(8,128)(2,1)S(1)}, u32[]{:S(2)}, u32[]{:S(2)}) collective-permute-start(bf16[32,2048]{1,0:T(8,128)(2,1)S(1)} %get-tuple-element.34), channel_id=1, source_target_pairs={{0,1},{1,0},{2,3},{3,2},{4,5},{5,4},{6,7},{7,6},{8,9},{9,8},{10,11... | collective-permute-start | bytes 393224 | tf_op jit(solution)/shard_map/ppermute | solution.py:378
  15.5 1.5 %collective-permute-start.8 = (bf16[48,2048]{1,0:T(8,128)(2,1)S(1)}, bf16[48,2048]{1,0:T(8,128)(2,1)S(1)}, u32[]{:S(2)}, u32[]{:S(2)}) collective-permute-start(bf16[48,2048]{1,0:T(8,128)(2,1)S(1)} %get-tuple-element.35), channel_id=1, source_target_pairs={{0,4},{2,6},{4,0},{6,2},{8,12},{10,14},{12,8},{14,10},{16,20},{18,... | collective-permute-start | bytes 589832 | tf_op jit(solution)/shard_map/ppermute | solution.py:372
  17.0 1.3 %collective-permute-done.4.refs_3_ = bf16[16,4096]{1,0:T(8,128)(2,1)S(1)} collective-permute-done((bf16[16,4096]{1,0:T(8,128)(2,1)S(1)}, bf16[16,4096]{1,0:T(8,128)(2,1)S(1)}, u32[]{:S(2)}, u32[]{:S(2)}) %collective-permute-start.4) | collective-permute-done | bytes 131104 | tf_op jit(solution)/shard_map/ppermute | solution.py:375
  18.3 1.6 %collective-permute-start.11 = (bf16[16,2048]{1,0:T(8,128)(2,1)S(1)}, bf16[16,2048]{1,0:T(8,128)(2,1)S(1)}, u32[]{:S(2)}, u32[]{:S(2)}) collective-permute-start(bf16[16,2048]{1,0:T(8,128)(2,1)S(1)} %get-tuple-element.52), channel_id=1, source_target_pairs={{0,1},{1,0},{2,3},{3,2},{4,5},{5,4},{6,7},{7,6},{8,9},{9,8},{10,11... | collective-permute-start | bytes 196616 | tf_op jit(solution)/shard_map/ppermute | solution.py:378
  19.9 0.6 %gram.1 = f32[32,128]{1,0:T(8,128)S(1)} custom-call(bf16[16,4096]{1,0:T(8,128)(2,1)S(1)} %get-tuple-element.30.lat.lat_keep, bf16[16,4096]{1,0:T(8,128)(2,1)S(1)} %collective-permute-done.lat_far, bf16[32,4096]{1,0:T(8,128)(2,1)S(1)} %collective-permute-done.2.lat_core, bf16[16,4096]{1,0:T(8,128)(2,1)S(1)} %split.1.refs_0_, ...), custom_call_target="tpu_custom_call" | custom-call | bytes 17500000 | tf_op jit(solution)/shard_map/gram/pallas_call | solution.py:211
  20.5 1.5 %collective-permute-start.9 = (f32[32,128]{1,0:T(8,128)S(1)}, f32[32,128]{1,0:T(8,128)S(1)}, u32[]{:S(2)}, u32[]{:S(2)}) collective-permute-start(f32[32,128]{1,0:T(8,128)S(1)} %gram.1), channel_id=1, source_target_pairs={{0,4},{2,6},{4,0},{6,2},{8,12},{10,14},{12,8},{14,10},{16,20},{18,... | collective-permute-start | bytes 49160 | tf_op jit(solution)/shard_map/ppermute | solution.py:372
  22.1 0.6 %collective-permute-start.10 = (f32[32,128]{1,0:T(8,128)S(1)}, f32[32,128]{1,0:T(8,128)S(1)}, u32[]{:S(2)}, u32[]{:S(2)}) collective-permute-start(f32[32,128]{1,0:T(8,128)S(1)} %gram.1), channel_id=1, source_target_pairs={{0,5},{1,4},{2,7},{3,6},{4,1},{5,0},{6,3},{7,2},{8,13},{9,12},{10,... | collective-permute-start | bytes 49160 | tf_op jit(solution)/shard_map/ppermute | solution.py:382
  22.7 1.5 %collective-permute-start.5 = (f32[32,128]{1,0:T(8,128)S(1)}, f32[32,128]{1,0:T(8,128)S(1)}, u32[]{:S(2)}, u32[]{:S(2)}) collective-permute-start(f32[32,128]{1,0:T(8,128)S(1)} %gram.1), channel_id=1, source_target_pairs={{0,1},{1,0},{2,3},{3,2},{4,5},{5,4},{6,7},{7,6},{8,9},{9,8},{10,11... | collective-permute-start | bytes 49160 | tf_op jit(solution)/shard_map/ppermute | solution.py:378
  24.3 1.6 %collective-permute-start.12 = (bf16[80,2048]{1,0:T(8,128)(2,1)S(1)}, bf16[80,2048]{1,0:T(8,128)(2,1)S(1)}, u32[]{:S(2)}, u32[]{:S(2)}) collective-permute-start(bf16[80,2048]{1,0:T(8,128)(2,1)S(1)} %pad_maximum_fusion), channel_id=1, source_target_pairs={{0,4},{2,6},{4,0},{6,2},{8,12},{10,14},{12,8},{14,10},{16,20},{18,... | collective-permute-start | bytes 983048 | tf_op jit(solution)/shard_map/ppermute | solution.py:372
  25.9 0.6 %collective-permute-done.5 = f32[32,128]{1,0:T(8,128)S(1)} collective-permute-done((f32[32,128]{1,0:T(8,128)S(1)}, f32[32,128]{1,0:T(8,128)S(1)}, u32[]{:S(2)}, u32[]{:S(2)}) %collective-permute-start.5) | collective-permute-done | bytes 16416 | tf_op jit(solution)/shard_map/ppermute | solution.py:378
  26.9 2.4 %collective-permute-start.15 = (f32[64,128]{1,0:T(8,128)S(1)}, f32[64,128]{1,0:T(8,128)S(1)}, u32[]{:S(2)}, u32[]{:S(2)}) collective-permute-start(f32[64,128]{1,0:T(8,128)S(1)} %pad_maximum_fusion.5), channel_id=1, source_target_pairs={{0,24},{2,26},{4,28},{6,30},{8,16},{10,18},{12,20},{14,22},{16,8},... | collective-permute-start | bytes 98312 | tf_op jit(solution)/shard_map/ppermute | solution.py:375
  29.6 1.8 %collective-permute-start.13 = (f32[64,128]{1,0:T(8,128)S(1)}, f32[64,128]{1,0:T(8,128)S(1)}, u32[]{:S(2)}, u32[]{:S(2)}) collective-permute-start(f32[64,128]{1,0:T(8,128)S(1)} %pad_maximum_fusion.5), channel_id=1, source_target_pairs={{0,8},{2,10},{4,12},{6,14},{8,0},{10,2},{12,4},{14,6},{16,24},{18,... | collective-permute-start | bytes 98312 | tf_op jit(solution)/shard_map/ppermute | solution.py:375
  31.4 1.3 %collective-permute-done.15 = f32[64,128]{1,0:T(8,128)S(1)} collective-permute-done((f32[64,128]{1,0:T(8,128)S(1)}, f32[64,128]{1,0:T(8,128)S(1)}, u32[]{:S(2)}, u32[]{:S(2)}) %collective-permute-start.15) | collective-permute-done | bytes 32800 | tf_op jit(solution)/shard_map/ppermute | solution.py:375
  32.7 1.5 %collective-permute-done.14 = f32[64,128]{1,0:T(8,128)S(1)} collective-permute-done((f32[64,128]{1,0:T(8,128)S(1)}, f32[64,128]{1,0:T(8,128)S(1)}, u32[]{:S(2)}, u32[]{:S(2)}) %collective-permute-start.14) | collective-permute-done | bytes 32800 | tf_op jit(solution)/shard_map/ppermute | solution.py:375
  34.9 1.5 %collective-permute-done.16.other = f32[256,128]{1,0:T(8,128)S(1)} collective-permute-done((f32[256,128]{1,0:T(8,128)S(1)}, f32[256,128]{1,0:T(8,128)S(1)}, u32[]{:S(2)}, u32[]{:S(2)}) %collective-permute-start.16) | collective-permute-done | bytes 131104 | tf_op jit(solution)/shard_map/ppermute | solution.py:369
  36.4 1.0 %plan.1.weights = bf16[16,256]{1,0:T(8,128)(2,1)S(1)} custom-call(f32[256,128]{1,0:T(8,128)S(1)} %constant_dynamic-update-slice_fusion.mine, f32[256,128]{1,0:T(8,128)S(1)} %collective-permute-done.16.other), custom_call_target="tpu_custom_call" | custom-call | tf_op jit(solution)/shard_map/plan/pallas_call | solution.py:264
  37.4 4.9 %finish.1 = bf16[1024,5120]{1,0:T(8,128)(2,1)} custom-call(f32[16,128]{1,0:T(8,128)S(1)} %get-tuple-element.28.column, bf16[16,256]{1,0:T(8,128)(2,1)S(1)} %plan.1.weights, bf16[16,4096]{1,0:T(8,128)(2,1)S(1)} %get-tuple-element.30.lat.lat_keep, bf16[16,2048]{1,0:T(8,128)(2,1)S(1)} %get-tuple-element.49.lat_got, ...), custom_call_target="tpu_custom_call" | custom-call | tf_op jit(solution)/shard_map/finish/pallas_call | solution.py:322
  (42 shorter events, 2.3 us)
Async XLA Ops:
  1.4 12.5 %collective-permute-start.3 = (bf16[16,4096]{1,0:T(8,128)(2,1)S(1)}, bf16[16,4096]{1,0:T(8,128)(2,1)S(1)}, u32[]{:S(2)}, u32[]{:S(2)}) collective-permute-start(bf16[16,4096]{1,0:T(8,128)(2,1)S(1)} %split.1.refs_0_), channel_id=1, source_target_pairs={{0,8},{2,10},{4,12},{6,14},{8,0},{10,2},{12,4},{14,6},{16,24},{18,... | collective-permute-start | bytes 393224 | tf_op jit(solution)/shard_map/ppermute | solution.py:375
  4.5 8.7 %collective-permute-start.1 = (bf16[16,4096]{1,0:T(8,128)(2,1)S(1)}, bf16[16,4096]{1,0:T(8,128)(2,1)S(1)}, u32[]{:S(2)}, u32[]{:S(2)}) collective-permute-start(bf16[16,4096]{1,0:T(8,128)(2,1)S(1)} %split.1.refs_0_), channel_id=1, source_target_pairs={{0,16},{2,18},{4,20},{6,22},{8,24},{10,26},{12,28},{14,30},{16,0},... | collective-permute-start | bytes 393224 | tf_op jit(solution)/shard_map/ppermute | solution.py:375
  8.3 5.0 %collective-permute-start = (bf16[16,4096]{1,0:T(8,128)(2,1)S(1)}, bf16[16,4096]{1,0:T(8,128)(2,1)S(1)}, u32[]{:S(2)}, u32[]{:S(2)}) collective-permute-start(bf16[16,4096]{1,0:T(8,128)(2,1)S(1)} %get-tuple-element.30.lat.lat_keep), channel_id=1, source_target_pairs={{0,4},{2,6},{4,0},{6,2},{8,12},{10,14},{12,8},{14,10},{16,20},{18,... | collective-permute-start | bytes 393224 | tf_op jit(solution)/shard_map/ppermute | solution.py:372
  9.8 12.2 %collective-permute-start.6 = (bf16[32,2048]{1,0:T(8,128)(2,1)S(1)}, bf16[32,2048]{1,0:T(8,128)(2,1)S(1)}, u32[]{:S(2)}, u32[]{:S(2)}) collective-permute-start(bf16[32,2048]{1,0:T(8,128)(2,1)S(1)} %pad_maximum_fusion.4), channel_id=1, source_target_pairs={{0,1},{1,0},{2,3},{3,2},{4,5},{5,4},{6,7},{7,6},{8,9},{9,8},{10,11... | collective-permute-start | bytes 393224 | tf_op jit(solution)/shard_map/ppermute | solution.py:378
  13.3 5.0 %collective-permute-start.4 = (bf16[16,4096]{1,0:T(8,128)(2,1)S(1)}, bf16[16,4096]{1,0:T(8,128)(2,1)S(1)}, u32[]{:S(2)}, u32[]{:S(2)}) collective-permute-start(bf16[16,4096]{1,0:T(8,128)(2,1)S(1)} %collective-permute-done.1.refs_2_), channel_id=1, source_target_pairs={{0,8},{2,10},{4,12},{6,14},{8,0},{10,2},{12,4},{14,6},{16,24},{18,... | collective-permute-start | bytes 393224 | tf_op jit(solution)/shard_map/ppermute | solution.py:375
  13.8 6.1 %collective-permute-start.2 = (bf16[32,4096]{1,0:T(8,128)(2,1)S(1)}, bf16[32,4096]{1,0:T(8,128)(2,1)S(1)}, u32[]{:S(2)}, u32[]{:S(2)}) collective-permute-start(bf16[32,4096]{1,0:T(8,128)(2,1)S(1)} %pad_maximum_fusion.1), channel_id=1, source_target_pairs={{0,2},{2,0},{4,6},{6,4},{8,10},{10,8},{12,14},{14,12},{16,18},{18,... | collective-permute-start | bytes 786440 | tf_op jit(solution)/shard_map/ppermute | solution.py:369
  13.9 8.2 %collective-permute-start.7 = (bf16[32,2048]{1,0:T(8,128)(2,1)S(1)}, bf16[32,2048]{1,0:T(8,128)(2,1)S(1)}, u32[]{:S(2)}, u32[]{:S(2)}) collective-permute-start(bf16[32,2048]{1,0:T(8,128)(2,1)S(1)} %get-tuple-element.34), channel_id=1, source_target_pairs={{0,1},{1,0},{2,3},{3,2},{4,5},{5,4},{6,7},{7,6},{8,9},{9,8},{10,11... | collective-permute-start | bytes 393224 | tf_op jit(solution)/shard_map/ppermute | solution.py:378
  15.5 7.2 %collective-permute-start.8 = (bf16[48,2048]{1,0:T(8,128)(2,1)S(1)}, bf16[48,2048]{1,0:T(8,128)(2,1)S(1)}, u32[]{:S(2)}, u32[]{:S(2)}) collective-permute-start(bf16[48,2048]{1,0:T(8,128)(2,1)S(1)} %get-tuple-element.35), channel_id=1, source_target_pairs={{0,4},{2,6},{4,0},{6,2},{8,12},{10,14},{12,8},{14,10},{16,20},{18,... | collective-permute-start | bytes 589832 | tf_op jit(solution)/shard_map/ppermute | solution.py:372
  18.3 6.0 %collective-permute-start.11 = (bf16[16,2048]{1,0:T(8,128)(2,1)S(1)}, bf16[16,2048]{1,0:T(8,128)(2,1)S(1)}, u32[]{:S(2)}, u32[]{:S(2)}) collective-permute-start(bf16[16,2048]{1,0:T(8,128)(2,1)S(1)} %get-tuple-element.52), channel_id=1, source_target_pairs={{0,1},{1,0},{2,3},{3,2},{4,5},{5,4},{6,7},{7,6},{8,9},{9,8},{10,11... | collective-permute-start | bytes 196616 | tf_op jit(solution)/shard_map/ppermute | solution.py:378
  20.5 3.8 %collective-permute-start.9 = (f32[32,128]{1,0:T(8,128)S(1)}, f32[32,128]{1,0:T(8,128)S(1)}, u32[]{:S(2)}, u32[]{:S(2)}) collective-permute-start(f32[32,128]{1,0:T(8,128)S(1)} %gram.1), channel_id=1, source_target_pairs={{0,4},{2,6},{4,0},{6,2},{8,12},{10,14},{12,8},{14,10},{16,20},{18,... | collective-permute-start | bytes 49160 | tf_op jit(solution)/shard_map/ppermute | solution.py:372
  22.0 15.3 %collective-permute-start.17 = (bf16[64,2048]{1,0:T(8,128)(2,1)S(1)}, bf16[64,2048]{1,0:T(8,128)(2,1)S(1)}, u32[]{:S(2)}, u32[]{:S(2)}) collective-permute-start(bf16[64,2048]{1,0:T(8,128)(2,1)S(1)} %pad_maximum_fusion.2.refs_0_), channel_id=1, source_target_pairs={{0,2},{2,0},{4,6},{6,4},{8,10},{10,8},{12,14},{14,12},{16,18},{18,... | collective-permute-start | bytes 786440 | tf_op jit(solution)/shard_map/ppermute | solution.py:369
  22.1 4.8 %collective-permute-start.10 = (f32[32,128]{1,0:T(8,128)S(1)}, f32[32,128]{1,0:T(8,128)S(1)}, u32[]{:S(2)}, u32[]{:S(2)}) collective-permute-start(f32[32,128]{1,0:T(8,128)S(1)} %gram.1), channel_id=1, source_target_pairs={{0,5},{1,4},{2,7},{3,6},{4,1},{5,0},{6,3},{7,2},{8,13},{9,12},{10,... | collective-permute-start | bytes 49160 | tf_op jit(solution)/shard_map/ppermute | solution.py:382
  22.7 3.8 %collective-permute-start.5 = (f32[32,128]{1,0:T(8,128)S(1)}, f32[32,128]{1,0:T(8,128)S(1)}, u32[]{:S(2)}, u32[]{:S(2)}) collective-permute-start(f32[32,128]{1,0:T(8,128)S(1)} %gram.1), channel_id=1, source_target_pairs={{0,1},{1,0},{2,3},{3,2},{4,5},{5,4},{6,7},{7,6},{8,9},{9,8},{10,11... | collective-permute-start | bytes 49160 | tf_op jit(solution)/shard_map/ppermute | solution.py:378
  24.3 9.9 %collective-permute-start.12 = (bf16[80,2048]{1,0:T(8,128)(2,1)S(1)}, bf16[80,2048]{1,0:T(8,128)(2,1)S(1)}, u32[]{:S(2)}, u32[]{:S(2)}) collective-permute-start(bf16[80,2048]{1,0:T(8,128)(2,1)S(1)} %pad_maximum_fusion), channel_id=1, source_target_pairs={{0,4},{2,6},{4,0},{6,2},{8,12},{10,14},{12,8},{14,10},{16,20},{18,... | collective-permute-start | bytes 983048 | tf_op jit(solution)/shard_map/ppermute | solution.py:372
  26.9 5.8 %collective-permute-start.15 = (f32[64,128]{1,0:T(8,128)S(1)}, f32[64,128]{1,0:T(8,128)S(1)}, u32[]{:S(2)}, u32[]{:S(2)}) collective-permute-start(f32[64,128]{1,0:T(8,128)S(1)} %pad_maximum_fusion.5), channel_id=1, source_target_pairs={{0,24},{2,26},{4,28},{6,30},{8,16},{10,18},{12,20},{14,22},{16,8},... | collective-permute-start | bytes 98312 | tf_op jit(solution)/shard_map/ppermute | solution.py:375
  29.4 4.8 %collective-permute-start.14 = (f32[64,128]{1,0:T(8,128)S(1)}, f32[64,128]{1,0:T(8,128)S(1)}, u32[]{:S(2)}, u32[]{:S(2)}) collective-permute-start(f32[64,128]{1,0:T(8,128)S(1)} %pad_maximum_fusion.5), channel_id=1, source_target_pairs={{0,16},{2,18},{4,20},{6,22},{8,24},{10,26},{12,28},{14,30},{16,0},... | collective-permute-start | bytes 98312 | tf_op jit(solution)/shard_map/ppermute | solution.py:375
  29.6 4.6 %collective-permute-start.13 = (f32[64,128]{1,0:T(8,128)S(1)}, f32[64,128]{1,0:T(8,128)S(1)}, u32[]{:S(2)}, u32[]{:S(2)}) collective-permute-start(f32[64,128]{1,0:T(8,128)S(1)} %pad_maximum_fusion.5), channel_id=1, source_target_pairs={{0,8},{2,10},{4,12},{6,14},{8,0},{10,2},{12,4},{14,6},{16,24},{18,... | collective-permute-start | bytes 98312 | tf_op jit(solution)/shard_map/ppermute | solution.py:375
  32.7 4.7 %collective-permute-start.19 = (bf16[48,2048]{1,0:T(8,128)(2,1)S(1)}, bf16[48,2048]{1,0:T(8,128)(2,1)S(1)}, u32[]{:S(2)}, u32[]{:S(2)}) collective-permute-start(bf16[48,2048]{1,0:T(8,128)(2,1)S(1)} %collective-permute-done.8.refs_4_), channel_id=1, source_target_pairs={{0,2},{2,0},{4,6},{6,4},{8,10},{10,8},{12,14},{14,12},{16,18},{18,... | collective-permute-start | bytes 589832 | tf_op jit(solution)/shard_map/ppermute | solution.py:369
  34.2 3.2 %collective-permute-start.18 = (bf16[64,2048]{1,0:T(8,128)(2,1)S(1)}, bf16[64,2048]{1,0:T(8,128)(2,1)S(1)}, u32[]{:S(2)}, u32[]{:S(2)}) collective-permute-start(bf16[64,2048]{1,0:T(8,128)(2,1)S(1)} %pad_maximum_fusion.3.refs_2_), channel_id=1, source_target_pairs={{0,2},{2,0},{4,6},{6,4},{8,10},{10,8},{12,14},{14,12},{16,18},{18,... | collective-permute-start | bytes 786440 | tf_op jit(solution)/shard_map/ppermute | solution.py:369
  34.2 3.2 %collective-permute-start.20 = (bf16[80,2048]{1,0:T(8,128)(2,1)S(1)}, bf16[80,2048]{1,0:T(8,128)(2,1)S(1)}, u32[]{:S(2)}, u32[]{:S(2)}) collective-permute-start(bf16[80,2048]{1,0:T(8,128)(2,1)S(1)} %collective-permute-done.12.refs_6_), channel_id=1, source_target_pairs={{0,2},{2,0},{4,6},{6,4},{8,10},{10,8},{12,14},{14,12},{16,18},{18,... | collective-permute-start | bytes 983048 | tf_op jit(solution)/shard_map/ppermute | solution.py:369
  34.7 1.6 %collective-permute-start.16 = (f32[256,128]{1,0:T(8,128)S(1)}, f32[256,128]{1,0:T(8,128)S(1)}, u32[]{:S(2)}, u32[]{:S(2)}) collective-permute-start(f32[256,128]{1,0:T(8,128)S(1)} %constant_dynamic-update-slice_fusion.mine), channel_id=1, source_target_pairs={{0,2},{2,0},{4,6},{6,4},{8,10},{10,8},{12,14},{14,12},{16,18},{18,... | collective-permute-start | bytes 393224 | tf_op jit(solution)/shard_map/ppermute | solution.py:369

commit v6 on v5

--- a/solution.py
+++ b/solution.py
@@ -103,15 +103,31 @@
 
 def split_kernel(offsets_in, noise_in, noise_out, offsets, noise, sems):
     small = pltpu.make_async_copy(offsets_in, offsets, sems.at[0])
-    load = pltpu.make_async_copy(noise_in, noise, sems.at[1])
     small.start()
-    load.start()
+    clips, values = noise.shape
+    cut = values // 2
+    pieces = 4
+    step = cut // pieces
+    loads = []
+    for k in range(pieces):
+        for h in range(2):
+            here = (slice(None), pl.ds(h * cut + k * step, step))
+            loads.append(pltpu.make_async_copy(noise_in.at[here], noise.at[here], sems.at[1 + 2 * k + h]))
+            loads[-1].start()
     val = lax.axis_index("val")
-    cut = noise.shape[1] // 2
     small.wait()
-    load.wait()
-    warp_frame(offsets, noise, val, noise_out.at[:, :cut])
-    warp_frame(offsets, noise, 1 - val, noise_out.at[:, cut:])
+    lane = lax.broadcasted_iota(jnp.int32, (clips, S), 1)
+    low = lane < FRAME
+    sources = [lane_sources(offsets, f + lane * 0, lane % FRAME, clips) for f in (val, 1 - val)]
+    for k in range(pieces):
+        loads[2 * k].wait()
+        loads[2 * k + 1].wait()
+        for at in range(k * step, (k + 1) * step, S):
+            near, far = slice(at, at + S), slice(cut + at, cut + at + S)
+            a, b = noise[:, near].astype(F32), noise[:, far].astype(F32)
+            for source, place in zip(sources, (near, far)):
+                moved = jnp.where(low, gather_lanes(a, source), gather_lanes(b, source))
+                noise_out[:, place] = moved.astype(BF16)
 
 
 def in_hbm(x):
@@ -126,7 +142,7 @@
         in_specs=[HBM] * 2,
         out_specs=VMEM,
         scratch_shapes=[pltpu.VMEM(x.shape, x.dtype) for x in inputs]
-        + [pltpu.SemaphoreType.DMA((2,))],
+        + [pltpu.SemaphoreType.DMA((9,))],
         compiler_params=params(),
         name="split",
     )(*map(in_hbm, inputs))
@@ -169,7 +185,7 @@
             pltpu.SemaphoreType.DMA((3,)),
         ],
         compiler_params=params(),
-        cost_estimate=cost(2),
+        cost_estimate=cost(1),
         name="stage",
     )(*map(in_hbm, (times, embed, latents)))
 
@@ -411,12 +427,12 @@
     got, lat_got = below(got_own[:clips], got_mid, got_last), got_own[clips:]
     far_rest = across(below(keep[3], got))
     pair = below(part + got_v, got_x + got_b)
-    rows = [along(pair, k) for k in (1, 2, 3)]
+    rows = [along(pair, k) for k in (2, 1, 3)]
     far_rest, *rows = lax.optimization_barrier([far_rest] + rows)
     mine = below(pair, *rows)
     line = below(*keep)
     beside_core = [core(x) for x in (line, got, far)]
-    other = core(mine)
+    other, *beside_core = lax.optimization_barrier([core(mine)] + beside_core)
     weights = plan(mine, other, clips)
     parts = [line, beside_core[0], got, beside_core[1]]
     parts += [far, beside_core[2], far_rest, core(far_rest)]

time: 42.5 us -> 42.3 us (level)
  transfers between devices with their start and end apart: 21 -> 21, of which waited for: 9 -> 10; matrix products, arithmetic and copies ran while one was open for 0% -> 0% of each run, Pallas kernels for 7% -> 7%
where the time goes in v6:
time: 42.3 us; the launch traced here: 42.1 us
  starting transfers between devices  24.3 us (57%)
  Pallas kernels  9.05 us (21%)
  waiting for transfers between devices  8.43 us (20%)
    ppermute x6, starting transfers between devices, along(): return lax.ppermute(x, 'clip', flip(n, 4 * k))  10.6 us
    ppermute x4, starting transfers between devices, other_val(): return lax.ppermute(x, 'val', [(0, 1), (1, 0)])  6.25 us
    ppermute x4, starting transfers between devices, across(): return lax.ppermute(x, 'clip', flip(n, 2))  6.15 us
    ppermute x6, waiting for transfers between devices, along(): return lax.ppermute(x, 'clip', flip(n, 4 * k))  6.02 us
    pallas_call x1, Pallas kernels, finish(): pl.pallas_call(functools.partial(finish_kernel, clips, block, layout), ou...  4.92 us
    pallas_call x1, Pallas kernels, split_frames(): pl.pallas_call(split_kernel, out_shape=jax.ShapeDtypeStruct(noise.shape,...  1.32 us
    ppermute x6, waiting for transfers between devices, core(): return lax.ppermute(x, 'clip', flip(n, 1))  1.22 us
    pallas_call x1, Pallas kernels, stage(): pl.pallas_call(stage_kernel, out_shape=[jax.ShapeDtypeStruct(embed.shape,...  1.19 us
  transfers between devices with their start and end apart: 21, of which 10 were waited for; matrix products, arithmetic and copies ran while one was open for 0% of the time, Pallas kernels for 7%

profile of v6, /device:TPU:0, one launch (start us, length us, event | category | flops | bytes accessed | tf_op | source)
XLA Modules:
  0.0 42.1 jit_solution(6761063443746355766)
XLA Ops:
  0.0 1.3 %split.1.refs_0_ = bf16[16,4096]{1,0:T(8,128)(2,1)S(1)} custom-call(s32[4,16]{1,0:T(4,128)} %bitcast.4, bf16[16,4096]{1,0:T(8,128)(2,1)} %noise_in.1), custom_call_target="tpu_custom_call" | custom-call | tf_op jit(solution)/shard_map/split/pallas_call | solution.py:139
  1.3 3.1 %collective-permute-start.3 = (bf16[16,4096]{1,0:T(8,128)(2,1)S(1)}, bf16[16,4096]{1,0:T(8,128)(2,1)S(1)}, u32[]{:S(2)}, u32[]{:S(2)}) collective-permute-start(bf16[16,4096]{1,0:T(8,128)(2,1)S(1)} %split.1.refs_0_), channel_id=1, source_target_pairs={{0,8},{2,10},{4,12},{6,14},{8,0},{10,2},{12,4},{14,6},{16,24},{18,... | collective-permute-start | bytes 393224 | tf_op jit(solution)/shard_map/ppermute | solution.py:391
  4.4 2.6 %collective-permute-start.1 = (bf16[16,4096]{1,0:T(8,128)(2,1)S(1)}, bf16[16,4096]{1,0:T(8,128)(2,1)S(1)}, u32[]{:S(2)}, u32[]{:S(2)}) collective-permute-start(bf16[16,4096]{1,0:T(8,128)(2,1)S(1)} %split.1.refs_0_), channel_id=1, source_target_pairs={{0,16},{2,18},{4,20},{6,22},{8,24},{10,26},{12,28},{14,30},{16,0},... | collective-permute-start | bytes 393224 | tf_op jit(solution)/shard_map/ppermute | solution.py:391
  7.0 1.2 %stage.1 = (bf16[64,5120]{1,0:T(8,128)(2,1)S(1)}, f32[16,128]{1,0:T(8,128)S(1)}, bf16[16,4096]{1,0:T(8,128)(2,1)S(1)}) custom-call(f32[16]{0:T(128)} %times_in, bf16[64,5120]{1,0:T(8,128)(2,1)} %embed, bf16[16,4096]{1,0:T(8,128)(2,1)} %latents_in), custom_call_target="tpu_custom_call" | custom-call | bytes 3500000 | tf_op jit(solution)/shard_map/stage/pallas_call | solution.py:173
  8.2 1.6 %collective-permute-start = (bf16[16,4096]{1,0:T(8,128)(2,1)S(1)}, bf16[16,4096]{1,0:T(8,128)(2,1)S(1)}, u32[]{:S(2)}, u32[]{:S(2)}) collective-permute-start(bf16[16,4096]{1,0:T(8,128)(2,1)S(1)} %get-tuple-element.34.lat.lat_keep), channel_id=1, source_target_pairs={{0,4},{2,6},{4,0},{6,2},{8,12},{10,14},{12,8},{14,10},{16,20},{18,... | collective-permute-start | bytes 393224 | tf_op jit(solution)/shard_map/ppermute | solution.py:388
  9.8 1.6 %collective-permute-start.6 = (bf16[32,2048]{1,0:T(8,128)(2,1)S(1)}, bf16[32,2048]{1,0:T(8,128)(2,1)S(1)}, u32[]{:S(2)}, u32[]{:S(2)}) collective-permute-start(bf16[32,2048]{1,0:T(8,128)(2,1)S(1)} %pad_maximum_fusion.4), channel_id=1, source_target_pairs={{0,1},{1,0},{2,3},{3,2},{4,5},{5,4},{6,7},{7,6},{8,9},{9,8},{10,11... | collective-permute-start | bytes 393224 | tf_op jit(solution)/shard_map/ppermute | solution.py:394
  11.4 1.7 %collective-permute-done.1.refs_2_ = bf16[16,4096]{1,0:T(8,128)(2,1)S(1)} collective-permute-done((bf16[16,4096]{1,0:T(8,128)(2,1)S(1)}, bf16[16,4096]{1,0:T(8,128)(2,1)S(1)}, u32[]{:S(2)}, u32[]{:S(2)}) %collective-permute-start.1) | collective-permute-done | bytes 131104 | tf_op jit(solution)/shard_map/ppermute | solution.py:391
  13.8 1.6 %collective-permute-start.7 = (bf16[32,2048]{1,0:T(8,128)(2,1)S(1)}, bf16[32,2048]{1,0:T(8,128)(2,1)S(1)}, u32[]{:S(2)}, u32[]{:S(2)}) collective-permute-start(bf16[32,2048]{1,0:T(8,128)(2,1)S(1)} %get-tuple-element.38), channel_id=1, source_target_pairs={{0,1},{1,0},{2,3},{3,2},{4,5},{5,4},{6,7},{7,6},{8,9},{9,8},{10,11... | collective-permute-start | bytes 393224 | tf_op jit(solution)/shard_map/ppermute | solution.py:394
  15.4 1.5 %collective-permute-start.8 = (bf16[48,2048]{1,0:T(8,128)(2,1)S(1)}, bf16[48,2048]{1,0:T(8,128)(2,1)S(1)}, u32[]{:S(2)}, u32[]{:S(2)}) collective-permute-start(bf16[48,2048]{1,0:T(8,128)(2,1)S(1)} %get-tuple-element.39), channel_id=1, source_target_pairs={{0,4},{2,6},{4,0},{6,2},{8,12},{10,14},{12,8},{14,10},{16,20},{18,... | collective-permute-start | bytes 589832 | tf_op jit(solution)/shard_map/ppermute | solution.py:388
  16.9 1.3 %collective-permute-done.4.refs_3_ = bf16[16,4096]{1,0:T(8,128)(2,1)S(1)} collective-permute-done((bf16[16,4096]{1,0:T(8,128)(2,1)S(1)}, bf16[16,4096]{1,0:T(8,128)(2,1)S(1)}, u32[]{:S(2)}, u32[]{:S(2)}) %collective-permute-start.4) | collective-permute-done | bytes 131104 | tf_op jit(solution)/shard_map/ppermute | solution.py:391
  18.2 1.6 %collective-permute-start.11 = (bf16[16,2048]{1,0:T(8,128)(2,1)S(1)}, bf16[16,2048]{1,0:T(8,128)(2,1)S(1)}, u32[]{:S(2)}, u32[]{:S(2)}) collective-permute-start(bf16[16,2048]{1,0:T(8,128)(2,1)S(1)} %get-tuple-element.60), channel_id=1, source_target_pairs={{0,1},{1,0},{2,3},{3,2},{4,5},{5,4},{6,7},{7,6},{8,9},{9,8},{10,11... | collective-permute-start | bytes 196616 | tf_op jit(solution)/shard_map/ppermute | solution.py:394
  19.8 0.6 %gram.1 = f32[32,128]{1,0:T(8,128)S(1)} custom-call(bf16[16,4096]{1,0:T(8,128)(2,1)S(1)} %get-tuple-element.34.lat.lat_keep, bf16[16,4096]{1,0:T(8,128)(2,1)S(1)} %collective-permute-done.lat_far, bf16[32,4096]{1,0:T(8,128)(2,1)S(1)} %collective-permute-done.2.lat_core, bf16[16,4096]{1,0:T(8,128)(2,1)S(1)} %split.1.refs_0_, ...), custom_call_target="tpu_custom_call" | custom-call | bytes 17500000 | tf_op jit(solution)/shard_map/gram/pallas_call | solution.py:227
  20.4 1.5 %collective-permute-start.9 = (f32[32,128]{1,0:T(8,128)S(1)}, f32[32,128]{1,0:T(8,128)S(1)}, u32[]{:S(2)}, u32[]{:S(2)}) collective-permute-start(f32[32,128]{1,0:T(8,128)S(1)} %gram.1), channel_id=1, source_target_pairs={{0,4},{2,6},{4,0},{6,2},{8,12},{10,14},{12,8},{14,10},{16,20},{18,... | collective-permute-start | bytes 49160 | tf_op jit(solution)/shard_map/ppermute | solution.py:388
  22.6 1.5 %collective-permute-start.5 = (f32[32,128]{1,0:T(8,128)S(1)}, f32[32,128]{1,0:T(8,128)S(1)}, u32[]{:S(2)}, u32[]{:S(2)}) collective-permute-start(f32[32,128]{1,0:T(8,128)S(1)} %gram.1), channel_id=1, source_target_pairs={{0,1},{1,0},{2,3},{3,2},{4,5},{5,4},{6,7},{7,6},{8,9},{9,8},{10,11... | collective-permute-start | bytes 49160 | tf_op jit(solution)/shard_map/ppermute | solution.py:394
  24.3 1.6 %collective-permute-start.12 = (bf16[80,2048]{1,0:T(8,128)(2,1)S(1)}, bf16[80,2048]{1,0:T(8,128)(2,1)S(1)}, u32[]{:S(2)}, u32[]{:S(2)}) collective-permute-start(bf16[80,2048]{1,0:T(8,128)(2,1)S(1)} %pad_maximum_fusion), channel_id=1, source_target_pairs={{0,4},{2,6},{4,0},{6,2},{8,12},{10,14},{12,8},{14,10},{16,20},{18,... | collective-permute-start | bytes 983048 | tf_op jit(solution)/shard_map/ppermute | solution.py:388
  25.8 0.6 %collective-permute-done.5 = f32[32,128]{1,0:T(8,128)S(1)} collective-permute-done((f32[32,128]{1,0:T(8,128)S(1)}, f32[32,128]{1,0:T(8,128)S(1)}, u32[]{:S(2)}, u32[]{:S(2)}) %collective-permute-start.5) | collective-permute-done | bytes 16416 | tf_op jit(solution)/shard_map/ppermute | solution.py:394
  26.9 2.5 %collective-permute-start.15 = (f32[64,128]{1,0:T(8,128)S(1)}, f32[64,128]{1,0:T(8,128)S(1)}, u32[]{:S(2)}, u32[]{:S(2)}) collective-permute-start(f32[64,128]{1,0:T(8,128)S(1)} %pad_maximum_fusion.5), channel_id=1, source_target_pairs={{0,24},{2,26},{4,28},{6,30},{8,16},{10,18},{12,20},{14,22},{16,8},... | collective-permute-start | bytes 98312 | tf_op jit(solution)/shard_map/ppermute | solution.py:391
  29.5 1.8 %collective-permute-start.13 = (f32[64,128]{1,0:T(8,128)S(1)}, f32[64,128]{1,0:T(8,128)S(1)}, u32[]{:S(2)}, u32[]{:S(2)}) collective-permute-start(f32[64,128]{1,0:T(8,128)S(1)} %pad_maximum_fusion.5), channel_id=1, source_target_pairs={{0,16},{2,18},{4,20},{6,22},{8,24},{10,26},{12,28},{14,30},{16,0},... | collective-permute-start | bytes 98312 | tf_op jit(solution)/shard_map/ppermute | solution.py:391
  31.3 1.3 %collective-permute-done.15 = f32[64,128]{1,0:T(8,128)S(1)} collective-permute-done((f32[64,128]{1,0:T(8,128)S(1)}, f32[64,128]{1,0:T(8,128)S(1)}, u32[]{:S(2)}, u32[]{:S(2)}) %collective-permute-start.15) | collective-permute-done | bytes 32800 | tf_op jit(solution)/shard_map/ppermute | solution.py:391
  32.6 0.6 %collective-permute-done.14 = f32[64,128]{1,0:T(8,128)S(1)} collective-permute-done((f32[64,128]{1,0:T(8,128)S(1)}, f32[64,128]{1,0:T(8,128)S(1)}, u32[]{:S(2)}, u32[]{:S(2)}) %collective-permute-start.14) | collective-permute-done | bytes 32800 | tf_op jit(solution)/shard_map/ppermute | solution.py:391
  33.2 1.1 %collective-permute-done.13 = f32[64,128]{1,0:T(8,128)S(1)} collective-permute-done((f32[64,128]{1,0:T(8,128)S(1)}, f32[64,128]{1,0:T(8,128)S(1)}, u32[]{:S(2)}, u32[]{:S(2)}) %collective-permute-start.13) | collective-permute-done | bytes 32800 | tf_op jit(solution)/shard_map/ppermute | solution.py:391
  35.0 1.2 %collective-permute-done.16.other = f32[256,128]{1,0:T(8,128)S(1)} collective-permute-done((f32[256,128]{1,0:T(8,128)S(1)}, f32[256,128]{1,0:T(8,128)S(1)}, u32[]{:S(2)}, u32[]{:S(2)}) %collective-permute-start.16) | collective-permute-done | bytes 131104 | tf_op jit(solution)/shard_map/ppermute | solution.py:385
  36.2 1.0 %plan.1.weights = bf16[16,256]{1,0:T(8,128)(2,1)S(1)} custom-call(f32[256,128]{1,0:T(8,128)S(1)} %constant_dynamic-update-slice_fusion.mine, f32[256,128]{1,0:T(8,128)S(1)} %collective-permute-done.16.other), custom_call_target="tpu_custom_call" | custom-call | tf_op jit(solution)/shard_map/plan/pallas_call | solution.py:280
  37.2 4.9 %finish.1 = bf16[1024,5120]{1,0:T(8,128)(2,1)} custom-call(f32[16,128]{1,0:T(8,128)S(1)} %get-tuple-element.32.column, bf16[16,256]{1,0:T(8,128)(2,1)S(1)} %plan.1.weights, bf16[16,4096]{1,0:T(8,128)(2,1)S(1)} %get-tuple-element.34.lat.lat_keep, bf16[16,2048]{1,0:T(8,128)(2,1)S(1)} %get-tuple-element.57.lat_got, ...), custom_call_target="tpu_custom_call" | custom-call | tf_op jit(solution)/shard_map/finish/pallas_call | solution.py:338
  (42 shorter events, 2.7 us)
Async XLA Ops:
  1.3 12.5 %collective-permute-start.3 = (bf16[16,4096]{1,0:T(8,128)(2,1)S(1)}, bf16[16,4096]{1,0:T(8,128)(2,1)S(1)}, u32[]{:S(2)}, u32[]{:S(2)}) collective-permute-start(bf16[16,4096]{1,0:T(8,128)(2,1)S(1)} %split.1.refs_0_), channel_id=1, source_target_pairs={{0,8},{2,10},{4,12},{6,14},{8,0},{10,2},{12,4},{14,6},{16,24},{18,... | collective-permute-start | bytes 393224 | tf_op jit(solution)/shard_map/ppermute | solution.py:391
  4.4 8.7 %collective-permute-start.1 = (bf16[16,4096]{1,0:T(8,128)(2,1)S(1)}, bf16[16,4096]{1,0:T(8,128)(2,1)S(1)}, u32[]{:S(2)}, u32[]{:S(2)}) collective-permute-start(bf16[16,4096]{1,0:T(8,128)(2,1)S(1)} %split.1.refs_0_), channel_id=1, source_target_pairs={{0,16},{2,18},{4,20},{6,22},{8,24},{10,26},{12,28},{14,30},{16,0},... | collective-permute-start | bytes 393224 | tf_op jit(solution)/shard_map/ppermute | solution.py:391
  8.2 5.0 %collective-permute-start = (bf16[16,4096]{1,0:T(8,128)(2,1)S(1)}, bf16[16,4096]{1,0:T(8,128)(2,1)S(1)}, u32[]{:S(2)}, u32[]{:S(2)}) collective-permute-start(bf16[16,4096]{1,0:T(8,128)(2,1)S(1)} %get-tuple-element.34.lat.lat_keep), channel_id=1, source_target_pairs={{0,4},{2,6},{4,0},{6,2},{8,12},{10,14},{12,8},{14,10},{16,20},{18,... | collective-permute-start | bytes 393224 | tf_op jit(solution)/shard_map/ppermute | solution.py:388
  9.8 12.2 %collective-permute-start.6 = (bf16[32,2048]{1,0:T(8,128)(2,1)S(1)}, bf16[32,2048]{1,0:T(8,128)(2,1)S(1)}, u32[]{:S(2)}, u32[]{:S(2)}) collective-permute-start(bf16[32,2048]{1,0:T(8,128)(2,1)S(1)} %pad_maximum_fusion.4), channel_id=1, source_target_pairs={{0,1},{1,0},{2,3},{3,2},{4,5},{5,4},{6,7},{7,6},{8,9},{9,8},{10,11... | collective-permute-start | bytes 393224 | tf_op jit(solution)/shard_map/ppermute | solution.py:394
  13.2 5.0 %collective-permute-start.4 = (bf16[16,4096]{1,0:T(8,128)(2,1)S(1)}, bf16[16,4096]{1,0:T(8,128)(2,1)S(1)}, u32[]{:S(2)}, u32[]{:S(2)}) collective-permute-start(bf16[16,4096]{1,0:T(8,128)(2,1)S(1)} %collective-permute-done.1.refs_2_), channel_id=1, source_target_pairs={{0,8},{2,10},{4,12},{6,14},{8,0},{10,2},{12,4},{14,6},{16,24},{18,... | collective-permute-start | bytes 393224 | tf_op jit(solution)/shard_map/ppermute | solution.py:391
  13.7 6.1 %collective-permute-start.2 = (bf16[32,4096]{1,0:T(8,128)(2,1)S(1)}, bf16[32,4096]{1,0:T(8,128)(2,1)S(1)}, u32[]{:S(2)}, u32[]{:S(2)}) collective-permute-start(bf16[32,4096]{1,0:T(8,128)(2,1)S(1)} %pad_maximum_fusion.1), channel_id=1, source_target_pairs={{0,2},{2,0},{4,6},{6,4},{8,10},{10,8},{12,14},{14,12},{16,18},{18,... | collective-permute-start | bytes 786440 | tf_op jit(solution)/shard_map/ppermute | solution.py:385
  13.8 8.2 %collective-permute-start.7 = (bf16[32,2048]{1,0:T(8,128)(2,1)S(1)}, bf16[32,2048]{1,0:T(8,128)(2,1)S(1)}, u32[]{:S(2)}, u32[]{:S(2)}) collective-permute-start(bf16[32,2048]{1,0:T(8,128)(2,1)S(1)} %get-tuple-element.38), channel_id=1, source_target_pairs={{0,1},{1,0},{2,3},{3,2},{4,5},{5,4},{6,7},{7,6},{8,9},{9,8},{10,11... | collective-permute-start | bytes 393224 | tf_op jit(solution)/shard_map/ppermute | solution.py:394
  15.4 7.2 %collective-permute-start.8 = (bf16[48,2048]{1,0:T(8,128)(2,1)S(1)}, bf16[48,2048]{1,0:T(8,128)(2,1)S(1)}, u32[]{:S(2)}, u32[]{:S(2)}) collective-permute-start(bf16[48,2048]{1,0:T(8,128)(2,1)S(1)} %get-tuple-element.39), channel_id=1, source_target_pairs={{0,4},{2,6},{4,0},{6,2},{8,12},{10,14},{12,8},{14,10},{16,20},{18,... | collective-permute-start | bytes 589832 | tf_op jit(solution)/shard_map/ppermute | solution.py:388
  18.2 6.0 %collective-permute-start.11 = (bf16[16,2048]{1,0:T(8,128)(2,1)S(1)}, bf16[16,2048]{1,0:T(8,128)(2,1)S(1)}, u32[]{:S(2)}, u32[]{:S(2)}) collective-permute-start(bf16[16,2048]{1,0:T(8,128)(2,1)S(1)} %get-tuple-element.60), channel_id=1, source_target_pairs={{0,1},{1,0},{2,3},{3,2},{4,5},{5,4},{6,7},{7,6},{8,9},{9,8},{10,11... | collective-permute-start | bytes 196616 | tf_op jit(solution)/shard_map/ppermute | solution.py:394
  20.4 3.8 %collective-permute-start.9 = (f32[32,128]{1,0:T(8,128)S(1)}, f32[32,128]{1,0:T(8,128)S(1)}, u32[]{:S(2)}, u32[]{:S(2)}) collective-permute-start(f32[32,128]{1,0:T(8,128)S(1)} %gram.1), channel_id=1, source_target_pairs={{0,4},{2,6},{4,0},{6,2},{8,12},{10,14},{12,8},{14,10},{16,20},{18,... | collective-permute-start | bytes 49160 | tf_op jit(solution)/shard_map/ppermute | solution.py:388
  22.0 13.0 %collective-permute-start.17 = (bf16[64,2048]{1,0:T(8,128)(2,1)S(1)}, bf16[64,2048]{1,0:T(8,128)(2,1)S(1)}, u32[]{:S(2)}, u32[]{:S(2)}) collective-permute-start(bf16[64,2048]{1,0:T(8,128)(2,1)S(1)} %pad_maximum_fusion.2.refs_0_), channel_id=1, source_target_pairs={{0,2},{2,0},{4,6},{6,4},{8,10},{10,8},{12,14},{14,12},{16,18},{18,... | collective-permute-start | bytes 786440 | tf_op jit(solution)/shard_map/ppermute | solution.py:385
  22.1 4.8 %collective-permute-start.10 = (f32[32,128]{1,0:T(8,128)S(1)}, f32[32,128]{1,0:T(8,128)S(1)}, u32[]{:S(2)}, u32[]{:S(2)}) collective-permute-start(f32[32,128]{1,0:T(8,128)S(1)} %gram.1), channel_id=1, source_target_pairs={{0,5},{1,4},{2,7},{3,6},{4,1},{5,0},{6,3},{7,2},{8,13},{9,12},{10,... | collective-permute-start | bytes 49160 | tf_op jit(solution)/shard_map/ppermute | solution.py:398
  22.6 3.8 %collective-permute-start.5 = (f32[32,128]{1,0:T(8,128)S(1)}, f32[32,128]{1,0:T(8,128)S(1)}, u32[]{:S(2)}, u32[]{:S(2)}) collective-permute-start(f32[32,128]{1,0:T(8,128)S(1)} %gram.1), channel_id=1, source_target_pairs={{0,1},{1,0},{2,3},{3,2},{4,5},{5,4},{6,7},{7,6},{8,9},{9,8},{10,11... | collective-permute-start | bytes 49160 | tf_op jit(solution)/shard_map/ppermute | solution.py:394
  24.3 10.1 %collective-permute-start.12 = (bf16[80,2048]{1,0:T(8,128)(2,1)S(1)}, bf16[80,2048]{1,0:T(8,128)(2,1)S(1)}, u32[]{:S(2)}, u32[]{:S(2)}) collective-permute-start(bf16[80,2048]{1,0:T(8,128)(2,1)S(1)} %pad_maximum_fusion), channel_id=1, source_target_pairs={{0,4},{2,6},{4,0},{6,2},{8,12},{10,14},{12,8},{14,10},{16,20},{18,... | collective-permute-start | bytes 983048 | tf_op jit(solution)/shard_map/ppermute | solution.py:388
  26.9 5.8 %collective-permute-start.15 = (f32[64,128]{1,0:T(8,128)S(1)}, f32[64,128]{1,0:T(8,128)S(1)}, u32[]{:S(2)}, u32[]{:S(2)}) collective-permute-start(f32[64,128]{1,0:T(8,128)S(1)} %pad_maximum_fusion.5), channel_id=1, source_target_pairs={{0,24},{2,26},{4,28},{6,30},{8,16},{10,18},{12,20},{14,22},{16,8},... | collective-permute-start | bytes 98312 | tf_op jit(solution)/shard_map/ppermute | solution.py:391
  29.3 3.9 %collective-permute-start.14 = (f32[64,128]{1,0:T(8,128)S(1)}, f32[64,128]{1,0:T(8,128)S(1)}, u32[]{:S(2)}, u32[]{:S(2)}) collective-permute-start(f32[64,128]{1,0:T(8,128)S(1)} %pad_maximum_fusion.5), channel_id=1, source_target_pairs={{0,8},{2,10},{4,12},{6,14},{8,0},{10,2},{12,4},{14,6},{16,24},{18,... | collective-permute-start | bytes 98312 | tf_op jit(solution)/shard_map/ppermute | solution.py:391
  29.5 4.8 %collective-permute-start.13 = (f32[64,128]{1,0:T(8,128)S(1)}, f32[64,128]{1,0:T(8,128)S(1)}, u32[]{:S(2)}, u32[]{:S(2)}) collective-permute-start(f32[64,128]{1,0:T(8,128)S(1)} %pad_maximum_fusion.5), channel_id=1, source_target_pairs={{0,16},{2,18},{4,20},{6,22},{8,24},{10,26},{12,28},{14,30},{16,0},... | collective-permute-start | bytes 98312 | tf_op jit(solution)/shard_map/ppermute | solution.py:391
  32.6 2.3 %collective-permute-start.19 = (bf16[48,2048]{1,0:T(8,128)(2,1)S(1)}, bf16[48,2048]{1,0:T(8,128)(2,1)S(1)}, u32[]{:S(2)}, u32[]{:S(2)}) collective-permute-start(bf16[48,2048]{1,0:T(8,128)(2,1)S(1)} %collective-permute-done.8.refs_4_), channel_id=1, source_target_pairs={{0,2},{2,0},{4,6},{6,4},{8,10},{10,8},{12,14},{14,12},{16,18},{18,... | collective-permute-start | bytes 589832 | tf_op jit(solution)/shard_map/ppermute | solution.py:385
  33.2 1.7 %collective-permute-start.18 = (bf16[64,2048]{1,0:T(8,128)(2,1)S(1)}, bf16[64,2048]{1,0:T(8,128)(2,1)S(1)}, u32[]{:S(2)}, u32[]{:S(2)}) collective-permute-start(bf16[64,2048]{1,0:T(8,128)(2,1)S(1)} %pad_maximum_fusion.3.refs_2_), channel_id=1, source_target_pairs={{0,2},{2,0},{4,6},{6,4},{8,10},{10,8},{12,14},{14,12},{16,18},{18,... | collective-permute-start | bytes 786440 | tf_op jit(solution)/shard_map/ppermute | solution.py:385
  34.3 2.8 %collective-permute-start.20 = (bf16[80,2048]{1,0:T(8,128)(2,1)S(1)}, bf16[80,2048]{1,0:T(8,128)(2,1)S(1)}, u32[]{:S(2)}, u32[]{:S(2)}) collective-permute-start(bf16[80,2048]{1,0:T(8,128)(2,1)S(1)} %collective-permute-done.12.refs_6_), channel_id=1, source_target_pairs={{0,2},{2,0},{4,6},{6,4},{8,10},{10,8},{12,14},{14,12},{16,18},{18,... | collective-permute-start | bytes 983048 | tf_op jit(solution)/shard_map/ppermute | solution.py:385
  34.4 1.8 %collective-permute-start.16 = (f32[256,128]{1,0:T(8,128)S(1)}, f32[256,128]{1,0:T(8,128)S(1)}, u32[]{:S(2)}, u32[]{:S(2)}) collective-permute-start(f32[256,128]{1,0:T(8,128)S(1)} %constant_dynamic-update-slice_fusion.mine), channel_id=1, source_target_pairs={{0,2},{2,0},{4,6},{6,4},{8,10},{10,8},{12,14},{14,12},{16,18},{18,... | collective-permute-start | bytes 393224 | tf_op jit(solution)/shard_map/ppermute | solution.py:385

commit v7 on v6

--- a/solution.py
+++ b/solution.py
@@ -332,7 +332,7 @@
         store(k).wait()
 
 
-def finish(column, weights, lat_keep, lat_got, table, parts, layout, block=FRAME):
+def finish(column, weights, lat_keep, lat_got, table, parts, layout, block=FRAME // 2):
     clips, values = lat_keep.shape
     tokens, width = clips * FRAME, table.shape[1]
     return pl.pallas_call(
@@ -431,11 +431,13 @@
     far_rest, *rows = lax.optimization_barrier([far_rest] + rows)
     mine = below(pair, *rows)
     line = below(*keep)
-    beside_core = [core(x) for x in (line, got, far)]
+    more = below(got, far)
+    beside_core = [core(x) for x in (line, more)]
     other, *beside_core = lax.optimization_barrier([core(mine)] + beside_core)
     weights = plan(mine, other, clips)
-    parts = [line, beside_core[0], got, beside_core[1]]
-    parts += [far, beside_core[2], far_rest, core(far_rest)]
+    r4 = 4 * clips
+    parts = [line, beside_core[0], got, beside_core[1][:r4]]
+    parts += [far, beside_core[1][r4:], far_rest, core(far_rest)]
     first, second = [], []
     for k in (0, 1):
         first += [(k, s * clips) for s in range(4)]

time: 42.3 us -> 42.3 us (level)
    ppermute x6 -> x5, waiting for transfers between devices: 1.22 us -> 1.2 us  [core(): return lax.ppermute(x, 'clip', flip(n, 1))]
  transfers between devices with their start and end apart: 21 -> 20, of which waited for: 10 -> 10; matrix products, arithmetic and copies ran while one was open for 0% -> 1% of each run, Pallas kernels for 7% -> 7%
where the time goes in v7:
time: 42.3 us; the launch traced here: 42.2 us
  starting transfers between devices  24.3 us (57%)
  Pallas kernels  9.09 us (21%)
  waiting for transfers between devices  8.39 us (20%)
    ppermute x6, starting transfers between devices, along(): return lax.ppermute(x, 'clip', flip(n, 4 * k))  10.6 us
    ppermute x4, starting transfers between devices, other_val(): return lax.ppermute(x, 'val', [(0, 1), (1, 0)])  6.25 us
    ppermute x4, starting transfers between devices, across(): return lax.ppermute(x, 'clip', flip(n, 2))  6.15 us
    ppermute x6, waiting for transfers between devices, along(): return lax.ppermute(x, 'clip', flip(n, 4 * k))  6.01 us
    pallas_call x1, Pallas kernels, finish(): pl.pallas_call(functools.partial(finish_kernel, clips, block, layout), ou...  4.95 us
    pallas_call x1, Pallas kernels, split_frames(): pl.pallas_call(split_kernel, out_shape=jax.ShapeDtypeStruct(noise.shape,...  1.32 us
    ppermute x5, waiting for transfers between devices, core(): return lax.ppermute(x, 'clip', flip(n, 1))  1.2 us
    pallas_call x1, Pallas kernels, stage(): pl.pallas_call(stage_kernel, out_shape=[jax.ShapeDtypeStruct(embed.shape,...  1.19 us
  transfers between devices with their start and end apart: 20, of which 10 were waited for; matrix products, arithmetic and copies ran while one was open for 1% of the time, Pallas kernels for 7%

profile of v7, /device:TPU:0, one launch (start us, length us, event | category | flops | bytes accessed | tf_op | source)
XLA Modules:
  0.0 42.2 jit_solution(13775807959547289550)
XLA Ops:
  0.0 1.3 %split.1.refs_0_ = bf16[16,4096]{1,0:T(8,128)(2,1)S(1)} custom-call(s32[4,16]{1,0:T(4,128)} %bitcast.4, bf16[16,4096]{1,0:T(8,128)(2,1)} %noise_in.1), custom_call_target="tpu_custom_call" | custom-call | tf_op jit(solution)/shard_map/split/pallas_call | solution.py:139
  1.3 3.1 %collective-permute-start.3 = (bf16[16,4096]{1,0:T(8,128)(2,1)S(1)}, bf16[16,4096]{1,0:T(8,128)(2,1)S(1)}, u32[]{:S(2)}, u32[]{:S(2)}) collective-permute-start(bf16[16,4096]{1,0:T(8,128)(2,1)S(1)} %split.1.refs_0_), channel_id=1, source_target_pairs={{0,8},{2,10},{4,12},{6,14},{8,0},{10,2},{12,4},{14,6},{16,24},{18,... | collective-permute-start | bytes 393224 | tf_op jit(solution)/shard_map/ppermute | solution.py:391
  4.4 2.6 %collective-permute-start.1 = (bf16[16,4096]{1,0:T(8,128)(2,1)S(1)}, bf16[16,4096]{1,0:T(8,128)(2,1)S(1)}, u32[]{:S(2)}, u32[]{:S(2)}) collective-permute-start(bf16[16,4096]{1,0:T(8,128)(2,1)S(1)} %split.1.refs_0_), channel_id=1, source_target_pairs={{0,16},{2,18},{4,20},{6,22},{8,24},{10,26},{12,28},{14,30},{16,0},... | collective-permute-start | bytes 393224 | tf_op jit(solution)/shard_map/ppermute | solution.py:391
  7.0 1.2 %stage.1 = (bf16[64,5120]{1,0:T(8,128)(2,1)S(1)}, f32[16,128]{1,0:T(8,128)S(1)}, bf16[16,4096]{1,0:T(8,128)(2,1)S(1)}) custom-call(f32[16]{0:T(128)} %times_in, bf16[64,5120]{1,0:T(8,128)(2,1)} %embed, bf16[16,4096]{1,0:T(8,128)(2,1)} %latents_in), custom_call_target="tpu_custom_call" | custom-call | bytes 3500000 | tf_op jit(solution)/shard_map/stage/pallas_call | solution.py:173
  8.2 1.6 %collective-permute-start = (bf16[16,4096]{1,0:T(8,128)(2,1)S(1)}, bf16[16,4096]{1,0:T(8,128)(2,1)S(1)}, u32[]{:S(2)}, u32[]{:S(2)}) collective-permute-start(bf16[16,4096]{1,0:T(8,128)(2,1)S(1)} %get-tuple-element.33.lat.lat_keep), channel_id=1, source_target_pairs={{0,4},{2,6},{4,0},{6,2},{8,12},{10,14},{12,8},{14,10},{16,20},{18,... | collective-permute-start | bytes 393224 | tf_op jit(solution)/shard_map/ppermute | solution.py:388
  9.8 1.6 %collective-permute-start.6 = (bf16[32,2048]{1,0:T(8,128)(2,1)S(1)}, bf16[32,2048]{1,0:T(8,128)(2,1)S(1)}, u32[]{:S(2)}, u32[]{:S(2)}) collective-permute-start(bf16[32,2048]{1,0:T(8,128)(2,1)S(1)} %pad_maximum_fusion.5), channel_id=1, source_target_pairs={{0,1},{1,0},{2,3},{3,2},{4,5},{5,4},{6,7},{7,6},{8,9},{9,8},{10,11... | collective-permute-start | bytes 393224 | tf_op jit(solution)/shard_map/ppermute | solution.py:394
  11.4 1.7 %collective-permute-done.1.refs_2_ = bf16[16,4096]{1,0:T(8,128)(2,1)S(1)} collective-permute-done((bf16[16,4096]{1,0:T(8,128)(2,1)S(1)}, bf16[16,4096]{1,0:T(8,128)(2,1)S(1)}, u32[]{:S(2)}, u32[]{:S(2)}) %collective-permute-start.1) | collective-permute-done | bytes 131104 | tf_op jit(solution)/shard_map/ppermute | solution.py:391
  13.8 1.6 %collective-permute-start.7 = (bf16[32,2048]{1,0:T(8,128)(2,1)S(1)}, bf16[32,2048]{1,0:T(8,128)(2,1)S(1)}, u32[]{:S(2)}, u32[]{:S(2)}) collective-permute-start(bf16[32,2048]{1,0:T(8,128)(2,1)S(1)} %get-tuple-element.37), channel_id=1, source_target_pairs={{0,1},{1,0},{2,3},{3,2},{4,5},{5,4},{6,7},{7,6},{8,9},{9,8},{10,11... | collective-permute-start | bytes 393224 | tf_op jit(solution)/shard_map/ppermute | solution.py:394
  15.4 1.5 %collective-permute-start.8 = (bf16[48,2048]{1,0:T(8,128)(2,1)S(1)}, bf16[48,2048]{1,0:T(8,128)(2,1)S(1)}, u32[]{:S(2)}, u32[]{:S(2)}) collective-permute-start(bf16[48,2048]{1,0:T(8,128)(2,1)S(1)} %get-tuple-element.38), channel_id=1, source_target_pairs={{0,4},{2,6},{4,0},{6,2},{8,12},{10,14},{12,8},{14,10},{16,20},{18,... | collective-permute-start | bytes 589832 | tf_op jit(solution)/shard_map/ppermute | solution.py:388
  16.9 1.3 %collective-permute-done.4.refs_3_ = bf16[16,4096]{1,0:T(8,128)(2,1)S(1)} collective-permute-done((bf16[16,4096]{1,0:T(8,128)(2,1)S(1)}, bf16[16,4096]{1,0:T(8,128)(2,1)S(1)}, u32[]{:S(2)}, u32[]{:S(2)}) %collective-permute-start.4) | collective-permute-done | bytes 131104 | tf_op jit(solution)/shard_map/ppermute | solution.py:391
  18.2 1.6 %collective-permute-start.11 = (bf16[16,2048]{1,0:T(8,128)(2,1)S(1)}, bf16[16,2048]{1,0:T(8,128)(2,1)S(1)}, u32[]{:S(2)}, u32[]{:S(2)}) collective-permute-start(bf16[16,2048]{1,0:T(8,128)(2,1)S(1)} %get-tuple-element.58), channel_id=1, source_target_pairs={{0,1},{1,0},{2,3},{3,2},{4,5},{5,4},{6,7},{7,6},{8,9},{9,8},{10,11... | collective-permute-start | bytes 196616 | tf_op jit(solution)/shard_map/ppermute | solution.py:394
  19.8 0.6 %gram.1 = f32[32,128]{1,0:T(8,128)S(1)} custom-call(bf16[16,4096]{1,0:T(8,128)(2,1)S(1)} %get-tuple-element.33.lat.lat_keep, bf16[16,4096]{1,0:T(8,128)(2,1)S(1)} %collective-permute-done.lat_far, bf16[32,4096]{1,0:T(8,128)(2,1)S(1)} %collective-permute-done.2.lat_core, bf16[16,4096]{1,0:T(8,128)(2,1)S(1)} %split.1.refs_0_, ...), custom_call_target="tpu_custom_call" | custom-call | bytes 17500000 | tf_op jit(solution)/shard_map/gram/pallas_call | solution.py:227
  20.4 1.5 %collective-permute-start.9 = (f32[32,128]{1,0:T(8,128)S(1)}, f32[32,128]{1,0:T(8,128)S(1)}, u32[]{:S(2)}, u32[]{:S(2)}) collective-permute-start(f32[32,128]{1,0:T(8,128)S(1)} %gram.1), channel_id=1, source_target_pairs={{0,4},{2,6},{4,0},{6,2},{8,12},{10,14},{12,8},{14,10},{16,20},{18,... | collective-permute-start | bytes 49160 | tf_op jit(solution)/shard_map/ppermute | solution.py:388
  22.6 1.5 %collective-permute-start.5 = (f32[32,128]{1,0:T(8,128)S(1)}, f32[32,128]{1,0:T(8,128)S(1)}, u32[]{:S(2)}, u32[]{:S(2)}) collective-permute-start(f32[32,128]{1,0:T(8,128)S(1)} %gram.1), channel_id=1, source_target_pairs={{0,1},{1,0},{2,3},{3,2},{4,5},{5,4},{6,7},{7,6},{8,9},{9,8},{10,11... | collective-permute-start | bytes 49160 | tf_op jit(solution)/shard_map/ppermute | solution.py:394
  24.3 1.6 %collective-permute-start.12 = (bf16[80,2048]{1,0:T(8,128)(2,1)S(1)}, bf16[80,2048]{1,0:T(8,128)(2,1)S(1)}, u32[]{:S(2)}, u32[]{:S(2)}) collective-permute-start(bf16[80,2048]{1,0:T(8,128)(2,1)S(1)} %pad_maximum_fusion.1), channel_id=1, source_target_pairs={{0,4},{2,6},{4,0},{6,2},{8,12},{10,14},{12,8},{14,10},{16,20},{18,... | collective-permute-start | bytes 983048 | tf_op jit(solution)/shard_map/ppermute | solution.py:388
  25.8 0.6 %collective-permute-done.5 = f32[32,128]{1,0:T(8,128)S(1)} collective-permute-done((f32[32,128]{1,0:T(8,128)S(1)}, f32[32,128]{1,0:T(8,128)S(1)}, u32[]{:S(2)}, u32[]{:S(2)}) %collective-permute-start.5) | collective-permute-done | bytes 16416 | tf_op jit(solution)/shard_map/ppermute | solution.py:394
  26.9 2.5 %collective-permute-start.15 = (f32[64,128]{1,0:T(8,128)S(1)}, f32[64,128]{1,0:T(8,128)S(1)}, u32[]{:S(2)}, u32[]{:S(2)}) collective-permute-start(f32[64,128]{1,0:T(8,128)S(1)} %pad_maximum_fusion.6), channel_id=1, source_target_pairs={{0,24},{2,26},{4,28},{6,30},{8,16},{10,18},{12,20},{14,22},{16,8},... | collective-permute-start | bytes 98312 | tf_op jit(solution)/shard_map/ppermute | solution.py:391
  29.5 1.8 %collective-permute-start.13 = (f32[64,128]{1,0:T(8,128)S(1)}, f32[64,128]{1,0:T(8,128)S(1)}, u32[]{:S(2)}, u32[]{:S(2)}) collective-permute-start(f32[64,128]{1,0:T(8,128)S(1)} %pad_maximum_fusion.6), channel_id=1, source_target_pairs={{0,16},{2,18},{4,20},{6,22},{8,24},{10,26},{12,28},{14,30},{16,0},... | collective-permute-start | bytes 98312 | tf_op jit(solution)/shard_map/ppermute | solution.py:391
  31.4 1.3 %collective-permute-done.15 = f32[64,128]{1,0:T(8,128)S(1)} collective-permute-done((f32[64,128]{1,0:T(8,128)S(1)}, f32[64,128]{1,0:T(8,128)S(1)}, u32[]{:S(2)}, u32[]{:S(2)}) %collective-permute-start.15) | collective-permute-done | bytes 32800 | tf_op jit(solution)/shard_map/ppermute | solution.py:391
  32.6 0.6 %collective-permute-done.14 = f32[64,128]{1,0:T(8,128)S(1)} collective-permute-done((f32[64,128]{1,0:T(8,128)S(1)}, f32[64,128]{1,0:T(8,128)S(1)}, u32[]{:S(2)}, u32[]{:S(2)}) %collective-permute-start.14) | collective-permute-done | bytes 32800 | tf_op jit(solution)/shard_map/ppermute | solution.py:391
  33.2 1.1 %collective-permute-done.13 = f32[64,128]{1,0:T(8,128)S(1)} collective-permute-done((f32[64,128]{1,0:T(8,128)S(1)}, f32[64,128]{1,0:T(8,128)S(1)}, u32[]{:S(2)}, u32[]{:S(2)}) %collective-permute-start.13) | collective-permute-done | bytes 32800 | tf_op jit(solution)/shard_map/ppermute | solution.py:391
  35.0 1.2 %collective-permute-done.16.other = f32[256,128]{1,0:T(8,128)S(1)} collective-permute-done((f32[256,128]{1,0:T(8,128)S(1)}, f32[256,128]{1,0:T(8,128)S(1)}, u32[]{:S(2)}, u32[]{:S(2)}) %collective-permute-start.16) | collective-permute-done | bytes 131104 | tf_op jit(solution)/shard_map/ppermute | solution.py:385
  36.2 1.0 %plan.1.weights = bf16[16,256]{1,0:T(8,128)(2,1)S(1)} custom-call(f32[256,128]{1,0:T(8,128)S(1)} %constant_dynamic-update-slice_fusion.mine, f32[256,128]{1,0:T(8,128)S(1)} %collective-permute-done.16.other), custom_call_target="tpu_custom_call" | custom-call | tf_op jit(solution)/shard_map/plan/pallas_call | solution.py:280
  37.2 4.9 %finish.1 = bf16[1024,5120]{1,0:T(8,128)(2,1)} custom-call(f32[16,128]{1,0:T(8,128)S(1)} %get-tuple-element.31.column, bf16[16,256]{1,0:T(8,128)(2,1)S(1)} %plan.1.weights, bf16[16,4096]{1,0:T(8,128)(2,1)S(1)} %get-tuple-element.33.lat.lat_keep, bf16[16,2048]{1,0:T(8,128)(2,1)S(1)} %get-tuple-element.55.lat_got, ...), custom_call_target="tpu_custom_call" | custom-call | tf_op jit(solution)/shard_map/finish/pallas_call | solution.py:338
  (43 shorter events, 2.8 us)
Async XLA Ops:
  1.3 12.5 %collective-permute-start.3 = (bf16[16,4096]{1,0:T(8,128)(2,1)S(1)}, bf16[16,4096]{1,0:T(8,128)(2,1)S(1)}, u32[]{:S(2)}, u32[]{:S(2)}) collective-permute-start(bf16[16,4096]{1,0:T(8,128)(2,1)S(1)} %split.1.refs_0_), channel_id=1, source_target_pairs={{0,8},{2,10},{4,12},{6,14},{8,0},{10,2},{12,4},{14,6},{16,24},{18,... | collective-permute-start | bytes 393224 | tf_op jit(solution)/shard_map/ppermute | solution.py:391
  4.4 8.7 %collective-permute-start.1 = (bf16[16,4096]{1,0:T(8,128)(2,1)S(1)}, bf16[16,4096]{1,0:T(8,128)(2,1)S(1)}, u32[]{:S(2)}, u32[]{:S(2)}) collective-permute-start(bf16[16,4096]{1,0:T(8,128)(2,1)S(1)} %split.1.refs_0_), channel_id=1, source_target_pairs={{0,16},{2,18},{4,20},{6,22},{8,24},{10,26},{12,28},{14,30},{16,0},... | collective-permute-start | bytes 393224 | tf_op jit(solution)/shard_map/ppermute | solution.py:391
  8.2 5.0 %collective-permute-start = (bf16[16,4096]{1,0:T(8,128)(2,1)S(1)}, bf16[16,4096]{1,0:T(8,128)(2,1)S(1)}, u32[]{:S(2)}, u32[]{:S(2)}) collective-permute-start(bf16[16,4096]{1,0:T(8,128)(2,1)S(1)} %get-tuple-element.33.lat.lat_keep), channel_id=1, source_target_pairs={{0,4},{2,6},{4,0},{6,2},{8,12},{10,14},{12,8},{14,10},{16,20},{18,... | collective-permute-start | bytes 393224 | tf_op jit(solution)/shard_map/ppermute | solution.py:388
  9.8 12.2 %collective-permute-start.6 = (bf16[32,2048]{1,0:T(8,128)(2,1)S(1)}, bf16[32,2048]{1,0:T(8,128)(2,1)S(1)}, u32[]{:S(2)}, u32[]{:S(2)}) collective-permute-start(bf16[32,2048]{1,0:T(8,128)(2,1)S(1)} %pad_maximum_fusion.5), channel_id=1, source_target_pairs={{0,1},{1,0},{2,3},{3,2},{4,5},{5,4},{6,7},{7,6},{8,9},{9,8},{10,11... | collective-permute-start | bytes 393224 | tf_op jit(solution)/shard_map/ppermute | solution.py:394
  13.2 5.0 %collective-permute-start.4 = (bf16[16,4096]{1,0:T(8,128)(2,1)S(1)}, bf16[16,4096]{1,0:T(8,128)(2,1)S(1)}, u32[]{:S(2)}, u32[]{:S(2)}) collective-permute-start(bf16[16,4096]{1,0:T(8,128)(2,1)S(1)} %collective-permute-done.1.refs_2_), channel_id=1, source_target_pairs={{0,8},{2,10},{4,12},{6,14},{8,0},{10,2},{12,4},{14,6},{16,24},{18,... | collective-permute-start | bytes 393224 | tf_op jit(solution)/shard_map/ppermute | solution.py:391
  13.7 6.1 %collective-permute-start.2 = (bf16[32,4096]{1,0:T(8,128)(2,1)S(1)}, bf16[32,4096]{1,0:T(8,128)(2,1)S(1)}, u32[]{:S(2)}, u32[]{:S(2)}) collective-permute-start(bf16[32,4096]{1,0:T(8,128)(2,1)S(1)} %pad_maximum_fusion.2), channel_id=1, source_target_pairs={{0,2},{2,0},{4,6},{6,4},{8,10},{10,8},{12,14},{14,12},{16,18},{18,... | collective-permute-start | bytes 786440 | tf_op jit(solution)/shard_map/ppermute | solution.py:385
  13.8 8.2 %collective-permute-start.7 = (bf16[32,2048]{1,0:T(8,128)(2,1)S(1)}, bf16[32,2048]{1,0:T(8,128)(2,1)S(1)}, u32[]{:S(2)}, u32[]{:S(2)}) collective-permute-start(bf16[32,2048]{1,0:T(8,128)(2,1)S(1)} %get-tuple-element.37), channel_id=1, source_target_pairs={{0,1},{1,0},{2,3},{3,2},{4,5},{5,4},{6,7},{7,6},{8,9},{9,8},{10,11... | collective-permute-start | bytes 393224 | tf_op jit(solution)/shard_map/ppermute | solution.py:394
  15.4 7.2 %collective-permute-start.8 = (bf16[48,2048]{1,0:T(8,128)(2,1)S(1)}, bf16[48,2048]{1,0:T(8,128)(2,1)S(1)}, u32[]{:S(2)}, u32[]{:S(2)}) collective-permute-start(bf16[48,2048]{1,0:T(8,128)(2,1)S(1)} %get-tuple-element.38), channel_id=1, source_target_pairs={{0,4},{2,6},{4,0},{6,2},{8,12},{10,14},{12,8},{14,10},{16,20},{18,... | collective-permute-start | bytes 589832 | tf_op jit(solution)/shard_map/ppermute | solution.py:388
  18.2 6.0 %collective-permute-start.11 = (bf16[16,2048]{1,0:T(8,128)(2,1)S(1)}, bf16[16,2048]{1,0:T(8,128)(2,1)S(1)}, u32[]{:S(2)}, u32[]{:S(2)}) collective-permute-start(bf16[16,2048]{1,0:T(8,128)(2,1)S(1)} %get-tuple-element.58), channel_id=1, source_target_pairs={{0,1},{1,0},{2,3},{3,2},{4,5},{5,4},{6,7},{7,6},{8,9},{9,8},{10,11... | collective-permute-start | bytes 196616 | tf_op jit(solution)/shard_map/ppermute | solution.py:394
  20.4 3.8 %collective-permute-start.9 = (f32[32,128]{1,0:T(8,128)S(1)}, f32[32,128]{1,0:T(8,128)S(1)}, u32[]{:S(2)}, u32[]{:S(2)}) collective-permute-start(f32[32,128]{1,0:T(8,128)S(1)} %gram.1), channel_id=1, source_target_pairs={{0,4},{2,6},{4,0},{6,2},{8,12},{10,14},{12,8},{14,10},{16,20},{18,... | collective-permute-start | bytes 49160 | tf_op jit(solution)/shard_map/ppermute | solution.py:388
  22.0 13.0 %collective-permute-start.17 = (bf16[64,2048]{1,0:T(8,128)(2,1)S(1)}, bf16[64,2048]{1,0:T(8,128)(2,1)S(1)}, u32[]{:S(2)}, u32[]{:S(2)}) collective-permute-start(bf16[64,2048]{1,0:T(8,128)(2,1)S(1)} %pad_maximum_fusion.3.refs_0_), channel_id=1, source_target_pairs={{0,2},{2,0},{4,6},{6,4},{8,10},{10,8},{12,14},{14,12},{16,18},{18,... | collective-permute-start | bytes 786440 | tf_op jit(solution)/shard_map/ppermute | solution.py:385
  22.1 4.8 %collective-permute-start.10 = (f32[32,128]{1,0:T(8,128)S(1)}, f32[32,128]{1,0:T(8,128)S(1)}, u32[]{:S(2)}, u32[]{:S(2)}) collective-permute-start(f32[32,128]{1,0:T(8,128)S(1)} %gram.1), channel_id=1, source_target_pairs={{0,5},{1,4},{2,7},{3,6},{4,1},{5,0},{6,3},{7,2},{8,13},{9,12},{10,... | collective-permute-start | bytes 49160 | tf_op jit(solution)/shard_map/ppermute | solution.py:398
  22.6 3.8 %collective-permute-start.5 = (f32[32,128]{1,0:T(8,128)S(1)}, f32[32,128]{1,0:T(8,128)S(1)}, u32[]{:S(2)}, u32[]{:S(2)}) collective-permute-start(f32[32,128]{1,0:T(8,128)S(1)} %gram.1), channel_id=1, source_target_pairs={{0,1},{1,0},{2,3},{3,2},{4,5},{5,4},{6,7},{7,6},{8,9},{9,8},{10,11... | collective-permute-start | bytes 49160 | tf_op jit(solution)/shard_map/ppermute | solution.py:394
  24.3 10.1 %collective-permute-start.12 = (bf16[80,2048]{1,0:T(8,128)(2,1)S(1)}, bf16[80,2048]{1,0:T(8,128)(2,1)S(1)}, u32[]{:S(2)}, u32[]{:S(2)}) collective-permute-start(bf16[80,2048]{1,0:T(8,128)(2,1)S(1)} %pad_maximum_fusion.1), channel_id=1, source_target_pairs={{0,4},{2,6},{4,0},{6,2},{8,12},{10,14},{12,8},{14,10},{16,20},{18,... | collective-permute-start | bytes 983048 | tf_op jit(solution)/shard_map/ppermute | solution.py:388
  26.9 5.8 %collective-permute-start.15 = (f32[64,128]{1,0:T(8,128)S(1)}, f32[64,128]{1,0:T(8,128)S(1)}, u32[]{:S(2)}, u32[]{:S(2)}) collective-permute-start(f32[64,128]{1,0:T(8,128)S(1)} %pad_maximum_fusion.6), channel_id=1, source_target_pairs={{0,24},{2,26},{4,28},{6,30},{8,16},{10,18},{12,20},{14,22},{16,8},... | collective-permute-start | bytes 98312 | tf_op jit(solution)/shard_map/ppermute | solution.py:391
  29.3 3.9 %collective-permute-start.14 = (f32[64,128]{1,0:T(8,128)S(1)}, f32[64,128]{1,0:T(8,128)S(1)}, u32[]{:S(2)}, u32[]{:S(2)}) collective-permute-start(f32[64,128]{1,0:T(8,128)S(1)} %pad_maximum_fusion.6), channel_id=1, source_target_pairs={{0,8},{2,10},{4,12},{6,14},{8,0},{10,2},{12,4},{14,6},{16,24},{18,... | collective-permute-start | bytes 98312 | tf_op jit(solution)/shard_map/ppermute | solution.py:391
  29.5 4.8 %collective-permute-start.13 = (f32[64,128]{1,0:T(8,128)S(1)}, f32[64,128]{1,0:T(8,128)S(1)}, u32[]{:S(2)}, u32[]{:S(2)}) collective-permute-start(f32[64,128]{1,0:T(8,128)S(1)} %pad_maximum_fusion.6), channel_id=1, source_target_pairs={{0,16},{2,18},{4,20},{6,22},{8,24},{10,26},{12,28},{14,30},{16,0},... | collective-permute-start | bytes 98312 | tf_op jit(solution)/shard_map/ppermute | solution.py:391
  32.6 3.5 %collective-permute-start.18 = (bf16[112,2048]{1,0:T(8,128)(2,1)S(1)}, bf16[112,2048]{1,0:T(8,128)(2,1)S(1)}, u32[]{:S(2)}, u32[]{:S(2)}) collective-permute-start(bf16[112,2048]{1,0:T(8,128)(2,1)S(1)} %pad_maximum_fusion), channel_id=1, source_target_pairs={{0,2},{2,0},{4,6},{6,4},{8,10},{10,8},{12,14},{14,12},{16,18},{18,... | collective-permute-start | bytes 1376264 | tf_op jit(solution)/shard_map/ppermute | solution.py:385
  34.3 2.9 %collective-permute-start.19 = (bf16[80,2048]{1,0:T(8,128)(2,1)S(1)}, bf16[80,2048]{1,0:T(8,128)(2,1)S(1)}, u32[]{:S(2)}, u32[]{:S(2)}) collective-permute-start(bf16[80,2048]{1,0:T(8,128)(2,1)S(1)} %collective-permute-done.12.refs_6_), channel_id=1, source_target_pairs={{0,2},{2,0},{4,6},{6,4},{8,10},{10,8},{12,14},{14,12},{16,18},{18,... | collective-permute-start | bytes 983048 | tf_op jit(solution)/shard_map/ppermute | solution.py:385
  34.4 1.8 %collective-permute-start.16 = (f32[256,128]{1,0:T(8,128)S(1)}, f32[256,128]{1,0:T(8,128)S(1)}, u32[]{:S(2)}, u32[]{:S(2)}) collective-permute-start(f32[256,128]{1,0:T(8,128)S(1)} %constant_dynamic-update-slice_fusion.mine), channel_id=1, source_target_pairs={{0,2},{2,0},{4,6},{6,4},{8,10},{10,8},{12,14},{14,12},{16,18},{18,... | collective-permute-start | bytes 393224 | tf_op jit(solution)/shard_map/ppermute | solution.py:385

commit v8 on v6

--- a/solution.py
+++ b/solution.py
@@ -267,7 +267,8 @@
             full[r : r + half, lanes] = jnp.where(low, g, pltpu.roll(h, 64, 1))
             full[r + half : r + 2 * half, lanes] = jnp.where(low, pltpu.roll(g, 64, 1), h)
     share, right = sinkhorn(full[...])
-    full[...] = share
+    column = 4 * clips
+    full[:column, :] = share[:column]
     own = full[pl.ds(pl.multiple_of(b * clips, clips), clips), :]
     weights = softmax_rows(own, right)
     for x in range(2):

time: 42.3 us -> 42.3 us (level)
  no operation moved by 1% of the time
where the time goes in v8:
time: 42.3 us; the launch traced here: 42.1 us
  starting transfers between devices  24.3 us (57%)
  Pallas kernels  9.06 us (21%)
  waiting for transfers between devices  8.43 us (20%)
    ppermute x6, starting transfers between devices, along(): return lax.ppermute(x, 'clip', flip(n, 4 * k))  10.6 us
    ppermute x4, starting transfers between devices, other_val(): return lax.ppermute(x, 'val', [(0, 1), (1, 0)])  6.25 us
    ppermute x4, starting transfers between devices, across(): return lax.ppermute(x, 'clip', flip(n, 2))  6.15 us
    ppermute x6, waiting for transfers between devices, along(): return lax.ppermute(x, 'clip', flip(n, 4 * k))  6.02 us
    pallas_call x1, Pallas kernels, finish(): pl.pallas_call(functools.partial(finish_kernel, clips, block, layout), ou...  4.93 us
    pallas_call x1, Pallas kernels, split_frames(): pl.pallas_call(split_kernel, out_shape=jax.ShapeDtypeStruct(noise.shape,...  1.32 us
    ppermute x6, waiting for transfers between devices, core(): return lax.ppermute(x, 'clip', flip(n, 1))  1.22 us
    pallas_call x1, Pallas kernels, stage(): pl.pallas_call(stage_kernel, out_shape=[jax.ShapeDtypeStruct(embed.shape,...  1.19 us
  transfers between devices with their start and end apart: 21, of which 10 were waited for; matrix products, arithmetic and copies ran while one was open for 0% of the time, Pallas kernels for 7%

profile of v8, /device:TPU:0, one launch (start us, length us, event | category | flops | bytes accessed | tf_op | source)
XLA Modules:
  0.0 42.1 jit_solution(14976177050500321663)
XLA Ops:
  0.0 1.3 %split.1.refs_0_ = bf16[16,4096]{1,0:T(8,128)(2,1)S(1)} custom-call(s32[4,16]{1,0:T(4,128)} %bitcast.4, bf16[16,4096]{1,0:T(8,128)(2,1)} %noise_in.1), custom_call_target="tpu_custom_call" | custom-call | tf_op jit(solution)/shard_map/split/pallas_call | solution.py:139
  1.3 3.1 %collective-permute-start.3 = (bf16[16,4096]{1,0:T(8,128)(2,1)S(1)}, bf16[16,4096]{1,0:T(8,128)(2,1)S(1)}, u32[]{:S(2)}, u32[]{:S(2)}) collective-permute-start(bf16[16,4096]{1,0:T(8,128)(2,1)S(1)} %split.1.refs_0_), channel_id=1, source_target_pairs={{0,8},{2,10},{4,12},{6,14},{8,0},{10,2},{12,4},{14,6},{16,24},{18,... | collective-permute-start | bytes 393224 | tf_op jit(solution)/shard_map/ppermute | solution.py:392
  4.4 2.6 %collective-permute-start.1 = (bf16[16,4096]{1,0:T(8,128)(2,1)S(1)}, bf16[16,4096]{1,0:T(8,128)(2,1)S(1)}, u32[]{:S(2)}, u32[]{:S(2)}) collective-permute-start(bf16[16,4096]{1,0:T(8,128)(2,1)S(1)} %split.1.refs_0_), channel_id=1, source_target_pairs={{0,16},{2,18},{4,20},{6,22},{8,24},{10,26},{12,28},{14,30},{16,0},... | collective-permute-start | bytes 393224 | tf_op jit(solution)/shard_map/ppermute | solution.py:392
  7.0 1.2 %stage.1 = (bf16[64,5120]{1,0:T(8,128)(2,1)S(1)}, f32[16,128]{1,0:T(8,128)S(1)}, bf16[16,4096]{1,0:T(8,128)(2,1)S(1)}) custom-call(f32[16]{0:T(128)} %times_in, bf16[64,5120]{1,0:T(8,128)(2,1)} %embed, bf16[16,4096]{1,0:T(8,128)(2,1)} %latents_in), custom_call_target="tpu_custom_call" | custom-call | bytes 3500000 | tf_op jit(solution)/shard_map/stage/pallas_call | solution.py:173
  8.2 1.6 %collective-permute-start = (bf16[16,4096]{1,0:T(8,128)(2,1)S(1)}, bf16[16,4096]{1,0:T(8,128)(2,1)S(1)}, u32[]{:S(2)}, u32[]{:S(2)}) collective-permute-start(bf16[16,4096]{1,0:T(8,128)(2,1)S(1)} %get-tuple-element.34.lat.lat_keep), channel_id=1, source_target_pairs={{0,4},{2,6},{4,0},{6,2},{8,12},{10,14},{12,8},{14,10},{16,20},{18,... | collective-permute-start | bytes 393224 | tf_op jit(solution)/shard_map/ppermute | solution.py:389
  9.8 1.6 %collective-permute-start.6 = (bf16[32,2048]{1,0:T(8,128)(2,1)S(1)}, bf16[32,2048]{1,0:T(8,128)(2,1)S(1)}, u32[]{:S(2)}, u32[]{:S(2)}) collective-permute-start(bf16[32,2048]{1,0:T(8,128)(2,1)S(1)} %pad_maximum_fusion.4), channel_id=1, source_target_pairs={{0,1},{1,0},{2,3},{3,2},{4,5},{5,4},{6,7},{7,6},{8,9},{9,8},{10,11... | collective-permute-start | bytes 393224 | tf_op jit(solution)/shard_map/ppermute | solution.py:395
  11.4 1.7 %collective-permute-done.1.refs_2_ = bf16[16,4096]{1,0:T(8,128)(2,1)S(1)} collective-permute-done((bf16[16,4096]{1,0:T(8,128)(2,1)S(1)}, bf16[16,4096]{1,0:T(8,128)(2,1)S(1)}, u32[]{:S(2)}, u32[]{:S(2)}) %collective-permute-start.1) | collective-permute-done | bytes 131104 | tf_op jit(solution)/shard_map/ppermute | solution.py:392
  13.8 1.6 %collective-permute-start.7 = (bf16[32,2048]{1,0:T(8,128)(2,1)S(1)}, bf16[32,2048]{1,0:T(8,128)(2,1)S(1)}, u32[]{:S(2)}, u32[]{:S(2)}) collective-permute-start(bf16[32,2048]{1,0:T(8,128)(2,1)S(1)} %get-tuple-element.38), channel_id=1, source_target_pairs={{0,1},{1,0},{2,3},{3,2},{4,5},{5,4},{6,7},{7,6},{8,9},{9,8},{10,11... | collective-permute-start | bytes 393224 | tf_op jit(solution)/shard_map/ppermute | solution.py:395
  15.4 1.5 %collective-permute-start.8 = (bf16[48,2048]{1,0:T(8,128)(2,1)S(1)}, bf16[48,2048]{1,0:T(8,128)(2,1)S(1)}, u32[]{:S(2)}, u32[]{:S(2)}) collective-permute-start(bf16[48,2048]{1,0:T(8,128)(2,1)S(1)} %get-tuple-element.39), channel_id=1, source_target_pairs={{0,4},{2,6},{4,0},{6,2},{8,12},{10,14},{12,8},{14,10},{16,20},{18,... | collective-permute-start | bytes 589832 | tf_op jit(solution)/shard_map/ppermute | solution.py:389
  16.9 1.3 %collective-permute-done.4.refs_3_ = bf16[16,4096]{1,0:T(8,128)(2,1)S(1)} collective-permute-done((bf16[16,4096]{1,0:T(8,128)(2,1)S(1)}, bf16[16,4096]{1,0:T(8,128)(2,1)S(1)}, u32[]{:S(2)}, u32[]{:S(2)}) %collective-permute-start.4) | collective-permute-done | bytes 131104 | tf_op jit(solution)/shard_map/ppermute | solution.py:392
  18.2 1.6 %collective-permute-start.11 = (bf16[16,2048]{1,0:T(8,128)(2,1)S(1)}, bf16[16,2048]{1,0:T(8,128)(2,1)S(1)}, u32[]{:S(2)}, u32[]{:S(2)}) collective-permute-start(bf16[16,2048]{1,0:T(8,128)(2,1)S(1)} %get-tuple-element.60), channel_id=1, source_target_pairs={{0,1},{1,0},{2,3},{3,2},{4,5},{5,4},{6,7},{7,6},{8,9},{9,8},{10,11... | collective-permute-start | bytes 196616 | tf_op jit(solution)/shard_map/ppermute | solution.py:395
  19.8 0.6 %gram.1 = f32[32,128]{1,0:T(8,128)S(1)} custom-call(bf16[16,4096]{1,0:T(8,128)(2,1)S(1)} %get-tuple-element.34.lat.lat_keep, bf16[16,4096]{1,0:T(8,128)(2,1)S(1)} %collective-permute-done.lat_far, bf16[32,4096]{1,0:T(8,128)(2,1)S(1)} %collective-permute-done.2.lat_core, bf16[16,4096]{1,0:T(8,128)(2,1)S(1)} %split.1.refs_0_, ...), custom_call_target="tpu_custom_call" | custom-call | bytes 17500000 | tf_op jit(solution)/shard_map/gram/pallas_call | solution.py:227
  20.4 1.5 %collective-permute-start.9 = (f32[32,128]{1,0:T(8,128)S(1)}, f32[32,128]{1,0:T(8,128)S(1)}, u32[]{:S(2)}, u32[]{:S(2)}) collective-permute-start(f32[32,128]{1,0:T(8,128)S(1)} %gram.1), channel_id=1, source_target_pairs={{0,4},{2,6},{4,0},{6,2},{8,12},{10,14},{12,8},{14,10},{16,20},{18,... | collective-permute-start | bytes 49160 | tf_op jit(solution)/shard_map/ppermute | solution.py:389
  22.6 1.5 %collective-permute-start.5 = (f32[32,128]{1,0:T(8,128)S(1)}, f32[32,128]{1,0:T(8,128)S(1)}, u32[]{:S(2)}, u32[]{:S(2)}) collective-permute-start(f32[32,128]{1,0:T(8,128)S(1)} %gram.1), channel_id=1, source_target_pairs={{0,1},{1,0},{2,3},{3,2},{4,5},{5,4},{6,7},{7,6},{8,9},{9,8},{10,11... | collective-permute-start | bytes 49160 | tf_op jit(solution)/shard_map/ppermute | solution.py:395
  24.3 1.6 %collective-permute-start.12 = (bf16[80,2048]{1,0:T(8,128)(2,1)S(1)}, bf16[80,2048]{1,0:T(8,128)(2,1)S(1)}, u32[]{:S(2)}, u32[]{:S(2)}) collective-permute-start(bf16[80,2048]{1,0:T(8,128)(2,1)S(1)} %pad_maximum_fusion), channel_id=1, source_target_pairs={{0,4},{2,6},{4,0},{6,2},{8,12},{10,14},{12,8},{14,10},{16,20},{18,... | collective-permute-start | bytes 983048 | tf_op jit(solution)/shard_map/ppermute | solution.py:389
  25.8 0.6 %collective-permute-done.5 = f32[32,128]{1,0:T(8,128)S(1)} collective-permute-done((f32[32,128]{1,0:T(8,128)S(1)}, f32[32,128]{1,0:T(8,128)S(1)}, u32[]{:S(2)}, u32[]{:S(2)}) %collective-permute-start.5) | collective-permute-done | bytes 16416 | tf_op jit(solution)/shard_map/ppermute | solution.py:395
  26.9 2.5 %collective-permute-start.15 = (f32[64,128]{1,0:T(8,128)S(1)}, f32[64,128]{1,0:T(8,128)S(1)}, u32[]{:S(2)}, u32[]{:S(2)}) collective-permute-start(f32[64,128]{1,0:T(8,128)S(1)} %pad_maximum_fusion.5), channel_id=1, source_target_pairs={{0,24},{2,26},{4,28},{6,30},{8,16},{10,18},{12,20},{14,22},{16,8},... | collective-permute-start | bytes 98312 | tf_op jit(solution)/shard_map/ppermute | solution.py:392
  29.5 1.8 %collective-permute-start.13 = (f32[64,128]{1,0:T(8,128)S(1)}, f32[64,128]{1,0:T(8,128)S(1)}, u32[]{:S(2)}, u32[]{:S(2)}) collective-permute-start(f32[64,128]{1,0:T(8,128)S(1)} %pad_maximum_fusion.5), channel_id=1, source_target_pairs={{0,16},{2,18},{4,20},{6,22},{8,24},{10,26},{12,28},{14,30},{16,0},... | collective-permute-start | bytes 98312 | tf_op jit(solution)/shard_map/ppermute | solution.py:392
  31.3 1.3 %collective-permute-done.15 = f32[64,128]{1,0:T(8,128)S(1)} collective-permute-done((f32[64,128]{1,0:T(8,128)S(1)}, f32[64,128]{1,0:T(8,128)S(1)}, u32[]{:S(2)}, u32[]{:S(2)}) %collective-permute-start.15) | collective-permute-done | bytes 32800 | tf_op jit(solution)/shard_map/ppermute | solution.py:392
  32.6 0.6 %collective-permute-done.14 = f32[64,128]{1,0:T(8,128)S(1)} collective-permute-done((f32[64,128]{1,0:T(8,128)S(1)}, f32[64,128]{1,0:T(8,128)S(1)}, u32[]{:S(2)}, u32[]{:S(2)}) %collective-permute-start.14) | collective-permute-done | bytes 32800 | tf_op jit(solution)/shard_map/ppermute | solution.py:392
  33.2 1.1 %collective-permute-done.13 = f32[64,128]{1,0:T(8,128)S(1)} collective-permute-done((f32[64,128]{1,0:T(8,128)S(1)}, f32[64,128]{1,0:T(8,128)S(1)}, u32[]{:S(2)}, u32[]{:S(2)}) %collective-permute-start.13) | collective-permute-done | bytes 32800 | tf_op jit(solution)/shard_map/ppermute | solution.py:392
  35.0 1.2 %collective-permute-done.16.other = f32[256,128]{1,0:T(8,128)S(1)} collective-permute-done((f32[256,128]{1,0:T(8,128)S(1)}, f32[256,128]{1,0:T(8,128)S(1)}, u32[]{:S(2)}, u32[]{:S(2)}) %collective-permute-start.16) | collective-permute-done | bytes 131104 | tf_op jit(solution)/shard_map/ppermute | solution.py:386
  36.2 1.0 %plan.1.weights = bf16[16,256]{1,0:T(8,128)(2,1)S(1)} custom-call(f32[256,128]{1,0:T(8,128)S(1)} %constant_dynamic-update-slice_fusion.mine, f32[256,128]{1,0:T(8,128)S(1)} %collective-permute-done.16.other), custom_call_target="tpu_custom_call" | custom-call | tf_op jit(solution)/shard_map/plan/pallas_call | solution.py:281
  37.2 4.9 %finish.1 = bf16[1024,5120]{1,0:T(8,128)(2,1)} custom-call(f32[16,128]{1,0:T(8,128)S(1)} %get-tuple-element.32.column, bf16[16,256]{1,0:T(8,128)(2,1)S(1)} %plan.1.weights, bf16[16,4096]{1,0:T(8,128)(2,1)S(1)} %get-tuple-element.34.lat.lat_keep, bf16[16,2048]{1,0:T(8,128)(2,1)S(1)} %get-tuple-element.57.lat_got, ...), custom_call_target="tpu_custom_call" | custom-call | tf_op jit(solution)/shard_map/finish/pallas_call | solution.py:339
  (42 shorter events, 2.7 us)
Async XLA Ops:
  1.3 12.5 %collective-permute-start.3 = (bf16[16,4096]{1,0:T(8,128)(2,1)S(1)}, bf16[16,4096]{1,0:T(8,128)(2,1)S(1)}, u32[]{:S(2)}, u32[]{:S(2)}) collective-permute-start(bf16[16,4096]{1,0:T(8,128)(2,1)S(1)} %split.1.refs_0_), channel_id=1, source_target_pairs={{0,8},{2,10},{4,12},{6,14},{8,0},{10,2},{12,4},{14,6},{16,24},{18,... | collective-permute-start | bytes 393224 | tf_op jit(solution)/shard_map/ppermute | solution.py:392
  4.4 8.7 %collective-permute-start.1 = (bf16[16,4096]{1,0:T(8,128)(2,1)S(1)}, bf16[16,4096]{1,0:T(8,128)(2,1)S(1)}, u32[]{:S(2)}, u32[]{:S(2)}) collective-permute-start(bf16[16,4096]{1,0:T(8,128)(2,1)S(1)} %split.1.refs_0_), channel_id=1, source_target_pairs={{0,16},{2,18},{4,20},{6,22},{8,24},{10,26},{12,28},{14,30},{16,0},... | collective-permute-start | bytes 393224 | tf_op jit(solution)/shard_map/ppermute | solution.py:392
  8.2 5.0 %collective-permute-start = (bf16[16,4096]{1,0:T(8,128)(2,1)S(1)}, bf16[16,4096]{1,0:T(8,128)(2,1)S(1)}, u32[]{:S(2)}, u32[]{:S(2)}) collective-permute-start(bf16[16,4096]{1,0:T(8,128)(2,1)S(1)} %get-tuple-element.34.lat.lat_keep), channel_id=1, source_target_pairs={{0,4},{2,6},{4,0},{6,2},{8,12},{10,14},{12,8},{14,10},{16,20},{18,... | collective-permute-start | bytes 393224 | tf_op jit(solution)/shard_map/ppermute | solution.py:389
  9.8 12.2 %collective-permute-start.6 = (bf16[32,2048]{1,0:T(8,128)(2,1)S(1)}, bf16[32,2048]{1,0:T(8,128)(2,1)S(1)}, u32[]{:S(2)}, u32[]{:S(2)}) collective-permute-start(bf16[32,2048]{1,0:T(8,128)(2,1)S(1)} %pad_maximum_fusion.4), channel_id=1, source_target_pairs={{0,1},{1,0},{2,3},{3,2},{4,5},{5,4},{6,7},{7,6},{8,9},{9,8},{10,11... | collective-permute-start | bytes 393224 | tf_op jit(solution)/shard_map/ppermute | solution.py:395
  13.2 5.0 %collective-permute-start.4 = (bf16[16,4096]{1,0:T(8,128)(2,1)S(1)}, bf16[16,4096]{1,0:T(8,128)(2,1)S(1)}, u32[]{:S(2)}, u32[]{:S(2)}) collective-permute-start(bf16[16,4096]{1,0:T(8,128)(2,1)S(1)} %collective-permute-done.1.refs_2_), channel_id=1, source_target_pairs={{0,8},{2,10},{4,12},{6,14},{8,0},{10,2},{12,4},{14,6},{16,24},{18,... | collective-permute-start | bytes 393224 | tf_op jit(solution)/shard_map/ppermute | solution.py:392
  13.7 6.1 %collective-permute-start.2 = (bf16[32,4096]{1,0:T(8,128)(2,1)S(1)}, bf16[32,4096]{1,0:T(8,128)(2,1)S(1)}, u32[]{:S(2)}, u32[]{:S(2)}) collective-permute-start(bf16[32,4096]{1,0:T(8,128)(2,1)S(1)} %pad_maximum_fusion.1), channel_id=1, source_target_pairs={{0,2},{2,0},{4,6},{6,4},{8,10},{10,8},{12,14},{14,12},{16,18},{18,... | collective-permute-start | bytes 786440 | tf_op jit(solution)/shard_map/ppermute | solution.py:386
  13.8 8.2 %collective-permute-start.7 = (bf16[32,2048]{1,0:T(8,128)(2,1)S(1)}, bf16[32,2048]{1,0:T(8,128)(2,1)S(1)}, u32[]{:S(2)}, u32[]{:S(2)}) collective-permute-start(bf16[32,2048]{1,0:T(8,128)(2,1)S(1)} %get-tuple-element.38), channel_id=1, source_target_pairs={{0,1},{1,0},{2,3},{3,2},{4,5},{5,4},{6,7},{7,6},{8,9},{9,8},{10,11... | collective-permute-start | bytes 393224 | tf_op jit(solution)/shard_map/ppermute | solution.py:395
  15.4 7.2 %collective-permute-start.8 = (bf16[48,2048]{1,0:T(8,128)(2,1)S(1)}, bf16[48,2048]{1,0:T(8,128)(2,1)S(1)}, u32[]{:S(2)}, u32[]{:S(2)}) collective-permute-start(bf16[48,2048]{1,0:T(8,128)(2,1)S(1)} %get-tuple-element.39), channel_id=1, source_target_pairs={{0,4},{2,6},{4,0},{6,2},{8,12},{10,14},{12,8},{14,10},{16,20},{18,... | collective-permute-start | bytes 589832 | tf_op jit(solution)/shard_map/ppermute | solution.py:389
  18.2 6.0 %collective-permute-start.11 = (bf16[16,2048]{1,0:T(8,128)(2,1)S(1)}, bf16[16,2048]{1,0:T(8,128)(2,1)S(1)}, u32[]{:S(2)}, u32[]{:S(2)}) collective-permute-start(bf16[16,2048]{1,0:T(8,128)(2,1)S(1)} %get-tuple-element.60), channel_id=1, source_target_pairs={{0,1},{1,0},{2,3},{3,2},{4,5},{5,4},{6,7},{7,6},{8,9},{9,8},{10,11... | collective-permute-start | bytes 196616 | tf_op jit(solution)/shard_map/ppermute | solution.py:395
  20.4 3.8 %collective-permute-start.9 = (f32[32,128]{1,0:T(8,128)S(1)}, f32[32,128]{1,0:T(8,128)S(1)}, u32[]{:S(2)}, u32[]{:S(2)}) collective-permute-start(f32[32,128]{1,0:T(8,128)S(1)} %gram.1), channel_id=1, source_target_pairs={{0,4},{2,6},{4,0},{6,2},{8,12},{10,14},{12,8},{14,10},{16,20},{18,... | collective-permute-start | bytes 49160 | tf_op jit(solution)/shard_map/ppermute | solution.py:389
  22.0 13.0 %collective-permute-start.17 = (bf16[64,2048]{1,0:T(8,128)(2,1)S(1)}, bf16[64,2048]{1,0:T(8,128)(2,1)S(1)}, u32[]{:S(2)}, u32[]{:S(2)}) collective-permute-start(bf16[64,2048]{1,0:T(8,128)(2,1)S(1)} %pad_maximum_fusion.2.refs_0_), channel_id=1, source_target_pairs={{0,2},{2,0},{4,6},{6,4},{8,10},{10,8},{12,14},{14,12},{16,18},{18,... | collective-permute-start | bytes 786440 | tf_op jit(solution)/shard_map/ppermute | solution.py:386
  22.1 4.8 %collective-permute-start.10 = (f32[32,128]{1,0:T(8,128)S(1)}, f32[32,128]{1,0:T(8,128)S(1)}, u32[]{:S(2)}, u32[]{:S(2)}) collective-permute-start(f32[32,128]{1,0:T(8,128)S(1)} %gram.1), channel_id=1, source_target_pairs={{0,5},{1,4},{2,7},{3,6},{4,1},{5,0},{6,3},{7,2},{8,13},{9,12},{10,... | collective-permute-start | bytes 49160 | tf_op jit(solution)/shard_map/ppermute | solution.py:399
  22.6 3.8 %collective-permute-start.5 = (f32[32,128]{1,0:T(8,128)S(1)}, f32[32,128]{1,0:T(8,128)S(1)}, u32[]{:S(2)}, u32[]{:S(2)}) collective-permute-start(f32[32,128]{1,0:T(8,128)S(1)} %gram.1), channel_id=1, source_target_pairs={{0,1},{1,0},{2,3},{3,2},{4,5},{5,4},{6,7},{7,6},{8,9},{9,8},{10,11... | collective-permute-start | bytes 49160 | tf_op jit(solution)/shard_map/ppermute | solution.py:395
  24.3 10.1 %collective-permute-start.12 = (bf16[80,2048]{1,0:T(8,128)(2,1)S(1)}, bf16[80,2048]{1,0:T(8,128)(2,1)S(1)}, u32[]{:S(2)}, u32[]{:S(2)}) collective-permute-start(bf16[80,2048]{1,0:T(8,128)(2,1)S(1)} %pad_maximum_fusion), channel_id=1, source_target_pairs={{0,4},{2,6},{4,0},{6,2},{8,12},{10,14},{12,8},{14,10},{16,20},{18,... | collective-permute-start | bytes 983048 | tf_op jit(solution)/shard_map/ppermute | solution.py:389
  26.9 5.8 %collective-permute-start.15 = (f32[64,128]{1,0:T(8,128)S(1)}, f32[64,128]{1,0:T(8,128)S(1)}, u32[]{:S(2)}, u32[]{:S(2)}) collective-permute-start(f32[64,128]{1,0:T(8,128)S(1)} %pad_maximum_fusion.5), channel_id=1, source_target_pairs={{0,24},{2,26},{4,28},{6,30},{8,16},{10,18},{12,20},{14,22},{16,8},... | collective-permute-start | bytes 98312 | tf_op jit(solution)/shard_map/ppermute | solution.py:392
  29.3 3.9 %collective-permute-start.14 = (f32[64,128]{1,0:T(8,128)S(1)}, f32[64,128]{1,0:T(8,128)S(1)}, u32[]{:S(2)}, u32[]{:S(2)}) collective-permute-start(f32[64,128]{1,0:T(8,128)S(1)} %pad_maximum_fusion.5), channel_id=1, source_target_pairs={{0,8},{2,10},{4,12},{6,14},{8,0},{10,2},{12,4},{14,6},{16,24},{18,... | collective-permute-start | bytes 98312 | tf_op jit(solution)/shard_map/ppermute | solution.py:392
  29.5 4.8 %collective-permute-start.13 = (f32[64,128]{1,0:T(8,128)S(1)}, f32[64,128]{1,0:T(8,128)S(1)}, u32[]{:S(2)}, u32[]{:S(2)}) collective-permute-start(f32[64,128]{1,0:T(8,128)S(1)} %pad_maximum_fusion.5), channel_id=1, source_target_pairs={{0,16},{2,18},{4,20},{6,22},{8,24},{10,26},{12,28},{14,30},{16,0},... | collective-permute-start | bytes 98312 | tf_op jit(solution)/shard_map/ppermute | solution.py:392
  32.6 2.3 %collective-permute-start.19 = (bf16[48,2048]{1,0:T(8,128)(2,1)S(1)}, bf16[48,2048]{1,0:T(8,128)(2,1)S(1)}, u32[]{:S(2)}, u32[]{:S(2)}) collective-permute-start(bf16[48,2048]{1,0:T(8,128)(2,1)S(1)} %collective-permute-done.8.refs_4_), channel_id=1, source_target_pairs={{0,2},{2,0},{4,6},{6,4},{8,10},{10,8},{12,14},{14,12},{16,18},{18,... | collective-permute-start | bytes 589832 | tf_op jit(solution)/shard_map/ppermute | solution.py:386
  33.2 1.7 %collective-permute-start.18 = (bf16[64,2048]{1,0:T(8,128)(2,1)S(1)}, bf16[64,2048]{1,0:T(8,128)(2,1)S(1)}, u32[]{:S(2)}, u32[]{:S(2)}) collective-permute-start(bf16[64,2048]{1,0:T(8,128)(2,1)S(1)} %pad_maximum_fusion.3.refs_2_), channel_id=1, source_target_pairs={{0,2},{2,0},{4,6},{6,4},{8,10},{10,8},{12,14},{14,12},{16,18},{18,... | collective-permute-start | bytes 786440 | tf_op jit(solution)/shard_map/ppermute | solution.py:386
  34.3 2.8 %collective-permute-start.20 = (bf16[80,2048]{1,0:T(8,128)(2,1)S(1)}, bf16[80,2048]{1,0:T(8,128)(2,1)S(1)}, u32[]{:S(2)}, u32[]{:S(2)}) collective-permute-start(bf16[80,2048]{1,0:T(8,128)(2,1)S(1)} %collective-permute-done.12.refs_6_), channel_id=1, source_target_pairs={{0,2},{2,0},{4,6},{6,4},{8,10},{10,8},{12,14},{14,12},{16,18},{18,... | collective-permute-start | bytes 983048 | tf_op jit(solution)/shard_map/ppermute | solution.py:386
  34.4 1.8 %collective-permute-start.16 = (f32[256,128]{1,0:T(8,128)S(1)}, f32[256,128]{1,0:T(8,128)S(1)}, u32[]{:S(2)}, u32[]{:S(2)}) collective-permute-start(f32[256,128]{1,0:T(8,128)S(1)} %constant_dynamic-update-slice_fusion.mine), channel_id=1, source_target_pairs={{0,2},{2,0},{4,6},{6,4},{8,10},{10,8},{12,14},{14,12},{16,18},{18,... | collective-permute-start | bytes 393224 | tf_op jit(solution)/shard_map/ppermute | solution.py:386

commit v9 on v8

--- a/solution.py
+++ b/solution.py
@@ -211,7 +211,7 @@
     square = (cols, cols)
     eye = lax.broadcasted_iota(jnp.int32, square, 0) == lax.broadcasted_iota(jnp.int32, square, 1)
     norm = jnp.sum(jnp.where(eye, prod[rows:], 0.0), axis=0, keepdims=True)
-    part = norm - 2.0 * prod[:rows]
+    part = (2.0 * prod[:rows] - norm) * SCALE
     blocks = [part[k * clips : (k + 1) * clips] for k in range(4)]
     near0 = jnp.where(c == 0, blocks[0], blocks[2])
     near1 = jnp.where(c == 0, blocks[2], blocks[0])
@@ -261,8 +261,8 @@
     for s in range(mine.shape[0] // (2 * half)):
         for x in range(2):
             r = s * 2 * half
-            g = mine[r + x * half : r + (x + 1) * half, :] * (-SCALE)
-            h = other[r + x * half : r + (x + 1) * half, :] * (-SCALE)
+            g = mine[r + x * half : r + (x + 1) * half, :]
+            h = other[r + x * half : r + (x + 1) * half, :]
             lanes = slice(x * 128, (x + 1) * 128)
             full[r : r + half, lanes] = jnp.where(low, g, pltpu.roll(h, 64, 1))
             full[r + half : r + 2 * half, lanes] = jnp.where(low, pltpu.roll(g, 64, 1), h)

time: 42.3 us -> 42.3 us (level)
  no operation moved by 1% of the time
where the time goes in v9:
time: 42.3 us; the launch traced here: 42.1 us
  starting transfers between devices  24.3 us (57%)
  Pallas kernels  9.06 us (21%)
  waiting for transfers between devices  8.43 us (20%)
    ppermute x6, starting transfers between devices, along(): return lax.ppermute(x, 'clip', flip(n, 4 * k))  10.6 us
    ppermute x4, starting transfers between devices, other_val(): return lax.ppermute(x, 'val', [(0, 1), (1, 0)])  6.25 us
    ppermute x4, starting transfers between devices, across(): return lax.ppermute(x, 'clip', flip(n, 2))  6.15 us
    ppermute x6, waiting for transfers between devices, along(): return lax.ppermute(x, 'clip', flip(n, 4 * k))  6.02 us
    pallas_call x1, Pallas kernels, finish(): pl.pallas_call(functools.partial(finish_kernel, clips, block, layout), ou...  4.93 us
    pallas_call x1, Pallas kernels, split_frames(): pl.pallas_call(split_kernel, out_shape=jax.ShapeDtypeStruct(noise.shape,...  1.32 us
    ppermute x6, waiting for transfers between devices, core(): return lax.ppermute(x, 'clip', flip(n, 1))  1.22 us
    pallas_call x1, Pallas kernels, stage(): pl.pallas_call(stage_kernel, out_shape=[jax.ShapeDtypeStruct(embed.shape,...  1.19 us
  transfers between devices with their start and end apart: 21, of which 10 were waited for; matrix products, arithmetic and copies ran while one was open for 0% of the time, Pallas kernels for 7%

profile of v9, /device:TPU:0, one launch (start us, length us, event | category | flops | bytes accessed | tf_op | source)
XLA Modules:
  0.0 42.1 jit_solution(15986593672274705400)
XLA Ops:
  0.0 1.3 %split.1.refs_0_ = bf16[16,4096]{1,0:T(8,128)(2,1)S(1)} custom-call(s32[4,16]{1,0:T(4,128)} %bitcast.4, bf16[16,4096]{1,0:T(8,128)(2,1)} %noise_in.1), custom_call_target="tpu_custom_call" | custom-call | tf_op jit(solution)/shard_map/split/pallas_call | solution.py:139
  1.3 3.1 %collective-permute-start.3 = (bf16[16,4096]{1,0:T(8,128)(2,1)S(1)}, bf16[16,4096]{1,0:T(8,128)(2,1)S(1)}, u32[]{:S(2)}, u32[]{:S(2)}) collective-permute-start(bf16[16,4096]{1,0:T(8,128)(2,1)S(1)} %split.1.refs_0_), channel_id=1, source_target_pairs={{0,8},{2,10},{4,12},{6,14},{8,0},{10,2},{12,4},{14,6},{16,24},{18,... | collective-permute-start | bytes 393224 | tf_op jit(solution)/shard_map/ppermute | solution.py:392
  4.4 2.6 %collective-permute-start.1 = (bf16[16,4096]{1,0:T(8,128)(2,1)S(1)}, bf16[16,4096]{1,0:T(8,128)(2,1)S(1)}, u32[]{:S(2)}, u32[]{:S(2)}) collective-permute-start(bf16[16,4096]{1,0:T(8,128)(2,1)S(1)} %split.1.refs_0_), channel_id=1, source_target_pairs={{0,16},{2,18},{4,20},{6,22},{8,24},{10,26},{12,28},{14,30},{16,0},... | collective-permute-start | bytes 393224 | tf_op jit(solution)/shard_map/ppermute | solution.py:392
  7.0 1.2 %stage.1 = (bf16[64,5120]{1,0:T(8,128)(2,1)S(1)}, f32[16,128]{1,0:T(8,128)S(1)}, bf16[16,4096]{1,0:T(8,128)(2,1)S(1)}) custom-call(f32[16]{0:T(128)} %times_in, bf16[64,5120]{1,0:T(8,128)(2,1)} %embed, bf16[16,4096]{1,0:T(8,128)(2,1)} %latents_in), custom_call_target="tpu_custom_call" | custom-call | bytes 3500000 | tf_op jit(solution)/shard_map/stage/pallas_call | solution.py:173
  8.2 1.6 %collective-permute-start = (bf16[16,4096]{1,0:T(8,128)(2,1)S(1)}, bf16[16,4096]{1,0:T(8,128)(2,1)S(1)}, u32[]{:S(2)}, u32[]{:S(2)}) collective-permute-start(bf16[16,4096]{1,0:T(8,128)(2,1)S(1)} %get-tuple-element.34.lat.lat_keep), channel_id=1, source_target_pairs={{0,4},{2,6},{4,0},{6,2},{8,12},{10,14},{12,8},{14,10},{16,20},{18,... | collective-permute-start | bytes 393224 | tf_op jit(solution)/shard_map/ppermute | solution.py:389
  9.8 1.6 %collective-permute-start.6 = (bf16[32,2048]{1,0:T(8,128)(2,1)S(1)}, bf16[32,2048]{1,0:T(8,128)(2,1)S(1)}, u32[]{:S(2)}, u32[]{:S(2)}) collective-permute-start(bf16[32,2048]{1,0:T(8,128)(2,1)S(1)} %pad_maximum_fusion.4), channel_id=1, source_target_pairs={{0,1},{1,0},{2,3},{3,2},{4,5},{5,4},{6,7},{7,6},{8,9},{9,8},{10,11... | collective-permute-start | bytes 393224 | tf_op jit(solution)/shard_map/ppermute | solution.py:395
  11.4 1.7 %collective-permute-done.1.refs_2_ = bf16[16,4096]{1,0:T(8,128)(2,1)S(1)} collective-permute-done((bf16[16,4096]{1,0:T(8,128)(2,1)S(1)}, bf16[16,4096]{1,0:T(8,128)(2,1)S(1)}, u32[]{:S(2)}, u32[]{:S(2)}) %collective-permute-start.1) | collective-permute-done | bytes 131104 | tf_op jit(solution)/shard_map/ppermute | solution.py:392
  13.8 1.6 %collective-permute-start.7 = (bf16[32,2048]{1,0:T(8,128)(2,1)S(1)}, bf16[32,2048]{1,0:T(8,128)(2,1)S(1)}, u32[]{:S(2)}, u32[]{:S(2)}) collective-permute-start(bf16[32,2048]{1,0:T(8,128)(2,1)S(1)} %get-tuple-element.38), channel_id=1, source_target_pairs={{0,1},{1,0},{2,3},{3,2},{4,5},{5,4},{6,7},{7,6},{8,9},{9,8},{10,11... | collective-permute-start | bytes 393224 | tf_op jit(solution)/shard_map/ppermute | solution.py:395
  15.4 1.5 %collective-permute-start.8 = (bf16[48,2048]{1,0:T(8,128)(2,1)S(1)}, bf16[48,2048]{1,0:T(8,128)(2,1)S(1)}, u32[]{:S(2)}, u32[]{:S(2)}) collective-permute-start(bf16[48,2048]{1,0:T(8,128)(2,1)S(1)} %get-tuple-element.39), channel_id=1, source_target_pairs={{0,4},{2,6},{4,0},{6,2},{8,12},{10,14},{12,8},{14,10},{16,20},{18,... | collective-permute-start | bytes 589832 | tf_op jit(solution)/shard_map/ppermute | solution.py:389
  16.9 1.3 %collective-permute-done.4.refs_3_ = bf16[16,4096]{1,0:T(8,128)(2,1)S(1)} collective-permute-done((bf16[16,4096]{1,0:T(8,128)(2,1)S(1)}, bf16[16,4096]{1,0:T(8,128)(2,1)S(1)}, u32[]{:S(2)}, u32[]{:S(2)}) %collective-permute-start.4) | collective-permute-done | bytes 131104 | tf_op jit(solution)/shard_map/ppermute | solution.py:392
  18.2 1.6 %collective-permute-start.11 = (bf16[16,2048]{1,0:T(8,128)(2,1)S(1)}, bf16[16,2048]{1,0:T(8,128)(2,1)S(1)}, u32[]{:S(2)}, u32[]{:S(2)}) collective-permute-start(bf16[16,2048]{1,0:T(8,128)(2,1)S(1)} %get-tuple-element.60), channel_id=1, source_target_pairs={{0,1},{1,0},{2,3},{3,2},{4,5},{5,4},{6,7},{7,6},{8,9},{9,8},{10,11... | collective-permute-start | bytes 196616 | tf_op jit(solution)/shard_map/ppermute | solution.py:395
  19.8 0.6 %gram.1 = f32[32,128]{1,0:T(8,128)S(1)} custom-call(bf16[16,4096]{1,0:T(8,128)(2,1)S(1)} %get-tuple-element.34.lat.lat_keep, bf16[16,4096]{1,0:T(8,128)(2,1)S(1)} %collective-permute-done.lat_far, bf16[32,4096]{1,0:T(8,128)(2,1)S(1)} %collective-permute-done.2.lat_core, bf16[16,4096]{1,0:T(8,128)(2,1)S(1)} %split.1.refs_0_, ...), custom_call_target="tpu_custom_call" | custom-call | bytes 17500000 | tf_op jit(solution)/shard_map/gram/pallas_call | solution.py:227
  20.4 1.5 %collective-permute-start.9 = (f32[32,128]{1,0:T(8,128)S(1)}, f32[32,128]{1,0:T(8,128)S(1)}, u32[]{:S(2)}, u32[]{:S(2)}) collective-permute-start(f32[32,128]{1,0:T(8,128)S(1)} %gram.1), channel_id=1, source_target_pairs={{0,4},{2,6},{4,0},{6,2},{8,12},{10,14},{12,8},{14,10},{16,20},{18,... | collective-permute-start | bytes 49160 | tf_op jit(solution)/shard_map/ppermute | solution.py:389
  22.6 1.5 %collective-permute-start.5 = (f32[32,128]{1,0:T(8,128)S(1)}, f32[32,128]{1,0:T(8,128)S(1)}, u32[]{:S(2)}, u32[]{:S(2)}) collective-permute-start(f32[32,128]{1,0:T(8,128)S(1)} %gram.1), channel_id=1, source_target_pairs={{0,1},{1,0},{2,3},{3,2},{4,5},{5,4},{6,7},{7,6},{8,9},{9,8},{10,11... | collective-permute-start | bytes 49160 | tf_op jit(solution)/shard_map/ppermute | solution.py:395
  24.3 1.6 %collective-permute-start.12 = (bf16[80,2048]{1,0:T(8,128)(2,1)S(1)}, bf16[80,2048]{1,0:T(8,128)(2,1)S(1)}, u32[]{:S(2)}, u32[]{:S(2)}) collective-permute-start(bf16[80,2048]{1,0:T(8,128)(2,1)S(1)} %pad_maximum_fusion), channel_id=1, source_target_pairs={{0,4},{2,6},{4,0},{6,2},{8,12},{10,14},{12,8},{14,10},{16,20},{18,... | collective-permute-start | bytes 983048 | tf_op jit(solution)/shard_map/ppermute | solution.py:389
  25.8 0.6 %collective-permute-done.5 = f32[32,128]{1,0:T(8,128)S(1)} collective-permute-done((f32[32,128]{1,0:T(8,128)S(1)}, f32[32,128]{1,0:T(8,128)S(1)}, u32[]{:S(2)}, u32[]{:S(2)}) %collective-permute-start.5) | collective-permute-done | bytes 16416 | tf_op jit(solution)/shard_map/ppermute | solution.py:395
  26.9 2.5 %collective-permute-start.15 = (f32[64,128]{1,0:T(8,128)S(1)}, f32[64,128]{1,0:T(8,128)S(1)}, u32[]{:S(2)}, u32[]{:S(2)}) collective-permute-start(f32[64,128]{1,0:T(8,128)S(1)} %pad_maximum_fusion.5), channel_id=1, source_target_pairs={{0,24},{2,26},{4,28},{6,30},{8,16},{10,18},{12,20},{14,22},{16,8},... | collective-permute-start | bytes 98312 | tf_op jit(solution)/shard_map/ppermute | solution.py:392
  29.5 1.8 %collective-permute-start.13 = (f32[64,128]{1,0:T(8,128)S(1)}, f32[64,128]{1,0:T(8,128)S(1)}, u32[]{:S(2)}, u32[]{:S(2)}) collective-permute-start(f32[64,128]{1,0:T(8,128)S(1)} %pad_maximum_fusion.5), channel_id=1, source_target_pairs={{0,16},{2,18},{4,20},{6,22},{8,24},{10,26},{12,28},{14,30},{16,0},... | collective-permute-start | bytes 98312 | tf_op jit(solution)/shard_map/ppermute | solution.py:392
  31.3 1.3 %collective-permute-done.15 = f32[64,128]{1,0:T(8,128)S(1)} collective-permute-done((f32[64,128]{1,0:T(8,128)S(1)}, f32[64,128]{1,0:T(8,128)S(1)}, u32[]{:S(2)}, u32[]{:S(2)}) %collective-permute-start.15) | collective-permute-done | bytes 32800 | tf_op jit(solution)/shard_map/ppermute | solution.py:392
  32.7 0.6 %collective-permute-done.14 = f32[64,128]{1,0:T(8,128)S(1)} collective-permute-done((f32[64,128]{1,0:T(8,128)S(1)}, f32[64,128]{1,0:T(8,128)S(1)}, u32[]{:S(2)}, u32[]{:S(2)}) %collective-permute-start.14) | collective-permute-done | bytes 32800 | tf_op jit(solution)/shard_map/ppermute | solution.py:392
  33.2 1.1 %collective-permute-done.13 = f32[64,128]{1,0:T(8,128)S(1)} collective-permute-done((f32[64,128]{1,0:T(8,128)S(1)}, f32[64,128]{1,0:T(8,128)S(1)}, u32[]{:S(2)}, u32[]{:S(2)}) %collective-permute-start.13) | collective-permute-done | bytes 32800 | tf_op jit(solution)/shard_map/ppermute | solution.py:392
  35.0 1.2 %collective-permute-done.16.other = f32[256,128]{1,0:T(8,128)S(1)} collective-permute-done((f32[256,128]{1,0:T(8,128)S(1)}, f32[256,128]{1,0:T(8,128)S(1)}, u32[]{:S(2)}, u32[]{:S(2)}) %collective-permute-start.16) | collective-permute-done | bytes 131104 | tf_op jit(solution)/shard_map/ppermute | solution.py:386
  36.2 1.0 %plan.1.weights = bf16[16,256]{1,0:T(8,128)(2,1)S(1)} custom-call(f32[256,128]{1,0:T(8,128)S(1)} %constant_dynamic-update-slice_fusion.mine, f32[256,128]{1,0:T(8,128)S(1)} %collective-permute-done.16.other), custom_call_target="tpu_custom_call" | custom-call | tf_op jit(solution)/shard_map/plan/pallas_call | solution.py:281
  37.2 4.9 %finish.1 = bf16[1024,5120]{1,0:T(8,128)(2,1)} custom-call(f32[16,128]{1,0:T(8,128)S(1)} %get-tuple-element.32.column, bf16[16,256]{1,0:T(8,128)(2,1)S(1)} %plan.1.weights, bf16[16,4096]{1,0:T(8,128)(2,1)S(1)} %get-tuple-element.34.lat.lat_keep, bf16[16,2048]{1,0:T(8,128)(2,1)S(1)} %get-tuple-element.57.lat_got, ...), custom_call_target="tpu_custom_call" | custom-call | tf_op jit(solution)/shard_map/finish/pallas_call | solution.py:339
  (42 shorter events, 2.7 us)
Async XLA Ops:
  1.3 12.5 %collective-permute-start.3 = (bf16[16,4096]{1,0:T(8,128)(2,1)S(1)}, bf16[16,4096]{1,0:T(8,128)(2,1)S(1)}, u32[]{:S(2)}, u32[]{:S(2)}) collective-permute-start(bf16[16,4096]{1,0:T(8,128)(2,1)S(1)} %split.1.refs_0_), channel_id=1, source_target_pairs={{0,8},{2,10},{4,12},{6,14},{8,0},{10,2},{12,4},{14,6},{16,24},{18,... | collective-permute-start | bytes 393224 | tf_op jit(solution)/shard_map/ppermute | solution.py:392
  4.4 8.7 %collective-permute-start.1 = (bf16[16,4096]{1,0:T(8,128)(2,1)S(1)}, bf16[16,4096]{1,0:T(8,128)(2,1)S(1)}, u32[]{:S(2)}, u32[]{:S(2)}) collective-permute-start(bf16[16,4096]{1,0:T(8,128)(2,1)S(1)} %split.1.refs_0_), channel_id=1, source_target_pairs={{0,16},{2,18},{4,20},{6,22},{8,24},{10,26},{12,28},{14,30},{16,0},... | collective-permute-start | bytes 393224 | tf_op jit(solution)/shard_map/ppermute | solution.py:392
  8.2 5.0 %collective-permute-start = (bf16[16,4096]{1,0:T(8,128)(2,1)S(1)}, bf16[16,4096]{1,0:T(8,128)(2,1)S(1)}, u32[]{:S(2)}, u32[]{:S(2)}) collective-permute-start(bf16[16,4096]{1,0:T(8,128)(2,1)S(1)} %get-tuple-element.34.lat.lat_keep), channel_id=1, source_target_pairs={{0,4},{2,6},{4,0},{6,2},{8,12},{10,14},{12,8},{14,10},{16,20},{18,... | collective-permute-start | bytes 393224 | tf_op jit(solution)/shard_map/ppermute | solution.py:389
  9.8 12.2 %collective-permute-start.6 = (bf16[32,2048]{1,0:T(8,128)(2,1)S(1)}, bf16[32,2048]{1,0:T(8,128)(2,1)S(1)}, u32[]{:S(2)}, u32[]{:S(2)}) collective-permute-start(bf16[32,2048]{1,0:T(8,128)(2,1)S(1)} %pad_maximum_fusion.4), channel_id=1, source_target_pairs={{0,1},{1,0},{2,3},{3,2},{4,5},{5,4},{6,7},{7,6},{8,9},{9,8},{10,11... | collective-permute-start | bytes 393224 | tf_op jit(solution)/shard_map/ppermute | solution.py:395
  13.2 5.0 %collective-permute-start.4 = (bf16[16,4096]{1,0:T(8,128)(2,1)S(1)}, bf16[16,4096]{1,0:T(8,128)(2,1)S(1)}, u32[]{:S(2)}, u32[]{:S(2)}) collective-permute-start(bf16[16,4096]{1,0:T(8,128)(2,1)S(1)} %collective-permute-done.1.refs_2_), channel_id=1, source_target_pairs={{0,8},{2,10},{4,12},{6,14},{8,0},{10,2},{12,4},{14,6},{16,24},{18,... | collective-permute-start | bytes 393224 | tf_op jit(solution)/shard_map/ppermute | solution.py:392
  13.7 6.1 %collective-permute-start.2 = (bf16[32,4096]{1,0:T(8,128)(2,1)S(1)}, bf16[32,4096]{1,0:T(8,128)(2,1)S(1)}, u32[]{:S(2)}, u32[]{:S(2)}) collective-permute-start(bf16[32,4096]{1,0:T(8,128)(2,1)S(1)} %pad_maximum_fusion.1), channel_id=1, source_target_pairs={{0,2},{2,0},{4,6},{6,4},{8,10},{10,8},{12,14},{14,12},{16,18},{18,... | collective-permute-start | bytes 786440 | tf_op jit(solution)/shard_map/ppermute | solution.py:386
  13.8 8.2 %collective-permute-start.7 = (bf16[32,2048]{1,0:T(8,128)(2,1)S(1)}, bf16[32,2048]{1,0:T(8,128)(2,1)S(1)}, u32[]{:S(2)}, u32[]{:S(2)}) collective-permute-start(bf16[32,2048]{1,0:T(8,128)(2,1)S(1)} %get-tuple-element.38), channel_id=1, source_target_pairs={{0,1},{1,0},{2,3},{3,2},{4,5},{5,4},{6,7},{7,6},{8,9},{9,8},{10,11... | collective-permute-start | bytes 393224 | tf_op jit(solution)/shard_map/ppermute | solution.py:395
  15.4 7.2 %collective-permute-start.8 = (bf16[48,2048]{1,0:T(8,128)(2,1)S(1)}, bf16[48,2048]{1,0:T(8,128)(2,1)S(1)}, u32[]{:S(2)}, u32[]{:S(2)}) collective-permute-start(bf16[48,2048]{1,0:T(8,128)(2,1)S(1)} %get-tuple-element.39), channel_id=1, source_target_pairs={{0,4},{2,6},{4,0},{6,2},{8,12},{10,14},{12,8},{14,10},{16,20},{18,... | collective-permute-start | bytes 589832 | tf_op jit(solution)/shard_map/ppermute | solution.py:389
  18.2 6.0 %collective-permute-start.11 = (bf16[16,2048]{1,0:T(8,128)(2,1)S(1)}, bf16[16,2048]{1,0:T(8,128)(2,1)S(1)}, u32[]{:S(2)}, u32[]{:S(2)}) collective-permute-start(bf16[16,2048]{1,0:T(8,128)(2,1)S(1)} %get-tuple-element.60), channel_id=1, source_target_pairs={{0,1},{1,0},{2,3},{3,2},{4,5},{5,4},{6,7},{7,6},{8,9},{9,8},{10,11... | collective-permute-start | bytes 196616 | tf_op jit(solution)/shard_map/ppermute | solution.py:395
  20.4 3.8 %collective-permute-start.9 = (f32[32,128]{1,0:T(8,128)S(1)}, f32[32,128]{1,0:T(8,128)S(1)}, u32[]{:S(2)}, u32[]{:S(2)}) collective-permute-start(f32[32,128]{1,0:T(8,128)S(1)} %gram.1), channel_id=1, source_target_pairs={{0,4},{2,6},{4,0},{6,2},{8,12},{10,14},{12,8},{14,10},{16,20},{18,... | collective-permute-start | bytes 49160 | tf_op jit(solution)/shard_map/ppermute | solution.py:389
  22.0 13.0 %collective-permute-start.17 = (bf16[64,2048]{1,0:T(8,128)(2,1)S(1)}, bf16[64,2048]{1,0:T(8,128)(2,1)S(1)}, u32[]{:S(2)}, u32[]{:S(2)}) collective-permute-start(bf16[64,2048]{1,0:T(8,128)(2,1)S(1)} %pad_maximum_fusion.2.refs_0_), channel_id=1, source_target_pairs={{0,2},{2,0},{4,6},{6,4},{8,10},{10,8},{12,14},{14,12},{16,18},{18,... | collective-permute-start | bytes 786440 | tf_op jit(solution)/shard_map/ppermute | solution.py:386
  22.1 4.8 %collective-permute-start.10 = (f32[32,128]{1,0:T(8,128)S(1)}, f32[32,128]{1,0:T(8,128)S(1)}, u32[]{:S(2)}, u32[]{:S(2)}) collective-permute-start(f32[32,128]{1,0:T(8,128)S(1)} %gram.1), channel_id=1, source_target_pairs={{0,5},{1,4},{2,7},{3,6},{4,1},{5,0},{6,3},{7,2},{8,13},{9,12},{10,... | collective-permute-start | bytes 49160 | tf_op jit(solution)/shard_map/ppermute | solution.py:399
  22.6 3.8 %collective-permute-start.5 = (f32[32,128]{1,0:T(8,128)S(1)}, f32[32,128]{1,0:T(8,128)S(1)}, u32[]{:S(2)}, u32[]{:S(2)}) collective-permute-start(f32[32,128]{1,0:T(8,128)S(1)} %gram.1), channel_id=1, source_target_pairs={{0,1},{1,0},{2,3},{3,2},{4,5},{5,4},{6,7},{7,6},{8,9},{9,8},{10,11... | collective-permute-start | bytes 49160 | tf_op jit(solution)/shard_map/ppermute | solution.py:395
  24.3 10.1 %collective-permute-start.12 = (bf16[80,2048]{1,0:T(8,128)(2,1)S(1)}, bf16[80,2048]{1,0:T(8,128)(2,1)S(1)}, u32[]{:S(2)}, u32[]{:S(2)}) collective-permute-start(bf16[80,2048]{1,0:T(8,128)(2,1)S(1)} %pad_maximum_fusion), channel_id=1, source_target_pairs={{0,4},{2,6},{4,0},{6,2},{8,12},{10,14},{12,8},{14,10},{16,20},{18,... | collective-permute-start | bytes 983048 | tf_op jit(solution)/shard_map/ppermute | solution.py:389
  26.9 5.8 %collective-permute-start.15 = (f32[64,128]{1,0:T(8,128)S(1)}, f32[64,128]{1,0:T(8,128)S(1)}, u32[]{:S(2)}, u32[]{:S(2)}) collective-permute-start(f32[64,128]{1,0:T(8,128)S(1)} %pad_maximum_fusion.5), channel_id=1, source_target_pairs={{0,24},{2,26},{4,28},{6,30},{8,16},{10,18},{12,20},{14,22},{16,8},... | collective-permute-start | bytes 98312 | tf_op jit(solution)/shard_map/ppermute | solution.py:392
  29.3 3.9 %collective-permute-start.14 = (f32[64,128]{1,0:T(8,128)S(1)}, f32[64,128]{1,0:T(8,128)S(1)}, u32[]{:S(2)}, u32[]{:S(2)}) collective-permute-start(f32[64,128]{1,0:T(8,128)S(1)} %pad_maximum_fusion.5), channel_id=1, source_target_pairs={{0,8},{2,10},{4,12},{6,14},{8,0},{10,2},{12,4},{14,6},{16,24},{18,... | collective-permute-start | bytes 98312 | tf_op jit(solution)/shard_map/ppermute | solution.py:392
  29.5 4.8 %collective-permute-start.13 = (f32[64,128]{1,0:T(8,128)S(1)}, f32[64,128]{1,0:T(8,128)S(1)}, u32[]{:S(2)}, u32[]{:S(2)}) collective-permute-start(f32[64,128]{1,0:T(8,128)S(1)} %pad_maximum_fusion.5), channel_id=1, source_target_pairs={{0,16},{2,18},{4,20},{6,22},{8,24},{10,26},{12,28},{14,30},{16,0},... | collective-permute-start | bytes 98312 | tf_op jit(solution)/shard_map/ppermute | solution.py:392
  32.6 2.3 %collective-permute-start.19 = (bf16[48,2048]{1,0:T(8,128)(2,1)S(1)}, bf16[48,2048]{1,0:T(8,128)(2,1)S(1)}, u32[]{:S(2)}, u32[]{:S(2)}) collective-permute-start(bf16[48,2048]{1,0:T(8,128)(2,1)S(1)} %collective-permute-done.8.refs_4_), channel_id=1, source_target_pairs={{0,2},{2,0},{4,6},{6,4},{8,10},{10,8},{12,14},{14,12},{16,18},{18,... | collective-permute-start | bytes 589832 | tf_op jit(solution)/shard_map/ppermute | solution.py:386
  33.2 1.7 %collective-permute-start.18 = (bf16[64,2048]{1,0:T(8,128)(2,1)S(1)}, bf16[64,2048]{1,0:T(8,128)(2,1)S(1)}, u32[]{:S(2)}, u32[]{:S(2)}) collective-permute-start(bf16[64,2048]{1,0:T(8,128)(2,1)S(1)} %pad_maximum_fusion.3.refs_2_), channel_id=1, source_target_pairs={{0,2},{2,0},{4,6},{6,4},{8,10},{10,8},{12,14},{14,12},{16,18},{18,... | collective-permute-start | bytes 786440 | tf_op jit(solution)/shard_map/ppermute | solution.py:386
  34.3 2.8 %collective-permute-start.20 = (bf16[80,2048]{1,0:T(8,128)(2,1)S(1)}, bf16[80,2048]{1,0:T(8,128)(2,1)S(1)}, u32[]{:S(2)}, u32[]{:S(2)}) collective-permute-start(bf16[80,2048]{1,0:T(8,128)(2,1)S(1)} %collective-permute-done.12.refs_6_), channel_id=1, source_target_pairs={{0,2},{2,0},{4,6},{6,4},{8,10},{10,8},{12,14},{14,12},{16,18},{18,... | collective-permute-start | bytes 983048 | tf_op jit(solution)/shard_map/ppermute | solution.py:386
  34.4 1.8 %collective-permute-start.16 = (f32[256,128]{1,0:T(8,128)S(1)}, f32[256,128]{1,0:T(8,128)S(1)}, u32[]{:S(2)}, u32[]{:S(2)}) collective-permute-start(f32[256,128]{1,0:T(8,128)S(1)} %constant_dynamic-update-slice_fusion.mine), channel_id=1, source_target_pairs={{0,2},{2,0},{4,6},{6,4},{8,10},{10,8},{12,14},{14,12},{16,18},{18,... | collective-permute-start | bytes 393224 | tf_op jit(solution)/shard_map/ppermute | solution.py:386
